TPU v7x, 256 devices: a whole 4x4x8 slice. The times are simulated.
256 devices in a mesh: dp: 32 (over y, z_lo, core), shard: 8 (over x, z_hi).
Axes of the slice: x: 4, y: 4, z: 8 (z_hi: 2, z_lo: 4; z = z_hi * 4 + z_lo), core: 2. Of those that a mesh axis runs over, the one named last changes fastest.
Arguments:
- features: bfloat16 [16384, 8192], P('dp', 'shard'), may hold values from -6 to 6
- out_grads: bfloat16 [16384, 28672], P('dp', 'shard'), may hold values from -0.046875 to 0.046875
- proj_basis: bfloat16 [8192, 512], P('shard'), may hold values from -0.0625 to 0.0625
- first_moment: float32 [8, 3584, 512], P('shard', 'dp'), may hold values from -2 to 2
- second_moment: float32 [8, 3584, 512], P('shard', 'dp'), may hold values from 0.02 to 1
Outputs:
- update: bfloat16 [8, 3584, 8192], P(None, 'dp', 'shard')
- first_new: float32 [8, 3584, 512], P('shard', 'dp')
- second_new: float32 [8, 3584, 512], P('shard', 'dp')
All inputs are finite; a program needn't handle non-finite values.
Results may differ from a plain program's by a relative error of at most 0.0052.
Values may be sent and summed in bfloat16 or wider, within the bound.
No kernel may reach another device: no remote copies, remote signals or barrier semaphores. Data moves between devices by JAX's collectives and lax.ppermute only.
A program may use at most 64 MiB of HBM per device.

v0:
```python
import jax
import jax.numpy as jnp
from jax import lax
from jax.sharding import PartitionSpec as P

beta_first = 0.9
beta_second = 0.99
correct_first = 0.9999734386011124
correct_second = 0.6339676587267705
epsilon = 1e-08
galore_scale = 4.0


def per_device(features, out_grads, proj_basis, first_moment, second_moment):
    partial_proj = jnp.dot(features, proj_basis, preferred_element_type=jnp.float32)
    projected = lax.psum(partial_proj, "shard").astype(jnp.bfloat16)
    low_grad = lax.psum_scatter(
        lax.dot_general(
            out_grads, projected, (((0,), (0,)), ((), ())), preferred_element_type=jnp.float32
        ),
        "dp",
        scatter_dimension=0,
        tiled=True,
    )[None]
    first_new = beta_first * first_moment + (1.0 - beta_first) * low_grad
    second_new = beta_second * second_moment + (1.0 - beta_second) * low_grad * low_grad
    direction = (
        first_new / correct_first / (jnp.sqrt(second_new / correct_second) + epsilon)
    ).astype(jnp.bfloat16)
    full_rows = lax.dot_general(
        direction[0],
        lax.all_gather(proj_basis, "shard", axis=0, tiled=True),
        (((1,), (1,)), ((), ())),
        preferred_element_type=jnp.float32,
    )
    full_rows = (galore_scale * full_rows).astype(jnp.bfloat16)[None]
    update = lax.all_to_all(full_rows, "shard", split_axis=2, concat_axis=0, tiled=True)
    return (update, first_new, second_new)


def solution(mesh):
    return jax.shard_map(
        per_device,
        mesh=mesh,
        in_specs=(
            P("dp", "shard"),
            P("dp", "shard"),
            P("shard", None),
            P("shard", "dp", None),
            P("shard", "dp", None),
        ),
        out_specs=(P(None, "dp", "shard"), P("shard", "dp", None), P("shard", "dp", None)),
        check_vma=False,
    )
```

profile of v0, /device:TPU:32, one launch (start us, length us, event | category | flops | bytes accessed | tf_op | source)
XLA Modules:
  0.0 558.2 jit_solution(14852601537491953891)
XLA Ops:
  8.0 0.0 copy-start
  8.0 0.0 reduce-scatter.4.cloned.1.call-start
  8.1 1.2 copy-done
  9.2 1.9 fusion.11
  11.2 147.4 %all-reduce.1 = bf16[512,512]{1,0:T(8,128)(2,1)S(1)} all-reduce(f32[512,512]{1,0:T(8,128)S(1)} %fusion.11), channel_id=1, replica_groups=mesh['dp'=32,'shard'=8] {'shard'}, use_global_device_ids=true, to_apply=%region_0.0 | all-reduce | flops 262144 | bytes 1572864 | tf_op jit(solution)/shard_map/psum | solution.py:16
  158.5 7.1 %convolution_bitcast_fusion = f32[3584,512]{0,1:T(8,128)} fusion(bf16[512,3584]{1,0:T(8,128)(2,1)} %param.6, bf16[512,512]{1,0:T(8,128)(2,1)S(1)} %all-reduce.1), kind=kOutput, calls=%fused_computation.3 | convolution fusion | flops 1879048192 | bytes 11534336 | tf_op jit(solution)/shard_map/dot_general | solution.py:18
  165.6 8.4 %copy.28 = f32[3584,512]{1,0:T(8,128)} copy(f32[3584,512]{0,1:T(8,128)} %convolution_bitcast_fusion) | data formatting | bytes 14680064
  174.0 0.0 reduce-scatter.4.cloned.1.call-update
  174.0 0.2 all-gather.2.cloned.1.call-start
  174.3 0.3 all-gather.2.cloned.1.call-update
  174.6 0.3 copy-done.3
  174.9 0.1 copy.19
  175.1 0.0 copy-done.4
  175.1 0.1 copy.20
  175.2 248.7 %reduce-scatter.4.cloned.1.call-done = f32[112,512]{1,0:T(8,128)} async-done(((f32[3584,512]{1,0:T(8,128)}), f32[112,512]{1,0:T(8,128)}) %reduce-scatter.4.cloned.1.call-update) | async-done | bytes 229392
  423.9 1.1 copy.29
  424.9 0.1 bitcast_add_fusion
  425.0 0.0 copy-start.1
  425.0 0.0 all-gather.2.cloned.1.call-done
  425.1 6.3 %fusion.1 = bf16[1,112,8192]{2,1,0:T(8,128)(2,1)S(1)} fusion(bf16[8192,512]{1,0:T(8,128)(2,1)} %all-gather.2.cloned.1.call-done, f32[1,112,512]{1,2,0:T(8,128)S(1)} %get-tuple-element.13, f32[1,112,512]{1,2,0:T(8,128)S(1)} %get-tuple-element.12), kind=kOutput, calls=%fused_computation.2 | convolution fusion | flops 941645824 | bytes 10682368 | tf_op jit(solution)/shard_map/dot_general | solution.py:30
  431.4 6.9 %copy.21 = bf16[1,112,8192]{1,0,2:T(2,128)(2,1)} copy(bf16[1,112,8192]{2,1,0:T(8,128)(2,1)S(1)} %fusion.1) | data formatting | bytes 3670016 | tf_op jit(solution)/shard_map/broadcast_in_dim | solution.py:36
  438.2 0.5 broadcast.4
  438.8 45.2 %reduce = bf16[8192,112]{1,0:T(8,128)(2,1)S(1)} reduce(bf16[8192,1,112]{2,1,0:T(2,128)(2,1)} %bitcast.26, bf16[]{:T(256)} %broadcast.4), dimensions={1}, to_apply=%bitcast.19.reduce_sub_computation | reduce | bytes 3670018
  484.0 5.5 reshape.12
  489.5 12.3 %all-to-all-start = ((bf16[8,2,57344]{2,1,0:T(2,128)(2,1)}), bf16[8,2,57344]{2,1,0:T(2,128)(2,1)S(1)}, u32[]{:S(2)}, u32[]{:S(2)}) async-start(bf16[8,2,57344]{2,1,0:T(2,128)(2,1)} %reshape.12), calls=%async_computation | async-start | bytes 3670016 | tf_op jit(solution)/shard_map/all_to_all | solution.py:37
  501.8 0.0 copy-done.2
  501.8 0.8 copy.24
  502.6 0.8 copy.25
  503.4 36.2 %all-to-all-done = bf16[8,2,57344]{2,1,0:T(2,128)(2,1)S(1)} async-done(((bf16[8,2,57344]{2,1,0:T(2,128)(2,1)}), bf16[8,2,57344]{2,1,0:T(2,128)(2,1)S(1)}, u32[]{:S(2)}, u32[]{:S(2)}) %all-to-all-start) | async-done | bytes 1835040 | tf_op jit(solution)/shard_map/all_to_all | solution.py:37
  539.6 6.1 %reshape.13 = bf16[8192,1,112]{2,1,0:T(2,128)(2,1)} reshape(bf16[8,2,57344]{2,1,0:T(2,128)(2,1)S(1)} %all-to-all-done) | data formatting | bytes 3670016
  545.8 2.5 copy.30
  548.2 2.5 copy.23
  (4 shorter events, 0.0 us)
Async XLA Ops:
  8.0 1.2 copy-start
  8.0 415.8 %reduce-scatter.4.cloned.1.call-start = ((), (), s32[]{:S(2)}) async-start(), calls=%async_computation.3 | async-start | bytes 7569408
  174.0 0.9 copy-start.3
  174.0 1.1 copy-start.4
  174.0 251.0 %all-gather.2.cloned.1.call-start = ((), (), s32[]{:S(2)}) async-start(), calls=%async_computation.2 | async-start | bytes 9437184 | tf_op jit(solution)/shard_map/all_gather | solution.py:32
  425.0 6.4 %copy-start.1 = (f32[1,112,512]{1,2,0:T(8,128)}, f32[1,112,512]{1,2,0:T(8,128)S(1)}, u32[]{:S(2)}) copy-start(f32[1,112,512]{1,2,0:T(8,128)S(1)} %get-tuple-element.12) | copy-start | bytes 688132
  489.5 12.3 %copy-start.2 = (f32[1,112,512]{1,2,0:T(8,128)S(1)}, f32[1,112,512]{1,2,0:T(8,128)}, u32[]{:S(2)}) copy-start(f32[1,112,512]{1,2,0:T(8,128)} %copy-done.1) | copy-start | bytes 688132
  489.5 50.2 %all-to-all-start = ((bf16[8,2,57344]{2,1,0:T(2,128)(2,1)}), bf16[8,2,57344]{2,1,0:T(2,128)(2,1)S(1)}, u32[]{:S(2)}, u32[]{:S(2)}) async-start(bf16[8,2,57344]{2,1,0:T(2,128)(2,1)} %reshape.12), calls=%async_computation | async-start | bytes 3670016 | tf_op jit(solution)/shard_map/all_to_all | solution.py:37
Sparse Core Ops, SparseCore 0:
  174.1 249.6 reduce-scatter.3
Sparse Core Ops, SparseCore 1:
  177.1 170.5 all-gather.1
where the time goes:
time: 561 us; the launch traced here: 558 us
  waiting for transfers between devices  285 us (51%)
  blocking collectives  147 us (26%)
  other arithmetic  45.3 us (8%)
  local copies, waits for them, and re-layouts  36.9 us (7%)
  between operations  15.6 us (3%)
  matrix products  15.3 us (3%)
  starting transfers between devices  12.6 us (2%)
    unnamed x3, waiting for transfers between devices  249 us
    psum x1, blocking collectives, per_device(): projected = lax.psum(partial_proj, 'shard').astype(jnp.bfloat16)  147 us
    unnamed x1, other arithmetic  45.2 us
    all_to_all x1, waiting for transfers between devices, per_device(): lax.all_to_all(full_rows, 'shard', split_axis=2, concat_axis=0, tiled=True)  36.2 us
    unnamed x21, local copies, waits for them, and re-layouts  30 us
    all_to_all x1, starting transfers between devices, per_device(): lax.all_to_all(full_rows, 'shard', split_axis=2, concat_axis=0, tiled=True)  12.3 us
  transfers between devices with their start and end apart: 3, of which 2 were waited for; matrix products, arithmetic and copies ran while one was open for 1% of the time, Pallas kernels for 0%

commit v1 on v0

v1 whole, which is shorter than its diff:
```python
import functools

import jax
import jax.numpy as jnp
from jax import lax
from jax.experimental import pallas as pl
from jax.experimental.pallas import tpu as pltpu
from jax.sharding import PartitionSpec as P

beta_first = 0.9
beta_second = 0.99
correct_first = 0.9999734386011124
correct_second = 0.6339676587267705
epsilon = 1e-08
galore_scale = 4.0

bf16, f32 = jnp.bfloat16, jnp.float32
NY, NZ, NC, NX, NH = 4, 4, 2, 4, 2
VMEM = pl.BlockSpec(memory_space=pltpu.VMEM)
ANY = pl.BlockSpec(memory_space=pl.ANY)


def dp_perm(step):
    pairs = []
    for y in range(NY):
        for z in range(NZ):
            for c in range(NC):
                ty, tz, tc = step(y, z, c)
                pairs.append(((y * NZ + z) * NC + c, ((ty % NY) * NZ + tz) * NC + tc))
    return pairs


def shard_perm(step):
    pairs = []
    for x in range(NX):
        for h in range(NH):
            tx, th = step(x, h)
            pairs.append((x * NH + h, (tx % NX) * NH + th))
    return pairs


def to_core(a):
    return lax.ppermute(a, "dp", dp_perm(lambda y, z, c: (y, z, 1 - c)))


def to_y(a, k):
    return lax.ppermute(a, "dp", dp_perm(lambda y, z, c: (y + k, z, c)))


def to_z(a, k):
    return lax.ppermute(a, "dp", dp_perm(lambda y, z, c: (y, z ^ k, c)))


def to_x(a, k):
    return lax.ppermute(a, "shard", shard_perm(lambda x, h: (x + k, h)))


def to_h(a):
    return lax.ppermute(a, "shard", shard_perm(lambda x, h: (x, 1 - h)))


def place():
    dp, shard = lax.axis_index("dp"), lax.axis_index("shard")
    return dp // (NZ * NC), (dp // NC) % NZ, dp % NC, shard // NH, shard % NH


def call(body, outs, n_in, scratch=(), limit=16, **kw):
    return pl.pallas_call(
        body,
        out_shape=[jax.ShapeDtypeStruct(s, d) for s, d in outs],
        in_specs=kw.pop("in_specs", [VMEM] * n_in),
        out_specs=kw.pop("out_specs", [VMEM] * len(outs)),
        scratch_shapes=list(scratch),
        compiler_params=pltpu.CompilerParams(vmem_limit_bytes=limit << 20),
        **kw,
    )


def project_body(feat, basis, own, s1, s2, s3):
    _, _, _, x, _ = place()
    rows = own.shape[0]
    for k, out in ((2, s2), (1, s1), (3, s3), (0, own)):
        start = pl.multiple_of(lax.rem(x + k, NX) * rows, rows)
        part = jnp.dot(feat[pl.ds(start, rows), :], basis[...], preferred_element_type=f32)
        out[...] = part.astype(out.dtype)


def turn_body(grads, basis, keep, send, basis_t, tmp):
    y, z, c, x, _ = place()
    rows = keep.shape[2]
    wide = NZ * NC * rows
    toks = grads.shape[0] // NX
    for ry in range(NY):
        col = pl.multiple_of(lax.rem(y + ry, NY) * wide, 128)
        for k in range(NX):
            tok = pl.multiple_of(lax.rem(x + NX - k, NX) * toks, toks)
            tmp[:, k * toks : (k + 1) * toks] = grads[pl.ds(tok, toks), pl.ds(col, wide)].T
        for rz in range(NZ):
            for cc, out in ((0, keep), (1, send)):
                start = pl.multiple_of(((z ^ rz) * NC + (c ^ cc)) * rows, 16)
                out[ry, rz] = tmp[pl.ds(start, rows), :]
    basis_t[...] = basis[...].T


def sum_x_body(own, r1, r2, r3, total, sent):
    t = own[...] + r1[...].astype(f32) + r2[...].astype(f32) + r3[...].astype(f32)
    total[...] = t
    sent[...] = t.astype(bf16)


def sum_h_body(own, other, out):
    out[...] = (own[...] + other[...].astype(f32)).astype(bf16)


def low_body(keep, other, p0, p1, p2, p3, q, own, s1, s2, s3):
    pieces = (p0, p1, p2, p3)
    toks = p0.shape[0]
    proj = jnp.concatenate([p[...] for p in pieces], axis=0)
    for ry, out in ((2, s2), (1, s1), (3, s3), (0, own)):
        a = keep[ry].reshape(out.shape[0], NX * toks)
        b = other[ry].reshape(out.shape[0], NX * toks)
        part = jnp.dot(a, proj, preferred_element_type=f32)
        part += jnp.dot(b, q[...], preferred_element_type=f32)
        out[...] = part.astype(out.dtype)


def sum_y_body(own, r1, r2, r3, total, s1, s2, s3):
    rows = total.shape[0]
    for rz, out in ((3, s3), (2, s2), (1, s1), (0, total)):
        part = slice(rz * rows, (rz + 1) * rows)
        t = own[part, :] + r1[part, :].astype(f32) + r2[part, :].astype(f32) + r3[part, :].astype(f32)
        out[...] = t.astype(out.dtype)


def adam_body(own, r1, r2, r3, first, second, first_new, second_new, direction):
    g = own[...] + r1[...].astype(f32) + r2[...].astype(f32) + r3[...].astype(f32)
    m = beta_first * first[0] + (1.0 - beta_first) * g
    v = beta_second * second[0] + (1.0 - beta_second) * g * g
    first_new[0] = m
    second_new[0] = v
    d = m / correct_first / (jnp.sqrt(v / correct_second) + epsilon)
    direction[...] = d.astype(bf16)


def update_body(moves, aliased, *refs):
    n = len(moves)
    dirs, basis_t = refs[:n], refs[n]
    out, buf, sems = refs[n + 1 + aliased :]
    _, _, _, x, h = place()
    copies = []
    for i, (k, flip) in enumerate(moves):
        t = galore_scale * jnp.dot(dirs[i][...], basis_t[...], preferred_element_type=f32)
        buf[i] = t.astype(bf16)
        block = lax.rem(x + NX - k, NX) * NH + (h ^ flip)
        copy = pltpu.make_async_copy(buf.at[i], out.at[block], sems.at[i])
        copy.start()
        copies.append(copy)
    for copy in copies:
        copy.wait()


def update_part(moves, dirs, basis_t, out):
    n = len(moves)
    rows, rank = dirs[0].shape
    cols = basis_t.shape[1]
    aliased = 0 if out is None else 1
    args = (*dirs, basis_t) + ((out,) if aliased else ())
    return call(
        functools.partial(update_body, moves, aliased),
        [((NX * NH, rows, cols), bf16)],
        len(args),
        scratch=[pltpu.VMEM((n, rows, cols), bf16), pltpu.SemaphoreType.DMA((n,))],
        in_specs=[VMEM] * (n + 1) + [ANY] * aliased,
        out_specs=[ANY],
        input_output_aliases={n + 1: 0} if aliased else {},
    )(*args)[0]


def per_device(features, out_grads, proj_basis, first_moment, second_moment):
    tokens, _ = features.shape
    width, rank = proj_basis.shape
    rows = first_moment.shape[1]
    toks = tokens // NX

    own, s1, s2, s3 = call(
        project_body, [((toks, rank), f32)] + [((toks, rank), bf16)] * 3, 2
    )(features, proj_basis)
    r2, r1, r3 = to_x(s2, 2), to_x(s1, 1), to_x(s3, 3)

    block = (NY, NZ, rows, tokens)
    keep, send, basis_t = call(
        turn_body,
        [(block, bf16), (block, bf16), ((rank, width), bf16)],
        2,
        scratch=[pltpu.VMEM((NZ * NC * rows, tokens), bf16)],
    )(out_grads, proj_basis)
    other = to_core(send)

    total, sent = call(sum_x_body, [((toks, rank), f32), ((toks, rank), bf16)], 4)(own, r1, r2, r3)
    p0 = call(sum_h_body, [((toks, rank), bf16)], 2)(total, to_h(sent))[0]
    p2, p1, p3 = to_x(p0, 2), to_x(p0, 1), to_x(p0, 3)
    q = to_core(jnp.concatenate([p0, p1, p2, p3], axis=0))

    own, s1, s2, s3 = call(
        low_body, [((NZ * rows, rank), f32)] + [((NZ * rows, rank), bf16)] * 3, 7
    )(keep, other, p0, p1, p2, p3, q)
    r2, r1, r3 = to_y(s2, 2), to_y(s1, 1), to_y(s3, 3)
    own, s1, s2, s3 = call(
        sum_y_body, [((rows, rank), f32)] + [((rows, rank), bf16)] * 3, 4
    )(own, r1, r2, r3)
    r3, r2, r1 = to_z(s3, 3), to_z(s2, 2), to_z(s1, 1)
    first_new, second_new, d0 = call(
        adam_body, [((1, rows, rank), f32)] * 2 + [((rows, rank), bf16)], 6
    )(own, r1, r2, r3, first_moment, second_moment)

    e0 = to_h(d0)
    d2, d1, d3 = to_x(d0, 2), to_x(d0, 1), to_x(d0, 3)
    e2, e1, e3 = to_x(e0, 2), to_x(e0, 1), to_x(e0, 3)
    update = update_part([(0, 0)], [d0], basis_t, None)
    update = update_part([(1, 0), (2, 0), (3, 0), (0, 1)], [d1, d2, d3, e0], basis_t, update)
    update = update_part([(1, 1), (2, 1), (3, 1)], [e1, e2, e3], basis_t, update)
    return (update, first_new, second_new)


def solution(mesh):
    return jax.shard_map(
        per_device,
        mesh=mesh,
        in_specs=(
            P("dp", "shard"),
            P("dp", "shard"),
            P("shard", None),
            P("shard", "dp", None),
            P("shard", "dp", None),
        ),
        out_specs=(P(None, "dp", "shard"), P("shard", "dp", None), P("shard", "dp", None)),
        check_vma=False,
    )
```

time: 561 us -> 105 us (0.19)
  waiting for transfers between devices: 285 us -> 54 us
  blocking collectives: 147 us -> 0 us
  other arithmetic: 45.3 us -> 0.03 us
  local copies, waits for them, and re-layouts: 36.9 us -> 3.27 us
  starting transfers between devices: 12.6 us -> 36.3 us
  matrix products: 15.3 us -> 0 us
  between operations: 15.6 us -> 0.95 us
  Pallas kernels: 0 us -> 9.22 us
    unnamed x3 -> x0, waiting for transfers between devices: 249 us -> none
    psum x1 -> x0, blocking collectives: 147 us -> none  [per_device(): projected = lax.psum(partial_proj, 'shard').astype(jnp.bfloat16)]
    ppermute x0 -> x22, waiting for transfers between devices: none -> 54 us  [the longest x3 19 us: to_y(): return lax.ppermute(a, 'dp', dp_perm(lambda y, z, c: (y + k, z, c)))]
    unnamed x1 -> x0, other arithmetic: 45.2 us -> none
    ppermute x0 -> x22, starting transfers between devices: none -> 36.3 us  [the longest x12 14.7 us: to_x(): return lax.ppermute(a, 'shard', shard_perm(lambda x, h: (x + k, h)))]
    all_to_all x1 -> x0, waiting for transfers between devices: 36.2 us -> none  [per_device(): lax.all_to_all(full_rows, 'shard', split_axis=2, concat_axis=0, tiled=True)]
    unnamed x21 -> x10, local copies, waits for them, and re-layouts: 30 us -> 3.27 us
    dot_general x3 -> x0, matrix products: 15.3 us -> none  [the longest x1 7.08 us: per_device(): lax.dot_general(out_grads, projected, (((0,), (0,)), ((), ())), preferred...]
  transfers between devices with their start and end apart: 3 -> 22, of which waited for: 2 -> 15; matrix products, arithmetic and copies ran while one was open for 1% -> 0% of each run, Pallas kernels for 0% -> 3%
where the time goes in v1:
time: 105 us; the launch traced here: 104 us
  waiting for transfers between devices  54 us (51%)
  starting transfers between devices  36.3 us (35%)
  Pallas kernels  9.22 us (9%)
  local copies, waits for them, and re-layouts  3.27 us (3%)
    ppermute x3, waiting for transfers between devices, to_y(): return lax.ppermute(a, 'dp', dp_perm(lambda y, z, c: (y + k, z, c)))  19 us
    ppermute x12, starting transfers between devices, to_x(): return lax.ppermute(a, 'shard', shard_perm(lambda x, h: (x + k, h)))  14.7 us
    ppermute x12, waiting for transfers between devices, to_x(): return lax.ppermute(a, 'shard', shard_perm(lambda x, h: (x + k, h)))  14.6 us
    ppermute x2, starting transfers between devices, to_h(): return lax.ppermute(a, 'shard', shard_perm(lambda x, h: (x, 1 - h)))  11.9 us
    ppermute x3, waiting for transfers between devices, to_z(): return lax.ppermute(a, 'dp', dp_perm(lambda y, z, c: (y, z ^ k, c)))  9.7 us
    ppermute x2, waiting for transfers between devices, to_h(): return lax.ppermute(a, 'shard', shard_perm(lambda x, h: (x, 1 - h)))  8.72 us
    ppermute x3, starting transfers between devices, to_y(): return lax.ppermute(a, 'dp', dp_perm(lambda y, z, c: (y + k, z, c)))  5.88 us
    pallas_call x3, Pallas kernels, update_part(): call(functools.partial(update_body, moves, aliased), [((NX * NH, rows, co...  3.81 us
  transfers between devices with their start and end apart: 22, of which 15 were waited for; matrix products, arithmetic and copies ran while one was open for 0% of the time, Pallas kernels for 3%

profile of v1, /device:TPU:32, one launch (start us, length us, event | category | flops | bytes accessed | tf_op | source)
XLA Modules:
  0.0 103.7 jit_solution(13398381644397647552)
XLA Ops:
  0.6 1.2 %copy-done = bf16[1024,512]{1,0:T(8,128)(2,1)S(1)} copy-done((bf16[1024,512]{1,0:T(8,128)(2,1)S(1)}, bf16[1024,512]{1,0:T(8,128)(2,1)}, u32[]{:S(2)}) %copy-start) | copy-done | bytes 1048600
  1.9 2.0 %copy-done.1 = bf16[512,3584]{1,0:T(8,128)(2,1)S(1)} copy-done((bf16[512,3584]{1,0:T(8,128)(2,1)S(1)}, bf16[512,3584]{1,0:T(8,128)(2,1)}, u32[]{:S(2)}) %copy-start.1) | copy-done | bytes 3670040
  3.9 1.5 %shard_map.76 = (bf16[4,4,112,512]{3,2,1,0:T(8,128)(2,1)S(1)}, bf16[4,4,112,512]{3,2,1,0:T(8,128)(2,1)S(1)}, bf16[512,1024]{1,0:T(8,128)(2,1)S(1)}) custom-call(bf16[512,3584]{1,0:T(8,128)(2,1)S(1)} %copy-done.1, bf16[1024,512]{1,0:T(8,128)(2,1)S(1)} %copy-done), custom_call_target="tpu_custom_call" | custom-call | tf_op jit(solution)/shard_map/pallas_call | solution.py:191
  6.2 1.6 %collective-permute-start.1 = (bf16[128,512]{1,0:T(8,128)(2,1)S(1)}, bf16[128,512]{1,0:T(8,128)(2,1)S(1)}, u32[]{:S(2)}, u32[]{:S(2)}) collective-permute-start(bf16[128,512]{1,0:T(8,128)(2,1)S(1)} %get-tuple-element.26), channel_id=1, source_target_pairs={{0,2},{1,3},{2,4},{3,5},{4,6},{5,7},{6,0},{7,1},{8,10},{9,11},{10,... | collective-permute-start | bytes 393224 | tf_op jit(solution)/shard_map/ppermute | solution.py:55
  7.8 2.7 %collective-permute-start.2 = (bf16[128,512]{1,0:T(8,128)(2,1)S(1)}, bf16[128,512]{1,0:T(8,128)(2,1)S(1)}, u32[]{:S(2)}, u32[]{:S(2)}) collective-permute-start(bf16[128,512]{1,0:T(8,128)(2,1)S(1)} %get-tuple-element.27), channel_id=1, source_target_pairs={{0,4},{1,5},{2,6},{3,7},{4,0},{5,1},{6,2},{7,3},{8,12},{9,13},{10,... | collective-permute-start | bytes 393224 | tf_op jit(solution)/shard_map/ppermute | solution.py:55
  10.5 1.4 %collective-permute-start.3 = (bf16[128,512]{1,0:T(8,128)(2,1)S(1)}, bf16[128,512]{1,0:T(8,128)(2,1)S(1)}, u32[]{:S(2)}, u32[]{:S(2)}) collective-permute-start(bf16[128,512]{1,0:T(8,128)(2,1)S(1)} %get-tuple-element.28), channel_id=1, source_target_pairs={{0,6},{1,7},{2,0},{3,1},{4,2},{5,3},{6,4},{7,5},{8,14},{9,15},{10,... | collective-permute-start | bytes 393224 | tf_op jit(solution)/shard_map/ppermute | solution.py:55
  11.9 1.4 %collective-permute-done.1.r1 = bf16[128,512]{1,0:T(8,128)(2,1)S(1)} collective-permute-done((bf16[128,512]{1,0:T(8,128)(2,1)S(1)}, bf16[128,512]{1,0:T(8,128)(2,1)S(1)}, u32[]{:S(2)}, u32[]{:S(2)}) %collective-permute-start.1) | collective-permute-done | bytes 131104 | tf_op jit(solution)/shard_map/ppermute | solution.py:55
  13.4 3.8 %collective-permute-done.2.r2 = bf16[128,512]{1,0:T(8,128)(2,1)S(1)} collective-permute-done((bf16[128,512]{1,0:T(8,128)(2,1)S(1)}, bf16[128,512]{1,0:T(8,128)(2,1)S(1)}, u32[]{:S(2)}, u32[]{:S(2)}) %collective-permute-start.2) | collective-permute-done | bytes 131104 | tf_op jit(solution)/shard_map/ppermute | solution.py:55
  17.3 6.4 %collective-permute-start.4 = (bf16[128,512]{1,0:T(8,128)(2,1)S(1)}, bf16[128,512]{1,0:T(8,128)(2,1)S(1)}, u32[]{:S(2)}, u32[]{:S(2)}) collective-permute-start(bf16[128,512]{1,0:T(8,128)(2,1)S(1)} %get-tuple-element.30), channel_id=1, source_target_pairs={{0,1},{1,0},{2,3},{3,2},{4,5},{5,4},{6,7},{7,6},{8,9},{9,8},{10,11... | collective-permute-start | bytes 393224 | tf_op jit(solution)/shard_map/ppermute | solution.py:59
  23.6 6.2 %collective-permute-done.4.other = bf16[128,512]{1,0:T(8,128)(2,1)S(1)} collective-permute-done((bf16[128,512]{1,0:T(8,128)(2,1)S(1)}, bf16[128,512]{1,0:T(8,128)(2,1)S(1)}, u32[]{:S(2)}, u32[]{:S(2)}) %collective-permute-start.4) | collective-permute-done | bytes 131104 | tf_op jit(solution)/shard_map/ppermute | solution.py:59
  29.9 2.3 %collective-permute-start.7 = (bf16[128,512]{1,0:T(8,128)(2,1)S(1)}, bf16[128,512]{1,0:T(8,128)(2,1)S(1)}, u32[]{:S(2)}, u32[]{:S(2)}) collective-permute-start(bf16[128,512]{1,0:T(8,128)(2,1)S(1)} %shard_map.79.p0), channel_id=1, source_target_pairs={{0,6},{1,7},{2,0},{3,1},{4,2},{5,3},{6,4},{7,5},{8,14},{9,15},{10,... | collective-permute-start | bytes 393224 | tf_op jit(solution)/shard_map/ppermute | solution.py:55
  33.7 2.4 %collective-permute-done.7.p3 = bf16[128,512]{1,0:T(8,128)(2,1)S(1)} collective-permute-done((bf16[128,512]{1,0:T(8,128)(2,1)S(1)}, bf16[128,512]{1,0:T(8,128)(2,1)S(1)}, u32[]{:S(2)}, u32[]{:S(2)}) %collective-permute-start.7) | collective-permute-done | bytes 131104 | tf_op jit(solution)/shard_map/ppermute | solution.py:55
  36.2 2.6 %collective-permute-done.6.p2 = bf16[128,512]{1,0:T(8,128)(2,1)S(1)} collective-permute-done((bf16[128,512]{1,0:T(8,128)(2,1)S(1)}, bf16[128,512]{1,0:T(8,128)(2,1)S(1)}, u32[]{:S(2)}, u32[]{:S(2)}) %collective-permute-start.6) | collective-permute-done | bytes 131104 | tf_op jit(solution)/shard_map/ppermute | solution.py:55
  38.8 1.3 %collective-permute-done.5.p1 = bf16[128,512]{1,0:T(8,128)(2,1)S(1)} collective-permute-done((bf16[128,512]{1,0:T(8,128)(2,1)S(1)}, bf16[128,512]{1,0:T(8,128)(2,1)S(1)}, u32[]{:S(2)}, u32[]{:S(2)}) %collective-permute-start.5) | collective-permute-done | bytes 131104 | tf_op jit(solution)/shard_map/ppermute | solution.py:55
  40.2 1.9 %collective-permute-done.8.q = bf16[512,512]{1,0:T(8,128)(2,1)S(1)} collective-permute-done((bf16[512,512]{1,0:T(8,128)(2,1)S(1)}, bf16[512,512]{1,0:T(8,128)(2,1)S(1)}, u32[]{:S(2)}, u32[]{:S(2)}) %collective-permute-start.8) | collective-permute-done | bytes 524320 | tf_op jit(solution)/shard_map/ppermute | solution.py:43
  42.1 2.1 %shard_map.80 = (f32[448,512]{1,0:T(8,128)S(1)}, bf16[448,512]{1,0:T(8,128)(2,1)S(1)}, bf16[448,512]{1,0:T(8,128)(2,1)S(1)}, bf16[448,512]{1,0:T(8,128)(2,1)S(1)}) custom-call(bf16[4,4,112,512]{3,2,1,0:T(8,128)(2,1)S(1)} %get-tuple-element.23.keep, bf16[4,4,112,512]{3,2,1,0:T(8,128)(2,1)S(1)} %collective-permute-done.other, ...), custom_call_target="tpu_custom_call" | custom-call | tf_op jit(solution)/shard_map/pallas_call | solution.py:204
  44.2 1.6 %collective-permute-start.9 = (bf16[448,512]{1,0:T(8,128)(2,1)S(1)}, bf16[448,512]{1,0:T(8,128)(2,1)S(1)}, u32[]{:S(2)}, u32[]{:S(2)}) collective-permute-start(bf16[448,512]{1,0:T(8,128)(2,1)S(1)} %get-tuple-element.32), channel_id=1, source_target_pairs={{0,64},{8,72},{16,80},{24,88},{32,96},{40,104},{48,112},{56,120},{... | collective-permute-start | bytes 1376264 | tf_op jit(solution)/shard_map/ppermute | solution.py:47
  45.9 2.9 %collective-permute-start.10 = (bf16[448,512]{1,0:T(8,128)(2,1)S(1)}, bf16[448,512]{1,0:T(8,128)(2,1)S(1)}, u32[]{:S(2)}, u32[]{:S(2)}) collective-permute-start(bf16[448,512]{1,0:T(8,128)(2,1)S(1)} %get-tuple-element.33), channel_id=1, source_target_pairs={{0,128},{8,136},{16,144},{24,152},{32,160},{40,168},{48,176},{56,1... | collective-permute-start | bytes 1376264 | tf_op jit(solution)/shard_map/ppermute | solution.py:47
  48.8 1.3 %collective-permute-start.11 = (bf16[448,512]{1,0:T(8,128)(2,1)S(1)}, bf16[448,512]{1,0:T(8,128)(2,1)S(1)}, u32[]{:S(2)}, u32[]{:S(2)}) collective-permute-start(bf16[448,512]{1,0:T(8,128)(2,1)S(1)} %get-tuple-element.34), channel_id=1, source_target_pairs={{0,192},{8,200},{16,208},{24,216},{32,224},{40,232},{48,240},{56,2... | collective-permute-start | bytes 1376264 | tf_op jit(solution)/shard_map/ppermute | solution.py:47
  50.1 8.0 %collective-permute-done.9.r1 = bf16[448,512]{1,0:T(8,128)(2,1)S(1)} collective-permute-done((bf16[448,512]{1,0:T(8,128)(2,1)S(1)}, bf16[448,512]{1,0:T(8,128)(2,1)S(1)}, u32[]{:S(2)}, u32[]{:S(2)}) %collective-permute-start.9) | collective-permute-done | bytes 458784 | tf_op jit(solution)/shard_map/ppermute | solution.py:47
  58.1 11.0 %collective-permute-done.10.r2 = bf16[448,512]{1,0:T(8,128)(2,1)S(1)} collective-permute-done((bf16[448,512]{1,0:T(8,128)(2,1)S(1)}, bf16[448,512]{1,0:T(8,128)(2,1)S(1)}, u32[]{:S(2)}, u32[]{:S(2)}) %collective-permute-start.10) | collective-permute-done | bytes 458784 | tf_op jit(solution)/shard_map/ppermute | solution.py:47
  69.4 3.6 %collective-permute-start.13 = (bf16[112,512]{1,0:T(8,128)(2,1)S(1)}, bf16[112,512]{1,0:T(8,128)(2,1)S(1)}, u32[]{:S(2)}, u32[]{:S(2)}) collective-permute-start(bf16[112,512]{1,0:T(8,128)(2,1)S(1)} %get-tuple-element.37), channel_id=1, source_target_pairs={{0,32},{8,40},{16,48},{24,56},{32,0},{40,8},{48,16},{56,24},{64,96... | collective-permute-start | bytes 344072 | tf_op jit(solution)/shard_map/ppermute | solution.py:51
  73.0 2.2 %collective-permute-done.12.r1 = bf16[112,512]{1,0:T(8,128)(2,1)S(1)} collective-permute-done((bf16[112,512]{1,0:T(8,128)(2,1)S(1)}, bf16[112,512]{1,0:T(8,128)(2,1)S(1)}, u32[]{:S(2)}, u32[]{:S(2)}) %collective-permute-start.12) | collective-permute-done | bytes 114720 | tf_op jit(solution)/shard_map/ppermute | solution.py:51
  75.2 5.4 %collective-permute-done.13.r2 = bf16[112,512]{1,0:T(8,128)(2,1)S(1)} collective-permute-done((bf16[112,512]{1,0:T(8,128)(2,1)S(1)}, bf16[112,512]{1,0:T(8,128)(2,1)S(1)}, u32[]{:S(2)}, u32[]{:S(2)}) %collective-permute-start.13) | collective-permute-done | bytes 114720 | tf_op jit(solution)/shard_map/ppermute | solution.py:51
  80.6 2.2 %collective-permute-done.14.r3 = bf16[112,512]{1,0:T(8,128)(2,1)S(1)} collective-permute-done((bf16[112,512]{1,0:T(8,128)(2,1)S(1)}, bf16[112,512]{1,0:T(8,128)(2,1)S(1)}, u32[]{:S(2)}, u32[]{:S(2)}) %collective-permute-start.14) | collective-permute-done | bytes 114720 | tf_op jit(solution)/shard_map/ppermute | solution.py:51
  83.6 5.5 %collective-permute-start.15 = (bf16[112,512]{1,0:T(8,128)(2,1)S(1)}, bf16[112,512]{1,0:T(8,128)(2,1)S(1)}, u32[]{:S(2)}, u32[]{:S(2)}) collective-permute-start(bf16[112,512]{1,0:T(8,128)(2,1)S(1)} %get-tuple-element.39.refs_0_), channel_id=1, source_target_pairs={{0,1},{1,0},{2,3},{3,2},{4,5},{5,4},{6,7},{7,6},{8,9},{9,8},{10,11... | collective-permute-start | bytes 344072 | tf_op jit(solution)/shard_map/ppermute | solution.py:59
  91.2 2.5 %collective-permute-done.15.refs_3_ = bf16[112,512]{1,0:T(8,128)(2,1)S(1)} collective-permute-done((bf16[112,512]{1,0:T(8,128)(2,1)S(1)}, bf16[112,512]{1,0:T(8,128)(2,1)S(1)}, u32[]{:S(2)}, u32[]{:S(2)}) %collective-permute-start.15) | collective-permute-done | bytes 114720 | tf_op jit(solution)/shard_map/ppermute | solution.py:59
  94.2 1.1 %collective-permute-start.17 = (bf16[112,512]{1,0:T(8,128)(2,1)S(1)}, bf16[112,512]{1,0:T(8,128)(2,1)S(1)}, u32[]{:S(2)}, u32[]{:S(2)}) collective-permute-start(bf16[112,512]{1,0:T(8,128)(2,1)S(1)} %collective-permute-done.15.refs_3_), channel_id=1, source_target_pairs={{0,4},{1,5},{2,6},{3,7},{4,0},{5,1},{6,2},{7,3},{8,12},{9,13},{10,... | collective-permute-start | bytes 344072 | tf_op jit(solution)/shard_map/ppermute | solution.py:55
  95.4 1.4 %collective-permute-start.16 = (bf16[112,512]{1,0:T(8,128)(2,1)S(1)}, bf16[112,512]{1,0:T(8,128)(2,1)S(1)}, u32[]{:S(2)}, u32[]{:S(2)}) collective-permute-start(bf16[112,512]{1,0:T(8,128)(2,1)S(1)} %collective-permute-done.15.refs_3_), channel_id=1, source_target_pairs={{0,2},{1,3},{2,4},{3,5},{4,6},{5,7},{6,0},{7,1},{8,10},{9,11},{10,... | collective-permute-start | bytes 344072 | tf_op jit(solution)/shard_map/ppermute | solution.py:55
  97.7 2.3 %collective-permute-done.19.refs_0_ = bf16[112,512]{1,0:T(8,128)(2,1)S(1)} collective-permute-done((bf16[112,512]{1,0:T(8,128)(2,1)S(1)}, bf16[112,512]{1,0:T(8,128)(2,1)S(1)}, u32[]{:S(2)}, u32[]{:S(2)}) %collective-permute-start.19) | collective-permute-done | bytes 114720 | tf_op jit(solution)/shard_map/ppermute | solution.py:55
  100.0 1.5 %shard_map.84.refs_4_ = bf16[8,112,1024]{2,1,0:T(8,128)(2,1)} custom-call(bf16[112,512]{1,0:T(8,128)(2,1)S(1)} %collective-permute-done.19.refs_0_, bf16[112,512]{1,0:T(8,128)(2,1)S(1)} %collective-permute-done.20.refs_1_, bf16[112,512]{1,0:T(8,128)(2,1)S(1)} %collective-permute-done.21.refs_2_, ...), custom_call_target="tpu_custom_call", output_to_operand_aliasing={{}: (5, {})} | custom-call | tf_op jit(solution)/shard_map/pallas_call | solution.py:168
  102.2 1.3 %shard_map.85 = bf16[8,112,1024]{2,1,0:T(8,128)(2,1)} custom-call(bf16[112,512]{1,0:T(8,128)(2,1)S(1)} %collective-permute-done.16.refs_0_, bf16[112,512]{1,0:T(8,128)(2,1)S(1)} %collective-permute-done.17.refs_1_, bf16[112,512]{1,0:T(8,128)(2,1)S(1)} %collective-permute-done.18.refs_2_, ...), custom_call_target="tpu_custom_call", output_to_operand_aliasing={{}: (4, {})} | custom-call | tf_op jit(solution)/shard_map/pallas_call | solution.py:168
  (33 shorter events, 8.1 us)
Async XLA Ops:
  0.6 1.2 %copy-start = (bf16[1024,512]{1,0:T(8,128)(2,1)S(1)}, bf16[1024,512]{1,0:T(8,128)(2,1)}, u32[]{:S(2)}) copy-start(bf16[1024,512]{1,0:T(8,128)(2,1)} %basis.3) | copy-start | bytes 3145732
  1.9 2.0 %copy-start.1 = (bf16[512,3584]{1,0:T(8,128)(2,1)S(1)}, bf16[512,3584]{1,0:T(8,128)(2,1)}, u32[]{:S(2)}) copy-start(bf16[512,3584]{1,0:T(8,128)(2,1)} %grads.1) | copy-start | bytes 11010052
  3.9 1.6 %copy-start.2 = (bf16[512,1024]{1,0:T(8,128)(2,1)S(1)}, bf16[512,1024]{1,0:T(8,128)(2,1)}, u32[]{:S(2)}) copy-start(bf16[512,1024]{1,0:T(8,128)(2,1)} %feat.1) | copy-start | bytes 3145732
  5.4 36.8 %collective-permute-start = (bf16[4,4,112,512]{3,2,1,0:T(8,128)(2,1)S(1)}, bf16[4,4,112,512]{3,2,1,0:T(8,128)(2,1)S(1)}, u32[]{:S(2)}, u32[]{:S(2)}) collective-permute-start(bf16[4,4,112,512]{3,2,1,0:T(8,128)(2,1)S(1)} %get-tuple-element.24), channel_id=1, source_target_pairs={{0,8},{8,0},{16,24},{24,16},{32,40},{40,32},{48,56},{56,48},{64,72... | collective-permute-start | bytes 5505032 | tf_op jit(solution)/shard_map/ppermute | solution.py:43
  6.2 7.2 %collective-permute-start.1 = (bf16[128,512]{1,0:T(8,128)(2,1)S(1)}, bf16[128,512]{1,0:T(8,128)(2,1)S(1)}, u32[]{:S(2)}, u32[]{:S(2)}) collective-permute-start(bf16[128,512]{1,0:T(8,128)(2,1)S(1)} %get-tuple-element.26), channel_id=1, source_target_pairs={{0,2},{1,3},{2,4},{3,5},{4,6},{5,7},{6,0},{7,1},{8,10},{9,11},{10,... | collective-permute-start | bytes 393224 | tf_op jit(solution)/shard_map/ppermute | solution.py:55
  7.8 9.4 %collective-permute-start.2 = (bf16[128,512]{1,0:T(8,128)(2,1)S(1)}, bf16[128,512]{1,0:T(8,128)(2,1)S(1)}, u32[]{:S(2)}, u32[]{:S(2)}) collective-permute-start(bf16[128,512]{1,0:T(8,128)(2,1)S(1)} %get-tuple-element.27), channel_id=1, source_target_pairs={{0,4},{1,5},{2,6},{3,7},{4,0},{5,1},{6,2},{7,3},{8,12},{9,13},{10,... | collective-permute-start | bytes 393224 | tf_op jit(solution)/shard_map/ppermute | solution.py:55
  10.5 6.7 %collective-permute-start.3 = (bf16[128,512]{1,0:T(8,128)(2,1)S(1)}, bf16[128,512]{1,0:T(8,128)(2,1)S(1)}, u32[]{:S(2)}, u32[]{:S(2)}) collective-permute-start(bf16[128,512]{1,0:T(8,128)(2,1)S(1)} %get-tuple-element.28), channel_id=1, source_target_pairs={{0,6},{1,7},{2,0},{3,1},{4,2},{5,3},{6,4},{7,5},{8,14},{9,15},{10,... | collective-permute-start | bytes 393224 | tf_op jit(solution)/shard_map/ppermute | solution.py:55
  17.3 12.6 %collective-permute-start.4 = (bf16[128,512]{1,0:T(8,128)(2,1)S(1)}, bf16[128,512]{1,0:T(8,128)(2,1)S(1)}, u32[]{:S(2)}, u32[]{:S(2)}) collective-permute-start(bf16[128,512]{1,0:T(8,128)(2,1)S(1)} %get-tuple-element.30), channel_id=1, source_target_pairs={{0,1},{1,0},{2,3},{3,2},{4,5},{5,4},{6,7},{7,6},{8,9},{9,8},{10,11... | collective-permute-start | bytes 393224 | tf_op jit(solution)/shard_map/ppermute | solution.py:59
  29.9 6.3 %collective-permute-start.7 = (bf16[128,512]{1,0:T(8,128)(2,1)S(1)}, bf16[128,512]{1,0:T(8,128)(2,1)S(1)}, u32[]{:S(2)}, u32[]{:S(2)}) collective-permute-start(bf16[128,512]{1,0:T(8,128)(2,1)S(1)} %shard_map.79.p0), channel_id=1, source_target_pairs={{0,6},{1,7},{2,0},{3,1},{4,2},{5,3},{6,4},{7,5},{8,14},{9,15},{10,... | collective-permute-start | bytes 393224 | tf_op jit(solution)/shard_map/ppermute | solution.py:55
  32.2 6.6 %collective-permute-start.6 = (bf16[128,512]{1,0:T(8,128)(2,1)S(1)}, bf16[128,512]{1,0:T(8,128)(2,1)S(1)}, u32[]{:S(2)}, u32[]{:S(2)}) collective-permute-start(bf16[128,512]{1,0:T(8,128)(2,1)S(1)} %shard_map.79.p0), channel_id=1, source_target_pairs={{0,4},{1,5},{2,6},{3,7},{4,0},{5,1},{6,2},{7,3},{8,12},{9,13},{10,... | collective-permute-start | bytes 393224 | tf_op jit(solution)/shard_map/ppermute | solution.py:55
  33.0 7.1 %collective-permute-start.5 = (bf16[128,512]{1,0:T(8,128)(2,1)S(1)}, bf16[128,512]{1,0:T(8,128)(2,1)S(1)}, u32[]{:S(2)}, u32[]{:S(2)}) collective-permute-start(bf16[128,512]{1,0:T(8,128)(2,1)S(1)} %shard_map.79.p0), channel_id=1, source_target_pairs={{0,2},{1,3},{2,4},{3,5},{4,6},{5,7},{6,0},{7,1},{8,10},{9,11},{10,... | collective-permute-start | bytes 393224 | tf_op jit(solution)/shard_map/ppermute | solution.py:55
  40.1 2.0 %collective-permute-start.8 = (bf16[512,512]{1,0:T(8,128)(2,1)S(1)}, bf16[512,512]{1,0:T(8,128)(2,1)S(1)}, u32[]{:S(2)}, u32[]{:S(2)}) collective-permute-start(bf16[512,512]{1,0:T(8,128)(2,1)S(1)} %pad_maximum_fusion), channel_id=1, source_target_pairs={{0,8},{8,0},{16,24},{24,16},{32,40},{40,32},{48,56},{56,48},{64,72... | collective-permute-start | bytes 1572872 | tf_op jit(solution)/shard_map/ppermute | solution.py:43
  44.2 38.5 %copy-start.3 = (f32[1,112,512]{2,1,0:T(8,128)S(1)}, f32[1,112,512]{2,1,0:T(8,128)}, u32[]{:S(2)}) copy-start(f32[1,112,512]{2,1,0:T(8,128)} %first.1) | copy-start | bytes 688132
  44.2 38.5 %copy-start.4 = (f32[1,112,512]{2,1,0:T(8,128)S(1)}, f32[1,112,512]{2,1,0:T(8,128)}, u32[]{:S(2)}) copy-start(f32[1,112,512]{2,1,0:T(8,128)} %second.1) | copy-start | bytes 688132
  44.2 13.9 %collective-permute-start.9 = (bf16[448,512]{1,0:T(8,128)(2,1)S(1)}, bf16[448,512]{1,0:T(8,128)(2,1)S(1)}, u32[]{:S(2)}, u32[]{:S(2)}) collective-permute-start(bf16[448,512]{1,0:T(8,128)(2,1)S(1)} %get-tuple-element.32), channel_id=1, source_target_pairs={{0,64},{8,72},{16,80},{24,88},{32,96},{40,104},{48,112},{56,120},{... | collective-permute-start | bytes 1376264 | tf_op jit(solution)/shard_map/ppermute | solution.py:47
  45.9 23.3 %collective-permute-start.10 = (bf16[448,512]{1,0:T(8,128)(2,1)S(1)}, bf16[448,512]{1,0:T(8,128)(2,1)S(1)}, u32[]{:S(2)}, u32[]{:S(2)}) collective-permute-start(bf16[448,512]{1,0:T(8,128)(2,1)S(1)} %get-tuple-element.33), channel_id=1, source_target_pairs={{0,128},{8,136},{16,144},{24,152},{32,160},{40,168},{48,176},{56,1... | collective-permute-start | bytes 1376264 | tf_op jit(solution)/shard_map/ppermute | solution.py:47
  48.8 20.4 %collective-permute-start.11 = (bf16[448,512]{1,0:T(8,128)(2,1)S(1)}, bf16[448,512]{1,0:T(8,128)(2,1)S(1)}, u32[]{:S(2)}, u32[]{:S(2)}) collective-permute-start(bf16[448,512]{1,0:T(8,128)(2,1)S(1)} %get-tuple-element.34), channel_id=1, source_target_pairs={{0,192},{8,200},{16,208},{24,216},{32,224},{40,232},{48,240},{56,2... | collective-permute-start | bytes 1376264 | tf_op jit(solution)/shard_map/ppermute | solution.py:47
  69.3 5.9 %collective-permute-start.12 = (bf16[112,512]{1,0:T(8,128)(2,1)S(1)}, bf16[112,512]{1,0:T(8,128)(2,1)S(1)}, u32[]{:S(2)}, u32[]{:S(2)}) collective-permute-start(bf16[112,512]{1,0:T(8,128)(2,1)S(1)} %get-tuple-element.36), channel_id=1, source_target_pairs={{0,16},{8,24},{16,0},{24,8},{32,48},{40,56},{48,32},{56,40},{64,80... | collective-permute-start | bytes 344072 | tf_op jit(solution)/shard_map/ppermute | solution.py:51
  69.4 11.2 %collective-permute-start.13 = (bf16[112,512]{1,0:T(8,128)(2,1)S(1)}, bf16[112,512]{1,0:T(8,128)(2,1)S(1)}, u32[]{:S(2)}, u32[]{:S(2)}) collective-permute-start(bf16[112,512]{1,0:T(8,128)(2,1)S(1)} %get-tuple-element.37), channel_id=1, source_target_pairs={{0,32},{8,40},{16,48},{24,56},{32,0},{40,8},{48,16},{56,24},{64,96... | collective-permute-start | bytes 344072 | tf_op jit(solution)/shard_map/ppermute | solution.py:51
  73.0 9.7 %collective-permute-start.14 = (bf16[112,512]{1,0:T(8,128)(2,1)S(1)}, bf16[112,512]{1,0:T(8,128)(2,1)S(1)}, u32[]{:S(2)}, u32[]{:S(2)}) collective-permute-start(bf16[112,512]{1,0:T(8,128)(2,1)S(1)} %get-tuple-element.38), channel_id=1, source_target_pairs={{0,48},{8,56},{16,32},{24,40},{32,16},{40,24},{48,0},{56,8},{64,11... | collective-permute-start | bytes 344072 | tf_op jit(solution)/shard_map/ppermute | solution.py:51
  83.6 10.1 %collective-permute-start.15 = (bf16[112,512]{1,0:T(8,128)(2,1)S(1)}, bf16[112,512]{1,0:T(8,128)(2,1)S(1)}, u32[]{:S(2)}, u32[]{:S(2)}) collective-permute-start(bf16[112,512]{1,0:T(8,128)(2,1)S(1)} %get-tuple-element.39.refs_0_), channel_id=1, source_target_pairs={{0,1},{1,0},{2,3},{3,2},{4,5},{5,4},{6,7},{7,6},{8,9},{9,8},{10,11... | collective-permute-start | bytes 344072 | tf_op jit(solution)/shard_map/ppermute | solution.py:59
  89.1 6.2 %collective-permute-start.21 = (bf16[112,512]{1,0:T(8,128)(2,1)S(1)}, bf16[112,512]{1,0:T(8,128)(2,1)S(1)}, u32[]{:S(2)}, u32[]{:S(2)}) collective-permute-start(bf16[112,512]{1,0:T(8,128)(2,1)S(1)} %get-tuple-element.39.refs_0_), channel_id=1, source_target_pairs={{0,6},{1,7},{2,0},{3,1},{4,2},{5,3},{6,4},{7,5},{8,14},{9,15},{10,... | collective-permute-start | bytes 344072 | tf_op jit(solution)/shard_map/ppermute | solution.py:55
  89.8 7.9 %collective-permute-start.20 = (bf16[112,512]{1,0:T(8,128)(2,1)S(1)}, bf16[112,512]{1,0:T(8,128)(2,1)S(1)}, u32[]{:S(2)}, u32[]{:S(2)}) collective-permute-start(bf16[112,512]{1,0:T(8,128)(2,1)S(1)} %get-tuple-element.39.refs_0_), channel_id=1, source_target_pairs={{0,4},{1,5},{2,6},{3,7},{4,0},{5,1},{6,2},{7,3},{8,12},{9,13},{10,... | collective-permute-start | bytes 344072 | tf_op jit(solution)/shard_map/ppermute | solution.py:55
  90.3 9.7 %collective-permute-start.19 = (bf16[112,512]{1,0:T(8,128)(2,1)S(1)}, bf16[112,512]{1,0:T(8,128)(2,1)S(1)}, u32[]{:S(2)}, u32[]{:S(2)}) collective-permute-start(bf16[112,512]{1,0:T(8,128)(2,1)S(1)} %get-tuple-element.39.refs_0_), channel_id=1, source_target_pairs={{0,2},{1,3},{2,4},{3,5},{4,6},{5,7},{6,0},{7,1},{8,10},{9,11},{10,... | collective-permute-start | bytes 344072 | tf_op jit(solution)/shard_map/ppermute | solution.py:55
  93.7 7.8 %collective-permute-start.18 = (bf16[112,512]{1,0:T(8,128)(2,1)S(1)}, bf16[112,512]{1,0:T(8,128)(2,1)S(1)}, u32[]{:S(2)}, u32[]{:S(2)}) collective-permute-start(bf16[112,512]{1,0:T(8,128)(2,1)S(1)} %collective-permute-done.15.refs_3_), channel_id=1, source_target_pairs={{0,6},{1,7},{2,0},{3,1},{4,2},{5,3},{6,4},{7,5},{8,14},{9,15},{10,... | collective-permute-start | bytes 344072 | tf_op jit(solution)/shard_map/ppermute | solution.py:55
  94.2 7.3 %collective-permute-start.17 = (bf16[112,512]{1,0:T(8,128)(2,1)S(1)}, bf16[112,512]{1,0:T(8,128)(2,1)S(1)}, u32[]{:S(2)}, u32[]{:S(2)}) collective-permute-start(bf16[112,512]{1,0:T(8,128)(2,1)S(1)} %collective-permute-done.15.refs_3_), channel_id=1, source_target_pairs={{0,4},{1,5},{2,6},{3,7},{4,0},{5,1},{6,2},{7,3},{8,12},{9,13},{10,... | collective-permute-start | bytes 344072 | tf_op jit(solution)/shard_map/ppermute | solution.py:55
  95.4 6.9 %collective-permute-start.16 = (bf16[112,512]{1,0:T(8,128)(2,1)S(1)}, bf16[112,512]{1,0:T(8,128)(2,1)S(1)}, u32[]{:S(2)}, u32[]{:S(2)}) collective-permute-start(bf16[112,512]{1,0:T(8,128)(2,1)S(1)} %collective-permute-done.15.refs_3_), channel_id=1, source_target_pairs={{0,2},{1,3},{2,4},{3,5},{4,6},{5,7},{6,0},{7,1},{8,10},{9,11},{10,... | collective-permute-start | bytes 344072 | tf_op jit(solution)/shard_map/ppermute | solution.py:55

commit v2 on v1

--- a/solution.py
+++ b/solution.py
@@ -18,6 +18,7 @@
 NY, NZ, NC, NX, NH = 4, 4, 2, 4, 2
 VMEM = pl.BlockSpec(memory_space=pltpu.VMEM)
 ANY = pl.BlockSpec(memory_space=pl.ANY)
+HBM = pl.BlockSpec(memory_space=pltpu.HBM)
 
 
 def dp_perm(step):
@@ -76,30 +77,46 @@
     )
 
 
-def project_body(feat, basis, own, s1, s2, s3):
+def project_body(feat, basis, own, s1, s2, s3, fbuf, bbuf, sems):
     _, _, _, x, _ = place()
     rows = own.shape[0]
-    for k, out in ((2, s2), (1, s1), (3, s3), (0, own)):
+    order = ((2, s2), (1, s1), (3, s3), (0, own))
+    copies = [pltpu.make_async_copy(basis, bbuf, sems.at[NX])]
+    for k, _ in order:
         start = pl.multiple_of(lax.rem(x + k, NX) * rows, rows)
-        part = jnp.dot(feat[pl.ds(start, rows), :], basis[...], preferred_element_type=f32)
+        copies.append(pltpu.make_async_copy(feat.at[pl.ds(start, rows), :], fbuf.at[k], sems.at[k]))
+    for copy in copies:
+        copy.start()
+    copies[0].wait()
+    for (k, out), copy in zip(order, copies[1:]):
+        copy.wait()
+        part = jnp.dot(fbuf[k], bbuf[...], preferred_element_type=f32)
         out[...] = part.astype(out.dtype)
 
 
-def turn_body(grads, basis, keep, send, basis_t, tmp):
+def turn_body(grads, basis, _, keep, send, basis_t, gbuf, bbuf, tmp, sems):
     y, z, c, x, _ = place()
     rows = keep.shape[2]
     wide = NZ * NC * rows
-    toks = grads.shape[0] // NX
+    toks = gbuf.shape[1] // NX
+    copies = []
     for ry in range(NY):
         col = pl.multiple_of(lax.rem(y + ry, NY) * wide, 128)
+        copies.append(pltpu.make_async_copy(grads.at[:, pl.ds(col, wide)], gbuf.at[ry], sems.at[ry]))
+    copies.append(pltpu.make_async_copy(basis, bbuf, sems.at[NY]))
+    for copy in copies:
+        copy.start()
+    for ry in range(NY):
+        copies[ry].wait()
         for k in range(NX):
             tok = pl.multiple_of(lax.rem(x + NX - k, NX) * toks, toks)
-            tmp[:, k * toks : (k + 1) * toks] = grads[pl.ds(tok, toks), pl.ds(col, wide)].T
+            tmp[:, k * toks : (k + 1) * toks] = gbuf[ry, pl.ds(tok, toks), :].T
         for rz in range(NZ):
             for cc, out in ((0, keep), (1, send)):
                 start = pl.multiple_of(((z ^ rz) * NC + (c ^ cc)) * rows, 16)
                 out[ry, rz] = tmp[pl.ds(start, rows), :]
-    basis_t[...] = basis[...].T
+    copies[NY].wait()
+    basis_t[...] = bbuf[...].T
 
 
 def sum_x_body(own, r1, r2, r3, total, sent):
@@ -112,22 +129,29 @@
     out[...] = (own[...] + other[...].astype(f32)).astype(bf16)
 
 
-def low_body(keep, other, p0, p1, p2, p3, q, own, s1, s2, s3):
-    pieces = (p0, p1, p2, p3)
-    toks = p0.shape[0]
-    proj = jnp.concatenate([p[...] for p in pieces], axis=0)
-    for ry, out in ((2, s2), (1, s1), (3, s3), (0, own)):
-        a = keep[ry].reshape(out.shape[0], NX * toks)
-        b = other[ry].reshape(out.shape[0], NX * toks)
-        part = jnp.dot(a, proj, preferred_element_type=f32)
-        part += jnp.dot(b, q[...], preferred_element_type=f32)
-        out[...] = part.astype(out.dtype)
-
-
-def sum_y_body(own, r1, r2, r3, total, s1, s2, s3):
-    rows = total.shape[0]
-    for rz, out in ((3, s3), (2, s2), (1, s1), (0, total)):
-        part = slice(rz * rows, (rz + 1) * rows)
+def low_own_body(keep, p0, p1, p2, p3, acc):
+    rows, toks = keep.shape[1] * keep.shape[2], keep.shape[3]
+    proj = jnp.concatenate([p[...] for p in (p0, p1, p2, p3)], axis=0)
+    for ry in range(NY):
+        a = keep[ry].reshape(rows, toks)
+        acc[ry] = jnp.dot(a, proj, preferred_element_type=f32)
+
+
+def low_body(group, acc, other, q, *refs):
+    outs = refs[-NY:]
+    rows, toks = other.shape[1] * other.shape[2], other.shape[3]
+    half = rows // 2
+    for ry in (2, 1, 3, 0):
+        part = other[ry, group * NZ // 2 : (group + 1) * NZ // 2].reshape(half, toks)
+        t = acc[ry, group * half : (group + 1) * half, :]
+        t = t + jnp.dot(part, q[...], preferred_element_type=f32)
+        outs[ry][...] = t.astype(outs[ry].dtype)
+
+
+def sum_y_body(own, r1, r2, r3, first, second):
+    rows = first.shape[0]
+    for i, out in enumerate((first, second)):
+        part = slice(i * rows, (i + 1) * rows)
         t = own[part, :] + r1[part, :].astype(f32) + r2[part, :].astype(f32) + r3[part, :].astype(f32)
         out[...] = t.astype(out.dtype)
 
@@ -182,33 +206,56 @@
     rows = first_moment.shape[1]
     toks = tokens // NX
 
+    features = pltpu.with_memory_space_constraint(features, pltpu.HBM)
+    basis_in = pltpu.with_memory_space_constraint(proj_basis, pltpu.HBM)
     own, s1, s2, s3 = call(
-        project_body, [((toks, rank), f32)] + [((toks, rank), bf16)] * 3, 2
-    )(features, proj_basis)
+        project_body,
+        [((toks, rank), f32)] + [((toks, rank), bf16)] * 3,
+        2,
+        scratch=[
+            pltpu.VMEM((NX, toks, width), bf16),
+            pltpu.VMEM((width, rank), bf16),
+            pltpu.SemaphoreType.DMA((NX + 1,)),
+        ],
+        in_specs=[HBM] * 2,
+        limit=16,
+    )(features, basis_in)
     r2, r1, r3 = to_x(s2, 2), to_x(s1, 1), to_x(s3, 3)
 
     block = (NY, NZ, rows, tokens)
+    wide = NZ * NC * rows
     keep, send, basis_t = call(
         turn_body,
         [(block, bf16), (block, bf16), ((rank, width), bf16)],
-        2,
-        scratch=[pltpu.VMEM((NZ * NC * rows, tokens), bf16)],
-    )(out_grads, proj_basis)
+        3,
+        scratch=[
+            pltpu.VMEM((NY, tokens, wide), bf16),
+            pltpu.VMEM((width, rank), bf16),
+            pltpu.VMEM((wide, tokens), bf16),
+            pltpu.SemaphoreType.DMA((NY + 1,)),
+        ],
+        in_specs=[HBM, HBM, ANY],
+    )(out_grads, proj_basis, own)
+    total, sent = call(sum_x_body, [((toks, rank), f32), ((toks, rank), bf16)], 4)(own, r1, r2, r3)
+    send, sent = lax.optimization_barrier((send, sent))
     other = to_core(send)
-
-    total, sent = call(sum_x_body, [((toks, rank), f32), ((toks, rank), bf16)], 4)(own, r1, r2, r3)
     p0 = call(sum_h_body, [((toks, rank), bf16)], 2)(total, to_h(sent))[0]
     p2, p1, p3 = to_x(p0, 2), to_x(p0, 1), to_x(p0, 3)
     q = to_core(jnp.concatenate([p0, p1, p2, p3], axis=0))
 
-    own, s1, s2, s3 = call(
-        low_body, [((NZ * rows, rank), f32)] + [((NZ * rows, rank), bf16)] * 3, 7
-    )(keep, other, p0, p1, p2, p3, q)
-    r2, r1, r3 = to_y(s2, 2), to_y(s1, 1), to_y(s3, 3)
-    own, s1, s2, s3 = call(
-        sum_y_body, [((rows, rank), f32)] + [((rows, rank), bf16)] * 3, 4
-    )(own, r1, r2, r3)
-    r3, r2, r1 = to_z(s3, 3), to_z(s2, 2), to_z(s1, 1)
+    acc = call(low_own_body, [((NY, NZ * rows, rank), f32)], 5)(keep, p0, p1, p2, p3)[0]
+    half = (NZ // 2 * rows, rank)
+    sums = [(half, f32)] + [(half, bf16)] * 3
+    own_b, b1, b2, b3 = call(functools.partial(low_body, 1), sums, 3)(acc, other, q)
+    b2, b1, b3 = to_y(b2, 2), to_y(b1, 1), to_y(b3, 3)
+    own_a, a1, a2, a3 = call(
+        functools.partial(low_body, 0), sums, 4, in_specs=[VMEM] * 3 + [ANY]
+    )(acc, other, q, b1)
+    a2, a1, a3 = to_y(a2, 2), to_y(a1, 1), to_y(a3, 3)
+    s2, s3 = call(sum_y_body, [((rows, rank), bf16)] * 2, 4)(own_b, b1, b2, b3)
+    r3, r2 = to_z(s3, 3), to_z(s2, 2)
+    own, s1 = call(sum_y_body, [((rows, rank), f32), ((rows, rank), bf16)], 4)(own_a, a1, a2, a3)
+    r1 = to_z(s1, 1)
     first_new, second_new, d0 = call(
         adam_body, [((1, rows, rank), f32)] * 2 + [((rows, rank), bf16)], 6
     )(own, r1, r2, r3, first_moment, second_moment)

time: 105 us -> 91.8 us (0.87)
  waiting for transfers between devices: 54 us -> 26.7 us
  starting transfers between devices: 36.3 us -> 48.9 us
  Pallas kernels: 9.22 us -> 12.2 us
  local copies, waits for them, and re-layouts: 3.27 us -> 2.06 us
    ppermute x3 -> x6, waiting for transfers between devices: 19 us -> 8.16 us  [to_y(): return lax.ppermute(a, 'dp', dp_perm(lambda y, z, c: (y + k, z, c)))]
    ppermute x3 -> x6, starting transfers between devices: 5.88 us -> 14.6 us  [to_y(): return lax.ppermute(a, 'dp', dp_perm(lambda y, z, c: (y + k, z, c)))]
    ppermute x12, waiting for transfers between devices: 14.6 us -> 6.07 us  [to_x(): return lax.ppermute(a, 'shard', shard_perm(lambda x, h: (x + k, h)))]
    ppermute x12, starting transfers between devices: 14.7 us -> 20.8 us  [to_x(): return lax.ppermute(a, 'shard', shard_perm(lambda x, h: (x + k, h)))]
    ppermute x3, waiting for transfers between devices: 9.7 us -> 4.77 us  [to_z(): return lax.ppermute(a, 'dp', dp_perm(lambda y, z, c: (y, z ^ k, c)))]
    pallas_call x4 -> x7, Pallas kernels: 4.44 us -> 7.46 us  [the longest x1 2.69 us: per_device(): call(project_body, [((toks, rank), f32)] + [((toks, rank), bf16)] * 3, 2,...]
    ppermute x3, starting transfers between devices: 3.7 us -> 1.42 us  [to_z(): return lax.ppermute(a, 'dp', dp_perm(lambda y, z, c: (y, z ^ k, c)))]
    ppermute x2, waiting for transfers between devices: 8.72 us -> 6.93 us  [to_h(): return lax.ppermute(a, 'shard', shard_perm(lambda x, h: (x, 1 - h)))]
  transfers between devices with their start and end apart: 22 -> 25, of which waited for: 15 -> 12; matrix products, arithmetic and copies ran while one was open for 0% -> 0% of each run, Pallas kernels for 3% -> 7%
where the time goes in v2:
time: 91.8 us; the launch traced here: 90.9 us
  starting transfers between devices  48.9 us (53%)
  waiting for transfers between devices  26.7 us (29%)
  Pallas kernels  12.2 us (13%)
  local copies, waits for them, and re-layouts  2.06 us (2%)
  between operations  0.98 us (1%)
    ppermute x12, starting transfers between devices, to_x(): return lax.ppermute(a, 'shard', shard_perm(lambda x, h: (x + k, h)))  20.8 us
    ppermute x6, starting transfers between devices, to_y(): return lax.ppermute(a, 'dp', dp_perm(lambda y, z, c: (y + k, z, c)))  14.6 us
    ppermute x2, starting transfers between devices, to_h(): return lax.ppermute(a, 'shard', shard_perm(lambda x, h: (x, 1 - h)))  11.9 us
    ppermute x6, waiting for transfers between devices, to_y(): return lax.ppermute(a, 'dp', dp_perm(lambda y, z, c: (y + k, z, c)))  8.16 us
    ppermute x2, waiting for transfers between devices, to_h(): return lax.ppermute(a, 'shard', shard_perm(lambda x, h: (x, 1 - h)))  6.93 us
    ppermute x12, waiting for transfers between devices, to_x(): return lax.ppermute(a, 'shard', shard_perm(lambda x, h: (x + k, h)))  6.07 us
    ppermute x3, waiting for transfers between devices, to_z(): return lax.ppermute(a, 'dp', dp_perm(lambda y, z, c: (y, z ^ k, c)))  4.77 us
    pallas_call x3, Pallas kernels, update_part(): call(functools.partial(update_body, moves, aliased), [((NX * NH, rows, co...  3.82 us
  transfers between devices with their start and end apart: 25, of which 12 were waited for; matrix products, arithmetic and copies ran while one was open for 0% of the time, Pallas kernels for 7%

profile of v2, /device:TPU:32, one launch (start us, length us, event | category | flops | bytes accessed | tf_op | source)
XLA Modules:
  0.0 90.9 jit_solution(5426026008408262630)
XLA Ops:
  0.6 2.7 %shard_map.76 = (f32[128,512]{1,0:T(8,128)S(1)}, bf16[128,512]{1,0:T(8,128)(2,1)S(1)}, bf16[128,512]{1,0:T(8,128)(2,1)S(1)}, bf16[128,512]{1,0:T(8,128)(2,1)S(1)}) custom-call(bf16[512,1024]{1,0:T(8,128)(2,1)} %feat.1, bf16[1024,512]{1,0:T(8,128)(2,1)} %basis.3), custom_call_target="tpu_custom_call" | custom-call | tf_op jit(solution)/shard_map/pallas_call | solution.py:211
  3.3 1.6 %collective-permute-start = (bf16[128,512]{1,0:T(8,128)(2,1)S(1)}, bf16[128,512]{1,0:T(8,128)(2,1)S(1)}, u32[]{:S(2)}, u32[]{:S(2)}) collective-permute-start(bf16[128,512]{1,0:T(8,128)(2,1)S(1)} %get-tuple-element.31), channel_id=1, source_target_pairs={{0,2},{1,3},{2,4},{3,5},{4,6},{5,7},{6,0},{7,1},{8,10},{9,11},{10,... | collective-permute-start | bytes 393224 | tf_op jit(solution)/shard_map/ppermute | solution.py:56
  4.9 2.7 %collective-permute-start.1 = (bf16[128,512]{1,0:T(8,128)(2,1)S(1)}, bf16[128,512]{1,0:T(8,128)(2,1)S(1)}, u32[]{:S(2)}, u32[]{:S(2)}) collective-permute-start(bf16[128,512]{1,0:T(8,128)(2,1)S(1)} %get-tuple-element.32), channel_id=1, source_target_pairs={{0,4},{1,5},{2,6},{3,7},{4,0},{5,1},{6,2},{7,3},{8,12},{9,13},{10,... | collective-permute-start | bytes 393224 | tf_op jit(solution)/shard_map/ppermute | solution.py:56
  7.6 1.4 %collective-permute-start.2 = (bf16[128,512]{1,0:T(8,128)(2,1)S(1)}, bf16[128,512]{1,0:T(8,128)(2,1)S(1)}, u32[]{:S(2)}, u32[]{:S(2)}) collective-permute-start(bf16[128,512]{1,0:T(8,128)(2,1)S(1)} %get-tuple-element.33), channel_id=1, source_target_pairs={{0,6},{1,7},{2,0},{3,1},{4,2},{5,3},{6,4},{7,5},{8,14},{9,15},{10,... | collective-permute-start | bytes 393224 | tf_op jit(solution)/shard_map/ppermute | solution.py:56
  9.1 2.0 %copy-done.1 = bf16[512,3584]{1,0:T(8,128)(2,1)S(1)} copy-done((bf16[512,3584]{1,0:T(8,128)(2,1)S(1)}, bf16[512,3584]{1,0:T(8,128)(2,1)}, u32[]{:S(2)}) %copy-start.1) | copy-done | bytes 3670040
  11.1 2.2 %shard_map.77 = (bf16[4,4,112,512]{3,2,1,0:T(8,128)(2,1)S(1)}, bf16[4,4,112,512]{3,2,1,0:T(8,128)(2,1)S(1)}, bf16[512,1024]{1,0:T(8,128)(2,1)S(1)}) custom-call(bf16[512,3584]{1,0:T(8,128)(2,1)S(1)} %copy-done.1, bf16[1024,512]{1,0:T(8,128)(2,1)S(1)} %copy-done, f32[128,512]{1,0:T(8,128)S(1)} %get-tuple-element.29._.own), custom_call_target="tpu_custom_call" | custom-call | tf_op jit(solution)/shard_map/pallas_call | solution.py:227
  13.8 6.4 %collective-permute-start.3 = (bf16[128,512]{1,0:T(8,128)(2,1)S(1)}, bf16[128,512]{1,0:T(8,128)(2,1)S(1)}, u32[]{:S(2)}, u32[]{:S(2)}) collective-permute-start(bf16[128,512]{1,0:T(8,128)(2,1)S(1)} %get-tuple-element.37), channel_id=1, source_target_pairs={{0,1},{1,0},{2,3},{3,2},{4,5},{5,4},{6,7},{7,6},{8,9},{9,8},{10,11... | collective-permute-start | bytes 393224 | tf_op jit(solution)/shard_map/ppermute | solution.py:60
  20.2 6.9 %collective-permute-done.3.other = bf16[128,512]{1,0:T(8,128)(2,1)S(1)} collective-permute-done((bf16[128,512]{1,0:T(8,128)(2,1)S(1)}, bf16[128,512]{1,0:T(8,128)(2,1)S(1)}, u32[]{:S(2)}, u32[]{:S(2)}) %collective-permute-start.3) | collective-permute-done | bytes 131104 | tf_op jit(solution)/shard_map/ppermute | solution.py:60
  27.2 1.4 %collective-permute-start.4 = (bf16[128,512]{1,0:T(8,128)(2,1)S(1)}, bf16[128,512]{1,0:T(8,128)(2,1)S(1)}, u32[]{:S(2)}, u32[]{:S(2)}) collective-permute-start(bf16[128,512]{1,0:T(8,128)(2,1)S(1)} %shard_map.79.p0), channel_id=1, source_target_pairs={{0,2},{1,3},{2,4},{3,5},{4,6},{5,7},{6,0},{7,1},{8,10},{9,11},{10,... | collective-permute-start | bytes 393224 | tf_op jit(solution)/shard_map/ppermute | solution.py:56
  28.6 2.4 %collective-permute-start.5 = (bf16[128,512]{1,0:T(8,128)(2,1)S(1)}, bf16[128,512]{1,0:T(8,128)(2,1)S(1)}, u32[]{:S(2)}, u32[]{:S(2)}) collective-permute-start(bf16[128,512]{1,0:T(8,128)(2,1)S(1)} %shard_map.79.p0), channel_id=1, source_target_pairs={{0,4},{1,5},{2,6},{3,7},{4,0},{5,1},{6,2},{7,3},{8,12},{9,13},{10,... | collective-permute-start | bytes 393224 | tf_op jit(solution)/shard_map/ppermute | solution.py:56
  31.0 1.6 %collective-permute-start.6 = (bf16[128,512]{1,0:T(8,128)(2,1)S(1)}, bf16[128,512]{1,0:T(8,128)(2,1)S(1)}, u32[]{:S(2)}, u32[]{:S(2)}) collective-permute-start(bf16[128,512]{1,0:T(8,128)(2,1)S(1)} %shard_map.79.p0), channel_id=1, source_target_pairs={{0,6},{1,7},{2,0},{3,1},{4,2},{5,3},{6,4},{7,5},{8,14},{9,15},{10,... | collective-permute-start | bytes 393224 | tf_op jit(solution)/shard_map/ppermute | solution.py:56
  32.5 1.8 %collective-permute-done.4.p1 = bf16[128,512]{1,0:T(8,128)(2,1)S(1)} collective-permute-done((bf16[128,512]{1,0:T(8,128)(2,1)S(1)}, bf16[128,512]{1,0:T(8,128)(2,1)S(1)}, u32[]{:S(2)}, u32[]{:S(2)}) %collective-permute-start.4) | collective-permute-done | bytes 131104 | tf_op jit(solution)/shard_map/ppermute | solution.py:56
  34.3 2.6 %collective-permute-done.5.p2 = bf16[128,512]{1,0:T(8,128)(2,1)S(1)} collective-permute-done((bf16[128,512]{1,0:T(8,128)(2,1)S(1)}, bf16[128,512]{1,0:T(8,128)(2,1)S(1)}, u32[]{:S(2)}, u32[]{:S(2)}) %collective-permute-start.5) | collective-permute-done | bytes 131104 | tf_op jit(solution)/shard_map/ppermute | solution.py:56
  39.7 1.7 %collective-permute-start.9 = (bf16[224,512]{1,0:T(8,128)(2,1)S(1)}, bf16[224,512]{1,0:T(8,128)(2,1)S(1)}, u32[]{:S(2)}, u32[]{:S(2)}) collective-permute-start(bf16[224,512]{1,0:T(8,128)(2,1)S(1)} %get-tuple-element.39), channel_id=1, source_target_pairs={{0,64},{8,72},{16,80},{24,88},{32,96},{40,104},{48,112},{56,120},{... | collective-permute-start | bytes 688136 | tf_op jit(solution)/shard_map/ppermute | solution.py:48
  41.4 2.9 %collective-permute-start.14 = (bf16[224,512]{1,0:T(8,128)(2,1)S(1)}, bf16[224,512]{1,0:T(8,128)(2,1)S(1)}, u32[]{:S(2)}, u32[]{:S(2)}) collective-permute-start(bf16[224,512]{1,0:T(8,128)(2,1)S(1)} %get-tuple-element.47), channel_id=1, source_target_pairs={{0,128},{8,136},{16,144},{24,152},{32,160},{40,168},{48,176},{56,1... | collective-permute-start | bytes 688136 | tf_op jit(solution)/shard_map/ppermute | solution.py:48
  44.3 1.3 %collective-permute-start.15 = (bf16[224,512]{1,0:T(8,128)(2,1)S(1)}, bf16[224,512]{1,0:T(8,128)(2,1)S(1)}, u32[]{:S(2)}, u32[]{:S(2)}) collective-permute-start(bf16[224,512]{1,0:T(8,128)(2,1)S(1)} %get-tuple-element.48), channel_id=1, source_target_pairs={{0,192},{8,200},{16,208},{24,216},{32,224},{40,232},{48,240},{56,2... | collective-permute-start | bytes 688136 | tf_op jit(solution)/shard_map/ppermute | solution.py:48
  45.6 3.1 %collective-permute-done.9.refs_0_.r1 = bf16[224,512]{1,0:T(8,128)(2,1)S(1)} collective-permute-done((bf16[224,512]{1,0:T(8,128)(2,1)S(1)}, bf16[224,512]{1,0:T(8,128)(2,1)S(1)}, u32[]{:S(2)}, u32[]{:S(2)}) %collective-permute-start.9) | collective-permute-done | bytes 229408 | tf_op jit(solution)/shard_map/ppermute | solution.py:48
  49.4 1.2 %collective-permute-start.10 = (bf16[224,512]{1,0:T(8,128)(2,1)S(1)}, bf16[224,512]{1,0:T(8,128)(2,1)S(1)}, u32[]{:S(2)}, u32[]{:S(2)}) collective-permute-start(bf16[224,512]{1,0:T(8,128)(2,1)S(1)} %get-tuple-element.41), channel_id=1, source_target_pairs={{0,64},{8,72},{16,80},{24,88},{32,96},{40,104},{48,112},{56,120},{... | collective-permute-start | bytes 688136 | tf_op jit(solution)/shard_map/ppermute | solution.py:48
  50.6 5.0 %collective-permute-start.11 = (bf16[224,512]{1,0:T(8,128)(2,1)S(1)}, bf16[224,512]{1,0:T(8,128)(2,1)S(1)}, u32[]{:S(2)}, u32[]{:S(2)}) collective-permute-start(bf16[224,512]{1,0:T(8,128)(2,1)S(1)} %get-tuple-element.42), channel_id=1, source_target_pairs={{0,128},{8,136},{16,144},{24,152},{32,160},{40,168},{48,176},{56,1... | collective-permute-start | bytes 688136 | tf_op jit(solution)/shard_map/ppermute | solution.py:48
  55.6 2.5 %collective-permute-start.12 = (bf16[224,512]{1,0:T(8,128)(2,1)S(1)}, bf16[224,512]{1,0:T(8,128)(2,1)S(1)}, u32[]{:S(2)}, u32[]{:S(2)}) collective-permute-start(bf16[224,512]{1,0:T(8,128)(2,1)S(1)} %get-tuple-element.43), channel_id=1, source_target_pairs={{0,192},{8,200},{16,208},{24,216},{32,224},{40,232},{48,240},{56,2... | collective-permute-start | bytes 688136 | tf_op jit(solution)/shard_map/ppermute | solution.py:48
  58.3 1.2 %collective-permute-start.17 = (bf16[112,512]{1,0:T(8,128)(2,1)S(1)}, bf16[112,512]{1,0:T(8,128)(2,1)S(1)}, u32[]{:S(2)}, u32[]{:S(2)}) collective-permute-start(bf16[112,512]{1,0:T(8,128)(2,1)S(1)} %get-tuple-element.50), channel_id=1, source_target_pairs={{0,48},{8,56},{16,32},{24,40},{32,16},{40,24},{48,0},{56,8},{64,11... | collective-permute-start | bytes 344072 | tf_op jit(solution)/shard_map/ppermute | solution.py:52
  59.6 2.4 %collective-permute-done.10.r1 = bf16[224,512]{1,0:T(8,128)(2,1)S(1)} collective-permute-done((bf16[224,512]{1,0:T(8,128)(2,1)S(1)}, bf16[224,512]{1,0:T(8,128)(2,1)S(1)}, u32[]{:S(2)}, u32[]{:S(2)}) %collective-permute-start.10) | collective-permute-done | bytes 229408 | tf_op jit(solution)/shard_map/ppermute | solution.py:48
  62.0 2.6 %collective-permute-done.11.r2 = bf16[224,512]{1,0:T(8,128)(2,1)S(1)} collective-permute-done((bf16[224,512]{1,0:T(8,128)(2,1)S(1)}, bf16[224,512]{1,0:T(8,128)(2,1)S(1)}, u32[]{:S(2)}, u32[]{:S(2)}) %collective-permute-start.11) | collective-permute-done | bytes 229408 | tf_op jit(solution)/shard_map/ppermute | solution.py:48
  64.9 4.7 %collective-permute-done.13.r1 = bf16[112,512]{1,0:T(8,128)(2,1)S(1)} collective-permute-done((bf16[112,512]{1,0:T(8,128)(2,1)S(1)}, bf16[112,512]{1,0:T(8,128)(2,1)S(1)}, u32[]{:S(2)}, u32[]{:S(2)}) %collective-permute-start.13) | collective-permute-done | bytes 114720 | tf_op jit(solution)/shard_map/ppermute | solution.py:52
  70.5 5.5 %collective-permute-start.18 = (bf16[112,512]{1,0:T(8,128)(2,1)S(1)}, bf16[112,512]{1,0:T(8,128)(2,1)S(1)}, u32[]{:S(2)}, u32[]{:S(2)}) collective-permute-start(bf16[112,512]{1,0:T(8,128)(2,1)S(1)} %get-tuple-element.51.refs_0_), channel_id=1, source_target_pairs={{0,1},{1,0},{2,3},{3,2},{4,5},{5,4},{6,7},{7,6},{8,9},{9,8},{10,11... | collective-permute-start | bytes 344072 | tf_op jit(solution)/shard_map/ppermute | solution.py:60
  76.0 1.7 %collective-permute-start.22 = (bf16[112,512]{1,0:T(8,128)(2,1)S(1)}, bf16[112,512]{1,0:T(8,128)(2,1)S(1)}, u32[]{:S(2)}, u32[]{:S(2)}) collective-permute-start(bf16[112,512]{1,0:T(8,128)(2,1)S(1)} %get-tuple-element.51.refs_0_), channel_id=1, source_target_pairs={{0,2},{1,3},{2,4},{3,5},{4,6},{5,7},{6,0},{7,1},{8,10},{9,11},{10,... | collective-permute-start | bytes 344072 | tf_op jit(solution)/shard_map/ppermute | solution.py:56
  77.7 2.5 %collective-permute-start.23 = (bf16[112,512]{1,0:T(8,128)(2,1)S(1)}, bf16[112,512]{1,0:T(8,128)(2,1)S(1)}, u32[]{:S(2)}, u32[]{:S(2)}) collective-permute-start(bf16[112,512]{1,0:T(8,128)(2,1)S(1)} %get-tuple-element.51.refs_0_), channel_id=1, source_target_pairs={{0,4},{1,5},{2,6},{3,7},{4,0},{5,1},{6,2},{7,3},{8,12},{9,13},{10,... | collective-permute-start | bytes 344072 | tf_op jit(solution)/shard_map/ppermute | solution.py:56
  80.2 1.1 %collective-permute-start.24 = (bf16[112,512]{1,0:T(8,128)(2,1)S(1)}, bf16[112,512]{1,0:T(8,128)(2,1)S(1)}, u32[]{:S(2)}, u32[]{:S(2)}) collective-permute-start(bf16[112,512]{1,0:T(8,128)(2,1)S(1)} %get-tuple-element.51.refs_0_), channel_id=1, source_target_pairs={{0,6},{1,7},{2,0},{3,1},{4,2},{5,3},{6,4},{7,5},{8,14},{9,15},{10,... | collective-permute-start | bytes 344072 | tf_op jit(solution)/shard_map/ppermute | solution.py:56
  82.2 2.3 %collective-permute-start.20 = (bf16[112,512]{1,0:T(8,128)(2,1)S(1)}, bf16[112,512]{1,0:T(8,128)(2,1)S(1)}, u32[]{:S(2)}, u32[]{:S(2)}) collective-permute-start(bf16[112,512]{1,0:T(8,128)(2,1)S(1)} %collective-permute-done.18.refs_3_), channel_id=1, source_target_pairs={{0,4},{1,5},{2,6},{3,7},{4,0},{5,1},{6,2},{7,3},{8,12},{9,13},{10,... | collective-permute-start | bytes 344072 | tf_op jit(solution)/shard_map/ppermute | solution.py:56
  84.5 1.1 %collective-permute-start.21 = (bf16[112,512]{1,0:T(8,128)(2,1)S(1)}, bf16[112,512]{1,0:T(8,128)(2,1)S(1)}, u32[]{:S(2)}, u32[]{:S(2)}) collective-permute-start(bf16[112,512]{1,0:T(8,128)(2,1)S(1)} %collective-permute-done.18.refs_3_), channel_id=1, source_target_pairs={{0,6},{1,7},{2,0},{3,1},{4,2},{5,3},{6,4},{7,5},{8,14},{9,15},{10,... | collective-permute-start | bytes 344072 | tf_op jit(solution)/shard_map/ppermute | solution.py:56
  86.7 1.5 %shard_map.87.refs_4_ = bf16[8,112,1024]{2,1,0:T(8,128)(2,1)} custom-call(bf16[112,512]{1,0:T(8,128)(2,1)S(1)} %collective-permute-done.22.refs_0_, bf16[112,512]{1,0:T(8,128)(2,1)S(1)} %collective-permute-done.23.refs_1_, bf16[112,512]{1,0:T(8,128)(2,1)S(1)} %collective-permute-done.24.refs_2_, ...), custom_call_target="tpu_custom_call", output_to_operand_aliasing={{}: (5, {})} | custom-call | tf_op jit(solution)/shard_map/pallas_call | solution.py:192
  89.4 1.3 %shard_map.88 = bf16[8,112,1024]{2,1,0:T(8,128)(2,1)} custom-call(bf16[112,512]{1,0:T(8,128)(2,1)S(1)} %collective-permute-done.19.refs_0_, bf16[112,512]{1,0:T(8,128)(2,1)S(1)} %collective-permute-done.20.refs_1_, bf16[112,512]{1,0:T(8,128)(2,1)S(1)} %collective-permute-done.21.refs_2_, ...), custom_call_target="tpu_custom_call", output_to_operand_aliasing={{}: (4, {})} | custom-call | tf_op jit(solution)/shard_map/pallas_call | solution.py:192
  (40 shorter events, 8.4 us)
Async XLA Ops:
  0.6 8.4 %copy-start = (bf16[1024,512]{1,0:T(8,128)(2,1)S(1)}, bf16[1024,512]{1,0:T(8,128)(2,1)}, u32[]{:S(2)}) copy-start(bf16[1024,512]{1,0:T(8,128)(2,1)} %basis.3) | copy-start | bytes 3145732
  3.3 10.0 %collective-permute-start = (bf16[128,512]{1,0:T(8,128)(2,1)S(1)}, bf16[128,512]{1,0:T(8,128)(2,1)S(1)}, u32[]{:S(2)}, u32[]{:S(2)}) collective-permute-start(bf16[128,512]{1,0:T(8,128)(2,1)S(1)} %get-tuple-element.31), channel_id=1, source_target_pairs={{0,2},{1,3},{2,4},{3,5},{4,6},{5,7},{6,0},{7,1},{8,10},{9,11},{10,... | collective-permute-start | bytes 393224 | tf_op jit(solution)/shard_map/ppermute | solution.py:56
  4.9 8.7 %collective-permute-start.1 = (bf16[128,512]{1,0:T(8,128)(2,1)S(1)}, bf16[128,512]{1,0:T(8,128)(2,1)S(1)}, u32[]{:S(2)}, u32[]{:S(2)}) collective-permute-start(bf16[128,512]{1,0:T(8,128)(2,1)S(1)} %get-tuple-element.32), channel_id=1, source_target_pairs={{0,4},{1,5},{2,6},{3,7},{4,0},{5,1},{6,2},{7,3},{8,12},{9,13},{10,... | collective-permute-start | bytes 393224 | tf_op jit(solution)/shard_map/ppermute | solution.py:56
  7.6 6.0 %collective-permute-start.2 = (bf16[128,512]{1,0:T(8,128)(2,1)S(1)}, bf16[128,512]{1,0:T(8,128)(2,1)S(1)}, u32[]{:S(2)}, u32[]{:S(2)}) collective-permute-start(bf16[128,512]{1,0:T(8,128)(2,1)S(1)} %get-tuple-element.33), channel_id=1, source_target_pairs={{0,6},{1,7},{2,0},{3,1},{4,2},{5,3},{6,4},{7,5},{8,14},{9,15},{10,... | collective-permute-start | bytes 393224 | tf_op jit(solution)/shard_map/ppermute | solution.py:56
  9.1 2.0 %copy-start.1 = (bf16[512,3584]{1,0:T(8,128)(2,1)S(1)}, bf16[512,3584]{1,0:T(8,128)(2,1)}, u32[]{:S(2)}) copy-start(bf16[512,3584]{1,0:T(8,128)(2,1)} %grads.1) | copy-start | bytes 11010052
  13.7 25.3 %collective-permute-start.7 = (bf16[4,4,112,512]{3,2,1,0:T(8,128)(2,1)S(1)}, bf16[4,4,112,512]{3,2,1,0:T(8,128)(2,1)S(1)}, u32[]{:S(2)}, u32[]{:S(2)}) collective-permute-start(bf16[4,4,112,512]{3,2,1,0:T(8,128)(2,1)S(1)} %get-tuple-element.38), channel_id=1, source_target_pairs={{0,8},{8,0},{16,24},{24,16},{32,40},{40,32},{48,56},{56,48},{64,72... | collective-permute-start | bytes 5505032 | tf_op jit(solution)/shard_map/ppermute | solution.py:44
  13.8 13.3 %collective-permute-start.3 = (bf16[128,512]{1,0:T(8,128)(2,1)S(1)}, bf16[128,512]{1,0:T(8,128)(2,1)S(1)}, u32[]{:S(2)}, u32[]{:S(2)}) collective-permute-start(bf16[128,512]{1,0:T(8,128)(2,1)S(1)} %get-tuple-element.37), channel_id=1, source_target_pairs={{0,1},{1,0},{2,3},{3,2},{4,5},{5,4},{6,7},{7,6},{8,9},{9,8},{10,11... | collective-permute-start | bytes 393224 | tf_op jit(solution)/shard_map/ppermute | solution.py:60
  27.2 7.2 %collective-permute-start.4 = (bf16[128,512]{1,0:T(8,128)(2,1)S(1)}, bf16[128,512]{1,0:T(8,128)(2,1)S(1)}, u32[]{:S(2)}, u32[]{:S(2)}) collective-permute-start(bf16[128,512]{1,0:T(8,128)(2,1)S(1)} %shard_map.79.p0), channel_id=1, source_target_pairs={{0,2},{1,3},{2,4},{3,5},{4,6},{5,7},{6,0},{7,1},{8,10},{9,11},{10,... | collective-permute-start | bytes 393224 | tf_op jit(solution)/shard_map/ppermute | solution.py:56
  28.6 8.4 %collective-permute-start.5 = (bf16[128,512]{1,0:T(8,128)(2,1)S(1)}, bf16[128,512]{1,0:T(8,128)(2,1)S(1)}, u32[]{:S(2)}, u32[]{:S(2)}) collective-permute-start(bf16[128,512]{1,0:T(8,128)(2,1)S(1)} %shard_map.79.p0), channel_id=1, source_target_pairs={{0,4},{1,5},{2,6},{3,7},{4,0},{5,1},{6,2},{7,3},{8,12},{9,13},{10,... | collective-permute-start | bytes 393224 | tf_op jit(solution)/shard_map/ppermute | solution.py:56
  31.0 6.0 %collective-permute-start.6 = (bf16[128,512]{1,0:T(8,128)(2,1)S(1)}, bf16[128,512]{1,0:T(8,128)(2,1)S(1)}, u32[]{:S(2)}, u32[]{:S(2)}) collective-permute-start(bf16[128,512]{1,0:T(8,128)(2,1)S(1)} %shard_map.79.p0), channel_id=1, source_target_pairs={{0,6},{1,7},{2,0},{3,1},{4,2},{5,3},{6,4},{7,5},{8,14},{9,15},{10,... | collective-permute-start | bytes 393224 | tf_op jit(solution)/shard_map/ppermute | solution.py:56
  37.1 2.0 %collective-permute-start.8 = (bf16[512,512]{1,0:T(8,128)(2,1)S(1)}, bf16[512,512]{1,0:T(8,128)(2,1)S(1)}, u32[]{:S(2)}, u32[]{:S(2)}) collective-permute-start(bf16[512,512]{1,0:T(8,128)(2,1)S(1)} %pad_maximum_fusion), channel_id=1, source_target_pairs={{0,8},{8,0},{16,24},{24,16},{32,40},{40,32},{48,56},{56,48},{64,72... | collective-permute-start | bytes 1572872 | tf_op jit(solution)/shard_map/ppermute | solution.py:44
  39.7 9.0 %collective-permute-start.9 = (bf16[224,512]{1,0:T(8,128)(2,1)S(1)}, bf16[224,512]{1,0:T(8,128)(2,1)S(1)}, u32[]{:S(2)}, u32[]{:S(2)}) collective-permute-start(bf16[224,512]{1,0:T(8,128)(2,1)S(1)} %get-tuple-element.39), channel_id=1, source_target_pairs={{0,64},{8,72},{16,80},{24,88},{32,96},{40,104},{48,112},{56,120},{... | collective-permute-start | bytes 688136 | tf_op jit(solution)/shard_map/ppermute | solution.py:48
  41.4 16.8 %collective-permute-start.14 = (bf16[224,512]{1,0:T(8,128)(2,1)S(1)}, bf16[224,512]{1,0:T(8,128)(2,1)S(1)}, u32[]{:S(2)}, u32[]{:S(2)}) collective-permute-start(bf16[224,512]{1,0:T(8,128)(2,1)S(1)} %get-tuple-element.47), channel_id=1, source_target_pairs={{0,128},{8,136},{16,144},{24,152},{32,160},{40,168},{48,176},{56,1... | collective-permute-start | bytes 688136 | tf_op jit(solution)/shard_map/ppermute | solution.py:48
  44.3 13.9 %collective-permute-start.15 = (bf16[224,512]{1,0:T(8,128)(2,1)S(1)}, bf16[224,512]{1,0:T(8,128)(2,1)S(1)}, u32[]{:S(2)}, u32[]{:S(2)}) collective-permute-start(bf16[224,512]{1,0:T(8,128)(2,1)S(1)} %get-tuple-element.48), channel_id=1, source_target_pairs={{0,192},{8,200},{16,208},{24,216},{32,224},{40,232},{48,240},{56,2... | collective-permute-start | bytes 688136 | tf_op jit(solution)/shard_map/ppermute | solution.py:48
  49.3 20.3 %copy-start.2 = (f32[1,112,512]{2,1,0:T(8,128)S(1)}, f32[1,112,512]{2,1,0:T(8,128)}, u32[]{:S(2)}) copy-start(f32[1,112,512]{2,1,0:T(8,128)} %first.1) | copy-start | bytes 688132
  49.4 20.3 %copy-start.3 = (f32[1,112,512]{2,1,0:T(8,128)S(1)}, f32[1,112,512]{2,1,0:T(8,128)}, u32[]{:S(2)}) copy-start(f32[1,112,512]{2,1,0:T(8,128)} %second.1) | copy-start | bytes 688132
  49.4 12.6 %collective-permute-start.10 = (bf16[224,512]{1,0:T(8,128)(2,1)S(1)}, bf16[224,512]{1,0:T(8,128)(2,1)S(1)}, u32[]{:S(2)}, u32[]{:S(2)}) collective-permute-start(bf16[224,512]{1,0:T(8,128)(2,1)S(1)} %get-tuple-element.41), channel_id=1, source_target_pairs={{0,64},{8,72},{16,80},{24,88},{32,96},{40,104},{48,112},{56,120},{... | collective-permute-start | bytes 688136 | tf_op jit(solution)/shard_map/ppermute | solution.py:48
  50.6 14.1 %collective-permute-start.11 = (bf16[224,512]{1,0:T(8,128)(2,1)S(1)}, bf16[224,512]{1,0:T(8,128)(2,1)S(1)}, u32[]{:S(2)}, u32[]{:S(2)}) collective-permute-start(bf16[224,512]{1,0:T(8,128)(2,1)S(1)} %get-tuple-element.42), channel_id=1, source_target_pairs={{0,128},{8,136},{16,144},{24,152},{32,160},{40,168},{48,176},{56,1... | collective-permute-start | bytes 688136 | tf_op jit(solution)/shard_map/ppermute | solution.py:48
  55.6 9.0 %collective-permute-start.12 = (bf16[224,512]{1,0:T(8,128)(2,1)S(1)}, bf16[224,512]{1,0:T(8,128)(2,1)S(1)}, u32[]{:S(2)}, u32[]{:S(2)}) collective-permute-start(bf16[224,512]{1,0:T(8,128)(2,1)S(1)} %get-tuple-element.43), channel_id=1, source_target_pairs={{0,192},{8,200},{16,208},{24,216},{32,224},{40,232},{48,240},{56,2... | collective-permute-start | bytes 688136 | tf_op jit(solution)/shard_map/ppermute | solution.py:48
  58.2 6.6 %collective-permute-start.16 = (bf16[112,512]{1,0:T(8,128)(2,1)S(1)}, bf16[112,512]{1,0:T(8,128)(2,1)S(1)}, u32[]{:S(2)}, u32[]{:S(2)}) collective-permute-start(bf16[112,512]{1,0:T(8,128)(2,1)S(1)} %get-tuple-element.49), channel_id=1, source_target_pairs={{0,32},{8,40},{16,48},{24,56},{32,0},{40,8},{48,16},{56,24},{64,96... | collective-permute-start | bytes 344072 | tf_op jit(solution)/shard_map/ppermute | solution.py:52
  58.3 6.5 %collective-permute-start.17 = (bf16[112,512]{1,0:T(8,128)(2,1)S(1)}, bf16[112,512]{1,0:T(8,128)(2,1)S(1)}, u32[]{:S(2)}, u32[]{:S(2)}) collective-permute-start(bf16[112,512]{1,0:T(8,128)(2,1)S(1)} %get-tuple-element.50), channel_id=1, source_target_pairs={{0,48},{8,56},{16,32},{24,40},{32,16},{40,24},{48,0},{56,8},{64,11... | collective-permute-start | bytes 344072 | tf_op jit(solution)/shard_map/ppermute | solution.py:52
  64.7 4.9 %collective-permute-start.13 = (bf16[112,512]{1,0:T(8,128)(2,1)S(1)}, bf16[112,512]{1,0:T(8,128)(2,1)S(1)}, u32[]{:S(2)}, u32[]{:S(2)}) collective-permute-start(bf16[112,512]{1,0:T(8,128)(2,1)S(1)} %get-tuple-element.45), channel_id=1, source_target_pairs={{0,16},{8,24},{16,0},{24,8},{32,48},{40,56},{48,32},{56,40},{64,80... | collective-permute-start | bytes 344072 | tf_op jit(solution)/shard_map/ppermute | solution.py:52
  70.5 10.8 %collective-permute-start.18 = (bf16[112,512]{1,0:T(8,128)(2,1)S(1)}, bf16[112,512]{1,0:T(8,128)(2,1)S(1)}, u32[]{:S(2)}, u32[]{:S(2)}) collective-permute-start(bf16[112,512]{1,0:T(8,128)(2,1)S(1)} %get-tuple-element.51.refs_0_), channel_id=1, source_target_pairs={{0,1},{1,0},{2,3},{3,2},{4,5},{5,4},{6,7},{7,6},{8,9},{9,8},{10,11... | collective-permute-start | bytes 344072 | tf_op jit(solution)/shard_map/ppermute | solution.py:60
  76.0 8.5 %collective-permute-start.22 = (bf16[112,512]{1,0:T(8,128)(2,1)S(1)}, bf16[112,512]{1,0:T(8,128)(2,1)S(1)}, u32[]{:S(2)}, u32[]{:S(2)}) collective-permute-start(bf16[112,512]{1,0:T(8,128)(2,1)S(1)} %get-tuple-element.51.refs_0_), channel_id=1, source_target_pairs={{0,2},{1,3},{2,4},{3,5},{4,6},{5,7},{6,0},{7,1},{8,10},{9,11},{10,... | collective-permute-start | bytes 344072 | tf_op jit(solution)/shard_map/ppermute | solution.py:56
  77.7 8.9 %collective-permute-start.23 = (bf16[112,512]{1,0:T(8,128)(2,1)S(1)}, bf16[112,512]{1,0:T(8,128)(2,1)S(1)}, u32[]{:S(2)}, u32[]{:S(2)}) collective-permute-start(bf16[112,512]{1,0:T(8,128)(2,1)S(1)} %get-tuple-element.51.refs_0_), channel_id=1, source_target_pairs={{0,4},{1,5},{2,6},{3,7},{4,0},{5,1},{6,2},{7,3},{8,12},{9,13},{10,... | collective-permute-start | bytes 344072 | tf_op jit(solution)/shard_map/ppermute | solution.py:56
  80.2 6.5 %collective-permute-start.24 = (bf16[112,512]{1,0:T(8,128)(2,1)S(1)}, bf16[112,512]{1,0:T(8,128)(2,1)S(1)}, u32[]{:S(2)}, u32[]{:S(2)}) collective-permute-start(bf16[112,512]{1,0:T(8,128)(2,1)S(1)} %get-tuple-element.51.refs_0_), channel_id=1, source_target_pairs={{0,6},{1,7},{2,0},{3,1},{4,2},{5,3},{6,4},{7,5},{8,14},{9,15},{10,... | collective-permute-start | bytes 344072 | tf_op jit(solution)/shard_map/ppermute | solution.py:56
  81.3 6.9 %collective-permute-start.19 = (bf16[112,512]{1,0:T(8,128)(2,1)S(1)}, bf16[112,512]{1,0:T(8,128)(2,1)S(1)}, u32[]{:S(2)}, u32[]{:S(2)}) collective-permute-start(bf16[112,512]{1,0:T(8,128)(2,1)S(1)} %collective-permute-done.18.refs_3_), channel_id=1, source_target_pairs={{0,2},{1,3},{2,4},{3,5},{4,6},{5,7},{6,0},{7,1},{8,10},{9,11},{10,... | collective-permute-start | bytes 344072 | tf_op jit(solution)/shard_map/ppermute | solution.py:56
  82.2 6.3 %collective-permute-start.20 = (bf16[112,512]{1,0:T(8,128)(2,1)S(1)}, bf16[112,512]{1,0:T(8,128)(2,1)S(1)}, u32[]{:S(2)}, u32[]{:S(2)}) collective-permute-start(bf16[112,512]{1,0:T(8,128)(2,1)S(1)} %collective-permute-done.18.refs_3_), channel_id=1, source_target_pairs={{0,4},{1,5},{2,6},{3,7},{4,0},{5,1},{6,2},{7,3},{8,12},{9,13},{10,... | collective-permute-start | bytes 344072 | tf_op jit(solution)/shard_map/ppermute | solution.py:56
  84.5 4.9 %collective-permute-start.21 = (bf16[112,512]{1,0:T(8,128)(2,1)S(1)}, bf16[112,512]{1,0:T(8,128)(2,1)S(1)}, u32[]{:S(2)}, u32[]{:S(2)}) collective-permute-start(bf16[112,512]{1,0:T(8,128)(2,1)S(1)} %collective-permute-done.18.refs_3_), channel_id=1, source_target_pairs={{0,6},{1,7},{2,0},{3,1},{4,2},{5,3},{6,4},{7,5},{8,14},{9,15},{10,... | collective-permute-start | bytes 344072 | tf_op jit(solution)/shard_map/ppermute | solution.py:56

commit v3 on v2

--- a/solution.py
+++ b/solution.py
@@ -16,6 +16,7 @@
 
 bf16, f32 = jnp.bfloat16, jnp.float32
 NY, NZ, NC, NX, NH = 4, 4, 2, 4, 2
+SPLIT = 2
 VMEM = pl.BlockSpec(memory_space=pltpu.VMEM)
 ANY = pl.BlockSpec(memory_space=pl.ANY)
 HBM = pl.BlockSpec(memory_space=pltpu.HBM)
@@ -81,20 +82,27 @@
     _, _, _, x, _ = place()
     rows = own.shape[0]
     order = ((2, s2), (1, s1), (3, s3), (0, own))
-    copies = [pltpu.make_async_copy(basis, bbuf, sems.at[NX])]
+    part = basis.shape[0] // NX
+    copies = []
+    for i in range(NX):
+        cut = pl.ds(i * part, part)
+        copies.append(pltpu.make_async_copy(basis.at[cut, :], bbuf.at[cut, :], sems.at[NX + i]))
     for k, _ in order:
         start = pl.multiple_of(lax.rem(x + k, NX) * rows, rows)
         copies.append(pltpu.make_async_copy(feat.at[pl.ds(start, rows), :], fbuf.at[k], sems.at[k]))
     for copy in copies:
         copy.start()
-    copies[0].wait()
-    for (k, out), copy in zip(order, copies[1:]):
+    for copy in copies[:NX]:
         copy.wait()
-        part = jnp.dot(fbuf[k], bbuf[...], preferred_element_type=f32)
-        out[...] = part.astype(out.dtype)
-
-
-def turn_body(grads, basis, _, keep, send, basis_t, gbuf, bbuf, tmp, sems):
+    for (k, out), copy in zip(order, copies[NX:]):
+        copy.wait()
+        t = jnp.dot(fbuf[k], bbuf[...], preferred_element_type=f32)
+        out[...] = t.astype(out.dtype)
+
+
+def turn_body(grads, basis, _, keep, *refs):
+    sends = refs[:SPLIT]
+    basis_t, gbuf, bbuf, tmp, sems = refs[SPLIT:]
     y, z, c, x, _ = place()
     rows = keep.shape[2]
     wide = NZ * NC * rows
@@ -112,9 +120,10 @@
             tok = pl.multiple_of(lax.rem(x + NX - k, NX) * toks, toks)
             tmp[:, k * toks : (k + 1) * toks] = gbuf[ry, pl.ds(tok, toks), :].T
         for rz in range(NZ):
-            for cc, out in ((0, keep), (1, send)):
-                start = pl.multiple_of(((z ^ rz) * NC + (c ^ cc)) * rows, 16)
-                out[ry, rz] = tmp[pl.ds(start, rows), :]
+            base = (z ^ rz) * NC
+            keep[ry, rz] = tmp[pl.ds(pl.multiple_of((base + c) * rows, 16), rows), :]
+            other = tmp[pl.ds(pl.multiple_of((base + 1 - c) * rows, 16), rows), :]
+            sends[ry * SPLIT // NY][ry % (NY // SPLIT), rz] = other
     copies[NY].wait()
     basis_t[...] = bbuf[...].T
 
@@ -137,33 +146,51 @@
         acc[ry] = jnp.dot(a, proj, preferred_element_type=f32)
 
 
-def low_body(group, acc, other, q, *refs):
-    outs = refs[-NY:]
-    rows, toks = other.shape[1] * other.shape[2], other.shape[3]
-    half = rows // 2
+def low_far_body(rz, acc, q, *refs):
+    other, outs = refs[:SPLIT], refs[SPLIT:]
+    rows = other[0].shape[2]
     for ry in (2, 1, 3, 0):
-        part = other[ry, group * NZ // 2 : (group + 1) * NZ // 2].reshape(half, toks)
-        t = acc[ry, group * half : (group + 1) * half, :]
-        t = t + jnp.dot(part, q[...], preferred_element_type=f32)
+        t = acc[ry, rz * rows : (rz + 1) * rows, :]
+        t = t + jnp.dot(other[ry * SPLIT // NY][ry % (NY // SPLIT), rz], q[...], preferred_element_type=f32)
         outs[ry][...] = t.astype(outs[ry].dtype)
 
 
-def sum_y_body(own, r1, r2, r3, first, second):
-    rows = first.shape[0]
-    for i, out in enumerate((first, second)):
-        part = slice(i * rows, (i + 1) * rows)
-        t = own[part, :] + r1[part, :].astype(f32) + r2[part, :].astype(f32) + r3[part, :].astype(f32)
-        out[...] = t.astype(out.dtype)
-
-
-def adam_body(own, r1, r2, r3, first, second, first_new, second_new, direction):
-    g = own[...] + r1[...].astype(f32) + r2[...].astype(f32) + r3[...].astype(f32)
+def low_near_body(acc, q, *refs):
+    other, (own, send) = refs[:SPLIT], refs[SPLIT:]
+    rows = other[0].shape[2]
+    for ry in range(NY):
+        for rz, out in ((1, send), (0, own)):
+            t = acc[ry, rz * rows : (rz + 1) * rows, :]
+            t = t + jnp.dot(other[ry * SPLIT // NY][ry % (NY // SPLIT), rz], q[...], preferred_element_type=f32)
+            out[ry * rows : (ry + 1) * rows, :] = t.astype(out.dtype)
+
+
+def sum_far_body(own, r1, r2, r3, out):
+    t = own[...] + r1[...].astype(f32) + r2[...].astype(f32) + r3[...].astype(f32)
+    out[...] = t.astype(out.dtype)
+
+
+def sum_near_body(own, near, total, s1, s2, s3):
+    rows = total.shape[0]
+    for ry, out in ((2, s2), (1, s1), (3, s3), (0, total)):
+        part = slice(ry * rows, (ry + 1) * rows)
+        out[...] = (own[part, :] + near[part, :].astype(f32)).astype(out.dtype)
+
+
+def direction_body(z3, z2, own, y1, y2, y3, first, second, grad, direction):
+    g = own[...] + y1[...].astype(f32) + y2[...].astype(f32) + y3[...].astype(f32)
+    g = g + z2[...].astype(f32) + z3[...].astype(f32)
+    grad[...] = g
     m = beta_first * first[0] + (1.0 - beta_first) * g
     v = beta_second * second[0] + (1.0 - beta_second) * g * g
-    first_new[0] = m
-    second_new[0] = v
     d = m / correct_first / (jnp.sqrt(v / correct_second) + epsilon)
     direction[...] = d.astype(bf16)
+
+
+def moments_body(grad, first, second, first_new, second_new):
+    g = grad[...]
+    first_new[0] = beta_first * first[0] + (1.0 - beta_first) * g
+    second_new[0] = beta_second * second[0] + (1.0 - beta_second) * g * g
 
 
 def update_body(moves, aliased, *refs):
@@ -207,6 +234,7 @@
     toks = tokens // NX
 
     features = pltpu.with_memory_space_constraint(features, pltpu.HBM)
+    grads_in = pltpu.with_memory_space_constraint(out_grads, pltpu.HBM)
     basis_in = pltpu.with_memory_space_constraint(proj_basis, pltpu.HBM)
     own, s1, s2, s3 = call(
         project_body,
@@ -215,7 +243,7 @@
         scratch=[
             pltpu.VMEM((NX, toks, width), bf16),
             pltpu.VMEM((width, rank), bf16),
-            pltpu.SemaphoreType.DMA((NX + 1,)),
+            pltpu.SemaphoreType.DMA((2 * NX,)),
         ],
         in_specs=[HBM] * 2,
         limit=16,
@@ -224,9 +252,9 @@
 
     block = (NY, NZ, rows, tokens)
     wide = NZ * NC * rows
-    keep, send, basis_t = call(
+    keep, *sends, basis_t = call(
         turn_body,
-        [(block, bf16), (block, bf16), ((rank, width), bf16)],
+        [(block, bf16)] + [((NY // SPLIT, NZ, rows, tokens), bf16)] * SPLIT + [((rank, width), bf16)],
         3,
         scratch=[
             pltpu.VMEM((NY, tokens, wide), bf16),
@@ -235,35 +263,48 @@
             pltpu.SemaphoreType.DMA((NY + 1,)),
         ],
         in_specs=[HBM, HBM, ANY],
-    )(out_grads, proj_basis, own)
+    )(grads_in, basis_in, own)
     total, sent = call(sum_x_body, [((toks, rank), f32), ((toks, rank), bf16)], 4)(own, r1, r2, r3)
-    send, sent = lax.optimization_barrier((send, sent))
-    other = to_core(send)
-    p0 = call(sum_h_body, [((toks, rank), bf16)], 2)(total, to_h(sent))[0]
+    half_sum = to_h(sent)
+    other = [to_core(a) for a in sends]
+    p0 = call(sum_h_body, [((toks, rank), bf16)], 2)(total, half_sum)[0]
     p2, p1, p3 = to_x(p0, 2), to_x(p0, 1), to_x(p0, 3)
     q = to_core(jnp.concatenate([p0, p1, p2, p3], axis=0))
 
     acc = call(low_own_body, [((NY, NZ * rows, rank), f32)], 5)(keep, p0, p1, p2, p3)[0]
-    half = (NZ // 2 * rows, rank)
-    sums = [(half, f32)] + [(half, bf16)] * 3
-    own_b, b1, b2, b3 = call(functools.partial(low_body, 1), sums, 3)(acc, other, q)
-    b2, b1, b3 = to_y(b2, 2), to_y(b1, 1), to_y(b3, 3)
-    own_a, a1, a2, a3 = call(
-        functools.partial(low_body, 0), sums, 4, in_specs=[VMEM] * 3 + [ANY]
-    )(acc, other, q, b1)
-    a2, a1, a3 = to_y(a2, 2), to_y(a1, 1), to_y(a3, 3)
-    s2, s3 = call(sum_y_body, [((rows, rank), bf16)] * 2, 4)(own_b, b1, b2, b3)
-    r3, r2 = to_z(s3, 3), to_z(s2, 2)
-    own, s1 = call(sum_y_body, [((rows, rank), f32), ((rows, rank), bf16)], 4)(own_a, a1, a2, a3)
-    r1 = to_z(s1, 1)
-    first_new, second_new, d0 = call(
-        adam_body, [((1, rows, rank), f32)] * 2 + [((rows, rank), bf16)], 6
-    )(own, r1, r2, r3, first_moment, second_moment)
-
+    one, four = (rows, rank), (NY * rows, rank)
+
+    def low_far(rz):
+        return call(functools.partial(low_far_body, rz), [(one, f32)] + [(one, bf16)] * 3, 2 + SPLIT)(
+            acc, q, *other
+        )
+
+    def over_y(s1, s2, s3):
+        r2, r1, r3 = to_y(s2, 2), to_y(s1, 1), to_y(s3, 3)
+        return r1, r2, r3
+
+    own3, *far3 = low_far(3)
+    far3 = over_y(*far3)
+    near, send = call(low_near_body, [(four, f32), (four, bf16)], 2 + SPLIT)(acc, q, *other)
+    send = to_z(send, 1)
+    own2, *far2 = low_far(2)
+    far2 = over_y(*far2)
+    z3 = to_z(call(sum_far_body, [(one, bf16)], 4)(own3, *far3)[0], 3)
+    z2 = to_z(call(sum_far_body, [(one, bf16)], 4)(own2, *far2)[0], 2)
+    own, y1, y2, y3 = call(sum_near_body, [(one, f32)] + [(one, bf16)] * 3, 2)(near, send)
+    y1, y2, y3 = over_y(y1, y2, y3)
+    grad, d0 = call(direction_body, [(one, f32), (one, bf16)], 8)(
+        z3, z2, own, y1, y2, y3, first_moment, second_moment
+    )
     e0 = to_h(d0)
     d2, d1, d3 = to_x(d0, 2), to_x(d0, 1), to_x(d0, 3)
+    update = update_part([(0, 0)], [d0], basis_t, None)
+    e0, update = lax.optimization_barrier((e0, update))
     e2, e1, e3 = to_x(e0, 2), to_x(e0, 1), to_x(e0, 3)
-    update = update_part([(0, 0)], [d0], basis_t, None)
+    grad, _ = lax.optimization_barrier((grad, e0))
+    first_new, second_new = call(moments_body, [((1, rows, rank), f32)] * 2, 3)(
+        grad, first_moment, second_moment
+    )
     update = update_part([(1, 0), (2, 0), (3, 0), (0, 1)], [d1, d2, d3, e0], basis_t, update)
     update = update_part([(1, 1), (2, 1), (3, 1)], [e1, e2, e3], basis_t, update)
     return (update, first_new, second_new)

time: 91.8 us -> 86.2 us (0.939)
  waiting for transfers between devices: 26.7 us -> 22.5 us
  local copies, waits for them, and re-layouts: 2.06 us -> 0.01 us
  Pallas kernels: 12.2 us -> 13.5 us
    ppermute x3, waiting for transfers between devices: 4.77 us -> 0.01 us  [to_z(): return lax.ppermute(a, 'dp', dp_perm(lambda y, z, c: (y, z ^ k, c)))]
    ppermute x3, starting transfers between devices: 1.42 us -> 5.73 us  [to_z(): return lax.ppermute(a, 'dp', dp_perm(lambda y, z, c: (y, z ^ k, c)))]
    ppermute x6 -> x9, starting transfers between devices: 14.6 us -> 12.2 us  [to_y(): return lax.ppermute(a, 'dp', dp_perm(lambda y, z, c: (y + k, z, c)))]
    unnamed x8 -> x4, local copies, waits for them, and re-layouts: 2.06 us -> 0.01 us
    ppermute x12, starting transfers between devices: 20.8 us -> 19.2 us  [to_x(): return lax.ppermute(a, 'shard', shard_perm(lambda x, h: (x + k, h)))]
    pallas_call x7 -> x10, Pallas kernels: 4.56 us -> 5.92 us  [the longest x1 2.98 us: per_device(): call(turn_body, [(block, bf16)] + [((NY // SPLIT, NZ, rows, tokens), bf16...]
    ppermute x2, waiting for transfers between devices: 6.93 us -> 5.61 us  [to_h(): return lax.ppermute(a, 'shard', shard_perm(lambda x, h: (x, 1 - h)))]
    ppermute x12, waiting for transfers between devices: 6.07 us -> 7.13 us  [to_x(): return lax.ppermute(a, 'shard', shard_perm(lambda x, h: (x + k, h)))]
  transfers between devices with their start and end apart: 25 -> 29, of which waited for: 12 -> 15; matrix products, arithmetic and copies ran while one was open for 0% -> 0% of each run, Pallas kernels for 7% -> 10%
where the time goes in v3:
time: 86.2 us; the launch traced here: 86 us
  starting transfers between devices  49 us (57%)
  waiting for transfers between devices  22.5 us (26%)
  Pallas kernels  13.5 us (16%)
  between operations  0.95 us (1%)
    ppermute x12, starting transfers between devices, to_x(): return lax.ppermute(a, 'shard', shard_perm(lambda x, h: (x + k, h)))  19.2 us
    ppermute x9, starting transfers between devices, to_y(): return lax.ppermute(a, 'dp', dp_perm(lambda y, z, c: (y + k, z, c)))  12.2 us
    ppermute x2, starting transfers between devices, to_h(): return lax.ppermute(a, 'shard', shard_perm(lambda x, h: (x, 1 - h)))  11.1 us
    ppermute x9, waiting for transfers between devices, to_y(): return lax.ppermute(a, 'dp', dp_perm(lambda y, z, c: (y + k, z, c)))  8.95 us
    ppermute x12, waiting for transfers between devices, to_x(): return lax.ppermute(a, 'shard', shard_perm(lambda x, h: (x + k, h)))  7.13 us
    ppermute x3, starting transfers between devices, to_z(): return lax.ppermute(a, 'dp', dp_perm(lambda y, z, c: (y, z ^ k, c)))  5.73 us
    ppermute x2, waiting for transfers between devices, to_h(): return lax.ppermute(a, 'shard', shard_perm(lambda x, h: (x, 1 - h)))  5.61 us
    pallas_call x3, Pallas kernels, update_part(): call(functools.partial(update_body, moves, aliased), [((NX * NH, rows, co...  3.83 us
  transfers between devices with their start and end apart: 29, of which 15 were waited for; matrix products, arithmetic and copies ran while one was open for 0% of the time, Pallas kernels for 10%

profile of v3, /device:TPU:32, one launch (start us, length us, event | category | flops | bytes accessed | tf_op | source)
XLA Modules:
  0.0 86.0 jit_solution(14306629240164610011)
XLA Ops:
  0.6 2.6 %shard_map.76 = (f32[128,512]{1,0:T(8,128)S(1)}, bf16[128,512]{1,0:T(8,128)(2,1)S(1)}, bf16[128,512]{1,0:T(8,128)(2,1)S(1)}, bf16[128,512]{1,0:T(8,128)(2,1)S(1)}) custom-call(bf16[512,1024]{1,0:T(8,128)(2,1)} %feat.1, bf16[1024,512]{1,0:T(8,128)(2,1)} %basis.3), custom_call_target="tpu_custom_call" | custom-call | tf_op jit(solution)/shard_map/pallas_call | solution.py:239
  3.2 1.6 %collective-permute-start = (bf16[128,512]{1,0:T(8,128)(2,1)S(1)}, bf16[128,512]{1,0:T(8,128)(2,1)S(1)}, u32[]{:S(2)}, u32[]{:S(2)}) collective-permute-start(bf16[128,512]{1,0:T(8,128)(2,1)S(1)} %get-tuple-element.36), channel_id=1, source_target_pairs={{0,2},{1,3},{2,4},{3,5},{4,6},{5,7},{6,0},{7,1},{8,10},{9,11},{10,... | collective-permute-start | bytes 393224 | tf_op jit(solution)/shard_map/ppermute | solution.py:57
  4.8 2.7 %collective-permute-start.1 = (bf16[128,512]{1,0:T(8,128)(2,1)S(1)}, bf16[128,512]{1,0:T(8,128)(2,1)S(1)}, u32[]{:S(2)}, u32[]{:S(2)}) collective-permute-start(bf16[128,512]{1,0:T(8,128)(2,1)S(1)} %get-tuple-element.37), channel_id=1, source_target_pairs={{0,4},{1,5},{2,6},{3,7},{4,0},{5,1},{6,2},{7,3},{8,12},{9,13},{10,... | collective-permute-start | bytes 393224 | tf_op jit(solution)/shard_map/ppermute | solution.py:57
  7.5 1.4 %collective-permute-start.2 = (bf16[128,512]{1,0:T(8,128)(2,1)S(1)}, bf16[128,512]{1,0:T(8,128)(2,1)S(1)}, u32[]{:S(2)}, u32[]{:S(2)}) collective-permute-start(bf16[128,512]{1,0:T(8,128)(2,1)S(1)} %get-tuple-element.38), channel_id=1, source_target_pairs={{0,6},{1,7},{2,0},{3,1},{4,2},{5,3},{6,4},{7,5},{8,14},{9,15},{10,... | collective-permute-start | bytes 393224 | tf_op jit(solution)/shard_map/ppermute | solution.py:57
  9.0 3.0 %shard_map.77 = (bf16[4,4,112,512]{3,2,1,0:T(8,128)(2,1)S(1)}, bf16[2,4,112,512]{3,2,1,0:T(8,128)(2,1)S(1)}, bf16[2,4,112,512]{3,2,1,0:T(8,128)(2,1)S(1)}, bf16[512,1024]{1,0:T(8,128)(2,1)S(1)}) custom-call(bf16[512,3584]{1,0:T(8,128)(2,1)} %grads.1, bf16[1024,512]{1,0:T(8,128)(2,1)} %basis.3, f32[128,512]{1,0:T(8,128)S(1)} %get-tuple-element.34._.own), custom_call_target="tpu_custom_call" | custom-call | tf_op jit(solution)/shard_map/pallas_call | solution.py:255
  13.6 6.4 %collective-permute-start.3 = (bf16[128,512]{1,0:T(8,128)(2,1)S(1)}, bf16[128,512]{1,0:T(8,128)(2,1)S(1)}, u32[]{:S(2)}, u32[]{:S(2)}) collective-permute-start(bf16[128,512]{1,0:T(8,128)(2,1)S(1)} %get-tuple-element.40), channel_id=1, source_target_pairs={{0,1},{1,0},{2,3},{3,2},{4,5},{5,4},{6,7},{7,6},{8,9},{9,8},{10,11... | collective-permute-start | bytes 393224 | tf_op jit(solution)/shard_map/ppermute | solution.py:61
  20.0 5.6 %collective-permute-done.3.other = bf16[128,512]{1,0:T(8,128)(2,1)S(1)} collective-permute-done((bf16[128,512]{1,0:T(8,128)(2,1)S(1)}, bf16[128,512]{1,0:T(8,128)(2,1)S(1)}, u32[]{:S(2)}, u32[]{:S(2)}) %collective-permute-start.3) | collective-permute-done | bytes 131104 | tf_op jit(solution)/shard_map/ppermute | solution.py:61
  25.6 1.4 %collective-permute-start.4 = (bf16[128,512]{1,0:T(8,128)(2,1)S(1)}, bf16[128,512]{1,0:T(8,128)(2,1)S(1)}, u32[]{:S(2)}, u32[]{:S(2)}) collective-permute-start(bf16[128,512]{1,0:T(8,128)(2,1)S(1)} %shard_map.79.p0), channel_id=1, source_target_pairs={{0,2},{1,3},{2,4},{3,5},{4,6},{5,7},{6,0},{7,1},{8,10},{9,11},{10,... | collective-permute-start | bytes 393224 | tf_op jit(solution)/shard_map/ppermute | solution.py:57
  27.1 2.5 %collective-permute-start.5 = (bf16[128,512]{1,0:T(8,128)(2,1)S(1)}, bf16[128,512]{1,0:T(8,128)(2,1)S(1)}, u32[]{:S(2)}, u32[]{:S(2)}) collective-permute-start(bf16[128,512]{1,0:T(8,128)(2,1)S(1)} %shard_map.79.p0), channel_id=1, source_target_pairs={{0,4},{1,5},{2,6},{3,7},{4,0},{5,1},{6,2},{7,3},{8,12},{9,13},{10,... | collective-permute-start | bytes 393224 | tf_op jit(solution)/shard_map/ppermute | solution.py:57
  30.2 1.7 %collective-permute-done.4.p1 = bf16[128,512]{1,0:T(8,128)(2,1)S(1)} collective-permute-done((bf16[128,512]{1,0:T(8,128)(2,1)S(1)}, bf16[128,512]{1,0:T(8,128)(2,1)S(1)}, u32[]{:S(2)}, u32[]{:S(2)}) %collective-permute-start.4) | collective-permute-done | bytes 131104 | tf_op jit(solution)/shard_map/ppermute | solution.py:57
  31.9 2.0 %collective-permute-done.5.p2 = bf16[128,512]{1,0:T(8,128)(2,1)S(1)} collective-permute-done((bf16[128,512]{1,0:T(8,128)(2,1)S(1)}, bf16[128,512]{1,0:T(8,128)(2,1)S(1)}, u32[]{:S(2)}, u32[]{:S(2)}) %collective-permute-start.5) | collective-permute-done | bytes 131104 | tf_op jit(solution)/shard_map/ppermute | solution.py:57
  34.7 1.1 %shard_map.80.acc = f32[4,448,512]{2,1,0:T(8,128)S(1)} custom-call(bf16[4,4,112,512]{3,2,1,0:T(8,128)(2,1)S(1)} %get-tuple-element.35.keep, bf16[128,512]{1,0:T(8,128)(2,1)S(1)} %shard_map.79.p0, bf16[128,512]{1,0:T(8,128)(2,1)S(1)} %collective-permute-done.4.p1, bf16[128,512]{1,0:T(8,128)(2,1)S(1)} %collective-permute-done.5.p2, ...), custom_call_target="tpu_custom_call" | custom-call | tf_op jit(solution)/shard_map/pallas_call | solution.py:274
  37.9 1.6 %collective-permute-start.10 = (bf16[112,512]{1,0:T(8,128)(2,1)S(1)}, bf16[112,512]{1,0:T(8,128)(2,1)S(1)}, u32[]{:S(2)}, u32[]{:S(2)}) collective-permute-start(bf16[112,512]{1,0:T(8,128)(2,1)S(1)} %get-tuple-element.44), channel_id=1, source_target_pairs={{0,64},{8,72},{16,80},{24,88},{32,96},{40,104},{48,112},{56,120},{... | collective-permute-start | bytes 344072 | tf_op jit(solution)/shard_map/ppermute | solution.py:49
  39.5 2.9 %collective-permute-start.11 = (bf16[112,512]{1,0:T(8,128)(2,1)S(1)}, bf16[112,512]{1,0:T(8,128)(2,1)S(1)}, u32[]{:S(2)}, u32[]{:S(2)}) collective-permute-start(bf16[112,512]{1,0:T(8,128)(2,1)S(1)} %get-tuple-element.45), channel_id=1, source_target_pairs={{0,128},{8,136},{16,144},{24,152},{32,160},{40,168},{48,176},{56,1... | collective-permute-start | bytes 344072 | tf_op jit(solution)/shard_map/ppermute | solution.py:49
  42.4 1.3 %collective-permute-start.12 = (bf16[112,512]{1,0:T(8,128)(2,1)S(1)}, bf16[112,512]{1,0:T(8,128)(2,1)S(1)}, u32[]{:S(2)}, u32[]{:S(2)}) collective-permute-start(bf16[112,512]{1,0:T(8,128)(2,1)S(1)} %get-tuple-element.46), channel_id=1, source_target_pairs={{0,192},{8,200},{16,208},{24,216},{32,224},{40,232},{48,240},{56,2... | collective-permute-start | bytes 344072 | tf_op jit(solution)/shard_map/ppermute | solution.py:49
  45.0 1.3 %collective-permute-start.15 = (bf16[112,512]{1,0:T(8,128)(2,1)S(1)}, bf16[112,512]{1,0:T(8,128)(2,1)S(1)}, u32[]{:S(2)}, u32[]{:S(2)}) collective-permute-start(bf16[112,512]{1,0:T(8,128)(2,1)S(1)} %get-tuple-element.49), channel_id=1, source_target_pairs={{0,128},{8,136},{16,144},{24,152},{32,160},{40,168},{48,176},{56,1... | collective-permute-start | bytes 344072 | tf_op jit(solution)/shard_map/ppermute | solution.py:49
  46.3 2.5 %collective-permute-done.11.r2 = bf16[112,512]{1,0:T(8,128)(2,1)S(1)} collective-permute-done((bf16[112,512]{1,0:T(8,128)(2,1)S(1)}, bf16[112,512]{1,0:T(8,128)(2,1)S(1)}, u32[]{:S(2)}, u32[]{:S(2)}) %collective-permute-start.11) | collective-permute-done | bytes 114720 | tf_op jit(solution)/shard_map/ppermute | solution.py:49
  48.9 2.2 %collective-permute-start.13 = (bf16[112,512]{1,0:T(8,128)(2,1)S(1)}, bf16[112,512]{1,0:T(8,128)(2,1)S(1)}, u32[]{:S(2)}, u32[]{:S(2)}) collective-permute-start(bf16[112,512]{1,0:T(8,128)(2,1)S(1)} %shard_map.82), channel_id=1, source_target_pairs={{0,48},{8,56},{16,32},{24,40},{32,16},{40,24},{48,0},{56,8},{64,11... | collective-permute-start | bytes 344072 | tf_op jit(solution)/shard_map/ppermute | solution.py:53
  51.4 1.6 %collective-permute-done.15.r2 = bf16[112,512]{1,0:T(8,128)(2,1)S(1)} collective-permute-done((bf16[112,512]{1,0:T(8,128)(2,1)S(1)}, bf16[112,512]{1,0:T(8,128)(2,1)S(1)}, u32[]{:S(2)}, u32[]{:S(2)}) %collective-permute-start.15) | collective-permute-done | bytes 114720 | tf_op jit(solution)/shard_map/ppermute | solution.py:49
  53.7 3.4 %collective-permute-start.17 = (bf16[112,512]{1,0:T(8,128)(2,1)S(1)}, bf16[112,512]{1,0:T(8,128)(2,1)S(1)}, u32[]{:S(2)}, u32[]{:S(2)}) collective-permute-start(bf16[112,512]{1,0:T(8,128)(2,1)S(1)} %shard_map.84), channel_id=1, source_target_pairs={{0,32},{8,40},{16,48},{24,56},{32,0},{40,8},{48,16},{56,24},{64,96... | collective-permute-start | bytes 344072 | tf_op jit(solution)/shard_map/ppermute | solution.py:53
  57.7 2.9 %collective-permute-start.20 = (bf16[112,512]{1,0:T(8,128)(2,1)S(1)}, bf16[112,512]{1,0:T(8,128)(2,1)S(1)}, u32[]{:S(2)}, u32[]{:S(2)}) collective-permute-start(bf16[112,512]{1,0:T(8,128)(2,1)S(1)} %get-tuple-element.55), channel_id=1, source_target_pairs={{0,128},{8,136},{16,144},{24,152},{32,160},{40,168},{48,176},{56,1... | collective-permute-start | bytes 344072 | tf_op jit(solution)/shard_map/ppermute | solution.py:49
  61.5 1.8 %collective-permute-done.19.y1 = bf16[112,512]{1,0:T(8,128)(2,1)S(1)} collective-permute-done((bf16[112,512]{1,0:T(8,128)(2,1)S(1)}, bf16[112,512]{1,0:T(8,128)(2,1)S(1)}, u32[]{:S(2)}, u32[]{:S(2)}) %collective-permute-start.19) | collective-permute-done | bytes 114720 | tf_op jit(solution)/shard_map/ppermute | solution.py:49
  63.3 1.4 %collective-permute-done.20.y2 = bf16[112,512]{1,0:T(8,128)(2,1)S(1)} collective-permute-done((bf16[112,512]{1,0:T(8,128)(2,1)S(1)}, bf16[112,512]{1,0:T(8,128)(2,1)S(1)}, u32[]{:S(2)}, u32[]{:S(2)}) %collective-permute-start.20) | collective-permute-done | bytes 114720 | tf_op jit(solution)/shard_map/ppermute | solution.py:49
  65.7 4.8 %collective-permute-start.22 = (bf16[112,512]{1,0:T(8,128)(2,1)S(1)}, bf16[112,512]{1,0:T(8,128)(2,1)S(1)}, u32[]{:S(2)}, u32[]{:S(2)}) collective-permute-start(bf16[112,512]{1,0:T(8,128)(2,1)S(1)} %get-tuple-element.57.refs_0_), channel_id=1, source_target_pairs={{0,1},{1,0},{2,3},{3,2},{4,5},{5,4},{6,7},{7,6},{8,9},{9,8},{10,11... | collective-permute-start | bytes 344072 | tf_op jit(solution)/shard_map/ppermute | solution.py:61
  70.5 1.1 %collective-permute-start.26 = (bf16[112,512]{1,0:T(8,128)(2,1)S(1)}, bf16[112,512]{1,0:T(8,128)(2,1)S(1)}, u32[]{:S(2)}, u32[]{:S(2)}) collective-permute-start(bf16[112,512]{1,0:T(8,128)(2,1)S(1)} %get-tuple-element.57.refs_0_), channel_id=1, source_target_pairs={{0,2},{1,3},{2,4},{3,5},{4,6},{5,7},{6,0},{7,1},{8,10},{9,11},{10,... | collective-permute-start | bytes 344072 | tf_op jit(solution)/shard_map/ppermute | solution.py:57
  71.6 3.0 %collective-permute-start.27 = (bf16[112,512]{1,0:T(8,128)(2,1)S(1)}, bf16[112,512]{1,0:T(8,128)(2,1)S(1)}, u32[]{:S(2)}, u32[]{:S(2)}) collective-permute-start(bf16[112,512]{1,0:T(8,128)(2,1)S(1)} %get-tuple-element.57.refs_0_), channel_id=1, source_target_pairs={{0,4},{1,5},{2,6},{3,7},{4,0},{5,1},{6,2},{7,3},{8,12},{9,13},{10,... | collective-permute-start | bytes 344072 | tf_op jit(solution)/shard_map/ppermute | solution.py:57
  74.8 1.0 %shard_map.88.refs_5_ = bf16[8,112,1024]{2,1,0:T(8,128)(2,1)} custom-call(bf16[112,512]{1,0:T(8,128)(2,1)S(1)} %get-tuple-element.57.refs_0_, bf16[512,1024]{1,0:T(8,128)(2,1)S(1)} %get-tuple-element.58.refs_1_.refs_4_.refs_3_), custom_call_target="tpu_custom_call" | custom-call | tf_op jit(solution)/shard_map/pallas_call | solution.py:219
  75.8 1.9 %collective-permute-start.23 = (bf16[112,512]{1,0:T(8,128)(2,1)S(1)}, bf16[112,512]{1,0:T(8,128)(2,1)S(1)}, u32[]{:S(2)}, u32[]{:S(2)}) collective-permute-start(bf16[112,512]{1,0:T(8,128)(2,1)S(1)} %collective-permute-done.22.refs_3_), channel_id=1, source_target_pairs={{0,2},{1,3},{2,4},{3,5},{4,6},{5,7},{6,0},{7,1},{8,10},{9,11},{10,... | collective-permute-start | bytes 344072 | tf_op jit(solution)/shard_map/ppermute | solution.py:57
  77.7 2.1 %collective-permute-start.24 = (bf16[112,512]{1,0:T(8,128)(2,1)S(1)}, bf16[112,512]{1,0:T(8,128)(2,1)S(1)}, u32[]{:S(2)}, u32[]{:S(2)}) collective-permute-start(bf16[112,512]{1,0:T(8,128)(2,1)S(1)} %collective-permute-done.22.refs_3_), channel_id=1, source_target_pairs={{0,4},{1,5},{2,6},{3,7},{4,0},{5,1},{6,2},{7,3},{8,12},{9,13},{10,... | collective-permute-start | bytes 344072 | tf_op jit(solution)/shard_map/ppermute | solution.py:57
  81.3 1.5 %shard_map.89.refs_4_ = bf16[8,112,1024]{2,1,0:T(8,128)(2,1)} custom-call(bf16[112,512]{1,0:T(8,128)(2,1)S(1)} %collective-permute-done.26.refs_0_, bf16[112,512]{1,0:T(8,128)(2,1)S(1)} %collective-permute-done.27.refs_1_, bf16[112,512]{1,0:T(8,128)(2,1)S(1)} %collective-permute-done.28.refs_2_, ...), custom_call_target="tpu_custom_call", output_to_operand_aliasing={{}: (5, {})} | custom-call | tf_op jit(solution)/shard_map/pallas_call | solution.py:219
  82.8 1.2 %collective-permute-done.24.refs_1_ = bf16[112,512]{1,0:T(8,128)(2,1)S(1)} collective-permute-done((bf16[112,512]{1,0:T(8,128)(2,1)S(1)}, bf16[112,512]{1,0:T(8,128)(2,1)S(1)}, u32[]{:S(2)}, u32[]{:S(2)}) %collective-permute-start.24) | collective-permute-done | bytes 114720 | tf_op jit(solution)/shard_map/ppermute | solution.py:57
  84.6 1.3 %shard_map.90 = bf16[8,112,1024]{2,1,0:T(8,128)(2,1)} custom-call(bf16[112,512]{1,0:T(8,128)(2,1)S(1)} %collective-permute-done.23.refs_0_, bf16[112,512]{1,0:T(8,128)(2,1)S(1)} %collective-permute-done.24.refs_1_, bf16[112,512]{1,0:T(8,128)(2,1)S(1)} %collective-permute-done.25.refs_2_, ...), custom_call_target="tpu_custom_call", output_to_operand_aliasing={{}: (4, {})} | custom-call | tf_op jit(solution)/shard_map/pallas_call | solution.py:219
  (47 shorter events, 12.2 us)
Async XLA Ops:
  3.2 9.3 %collective-permute-start = (bf16[128,512]{1,0:T(8,128)(2,1)S(1)}, bf16[128,512]{1,0:T(8,128)(2,1)S(1)}, u32[]{:S(2)}, u32[]{:S(2)}) collective-permute-start(bf16[128,512]{1,0:T(8,128)(2,1)S(1)} %get-tuple-element.36), channel_id=1, source_target_pairs={{0,2},{1,3},{2,4},{3,5},{4,6},{5,7},{6,0},{7,1},{8,10},{9,11},{10,... | collective-permute-start | bytes 393224 | tf_op jit(solution)/shard_map/ppermute | solution.py:57
  4.8 8.7 %collective-permute-start.1 = (bf16[128,512]{1,0:T(8,128)(2,1)S(1)}, bf16[128,512]{1,0:T(8,128)(2,1)S(1)}, u32[]{:S(2)}, u32[]{:S(2)}) collective-permute-start(bf16[128,512]{1,0:T(8,128)(2,1)S(1)} %get-tuple-element.37), channel_id=1, source_target_pairs={{0,4},{1,5},{2,6},{3,7},{4,0},{5,1},{6,2},{7,3},{8,12},{9,13},{10,... | collective-permute-start | bytes 393224 | tf_op jit(solution)/shard_map/ppermute | solution.py:57
  7.5 6.0 %collective-permute-start.2 = (bf16[128,512]{1,0:T(8,128)(2,1)S(1)}, bf16[128,512]{1,0:T(8,128)(2,1)S(1)}, u32[]{:S(2)}, u32[]{:S(2)}) collective-permute-start(bf16[128,512]{1,0:T(8,128)(2,1)S(1)} %get-tuple-element.38), channel_id=1, source_target_pairs={{0,6},{1,7},{2,0},{3,1},{4,2},{5,3},{6,4},{7,5},{8,14},{9,15},{10,... | collective-permute-start | bytes 393224 | tf_op jit(solution)/shard_map/ppermute | solution.py:57
  12.0 24.6 %collective-permute-start.8 = (bf16[2,4,112,512]{3,2,1,0:T(8,128)(2,1)S(1)}, bf16[2,4,112,512]{3,2,1,0:T(8,128)(2,1)S(1)}, u32[]{:S(2)}, u32[]{:S(2)}) collective-permute-start(bf16[2,4,112,512]{3,2,1,0:T(8,128)(2,1)S(1)} %get-tuple-element.41), channel_id=1, source_target_pairs={{0,8},{8,0},{16,24},{24,16},{32,40},{40,32},{48,56},{56,48},{64,72... | collective-permute-start | bytes 2752520 | tf_op jit(solution)/shard_map/ppermute | solution.py:45
  12.1 24.5 %collective-permute-start.9 = (bf16[2,4,112,512]{3,2,1,0:T(8,128)(2,1)S(1)}, bf16[2,4,112,512]{3,2,1,0:T(8,128)(2,1)S(1)}, u32[]{:S(2)}, u32[]{:S(2)}) collective-permute-start(bf16[2,4,112,512]{3,2,1,0:T(8,128)(2,1)S(1)} %get-tuple-element.42), channel_id=1, source_target_pairs={{0,8},{8,0},{16,24},{24,16},{32,40},{40,32},{48,56},{56,48},{64,72... | collective-permute-start | bytes 2752520 | tf_op jit(solution)/shard_map/ppermute | solution.py:45
  13.6 12.0 %collective-permute-start.3 = (bf16[128,512]{1,0:T(8,128)(2,1)S(1)}, bf16[128,512]{1,0:T(8,128)(2,1)S(1)}, u32[]{:S(2)}, u32[]{:S(2)}) collective-permute-start(bf16[128,512]{1,0:T(8,128)(2,1)S(1)} %get-tuple-element.40), channel_id=1, source_target_pairs={{0,1},{1,0},{2,3},{3,2},{4,5},{5,4},{6,7},{7,6},{8,9},{9,8},{10,11... | collective-permute-start | bytes 393224 | tf_op jit(solution)/shard_map/ppermute | solution.py:61
  25.6 6.3 %collective-permute-start.4 = (bf16[128,512]{1,0:T(8,128)(2,1)S(1)}, bf16[128,512]{1,0:T(8,128)(2,1)S(1)}, u32[]{:S(2)}, u32[]{:S(2)}) collective-permute-start(bf16[128,512]{1,0:T(8,128)(2,1)S(1)} %shard_map.79.p0), channel_id=1, source_target_pairs={{0,2},{1,3},{2,4},{3,5},{4,6},{5,7},{6,0},{7,1},{8,10},{9,11},{10,... | collective-permute-start | bytes 393224 | tf_op jit(solution)/shard_map/ppermute | solution.py:57
  27.1 6.8 %collective-permute-start.5 = (bf16[128,512]{1,0:T(8,128)(2,1)S(1)}, bf16[128,512]{1,0:T(8,128)(2,1)S(1)}, u32[]{:S(2)}, u32[]{:S(2)}) collective-permute-start(bf16[128,512]{1,0:T(8,128)(2,1)S(1)} %shard_map.79.p0), channel_id=1, source_target_pairs={{0,4},{1,5},{2,6},{3,7},{4,0},{5,1},{6,2},{7,3},{8,12},{9,13},{10,... | collective-permute-start | bytes 393224 | tf_op jit(solution)/shard_map/ppermute | solution.py:57
  29.6 5.0 %collective-permute-start.6 = (bf16[128,512]{1,0:T(8,128)(2,1)S(1)}, bf16[128,512]{1,0:T(8,128)(2,1)S(1)}, u32[]{:S(2)}, u32[]{:S(2)}) collective-permute-start(bf16[128,512]{1,0:T(8,128)(2,1)S(1)} %shard_map.79.p0), channel_id=1, source_target_pairs={{0,6},{1,7},{2,0},{3,1},{4,2},{5,3},{6,4},{7,5},{8,14},{9,15},{10,... | collective-permute-start | bytes 393224 | tf_op jit(solution)/shard_map/ppermute | solution.py:57
  34.6 2.0 %collective-permute-start.7 = (bf16[512,512]{1,0:T(8,128)(2,1)S(1)}, bf16[512,512]{1,0:T(8,128)(2,1)S(1)}, u32[]{:S(2)}, u32[]{:S(2)}) collective-permute-start(bf16[512,512]{1,0:T(8,128)(2,1)S(1)} %pad_maximum_fusion), channel_id=1, source_target_pairs={{0,8},{8,0},{16,24},{24,16},{32,40},{40,32},{48,56},{56,48},{64,72... | collective-permute-start | bytes 1572872 | tf_op jit(solution)/shard_map/ppermute | solution.py:45
  37.3 19.8 %collective-permute-start.18 = (bf16[448,512]{1,0:T(8,128)(2,1)S(1)}, bf16[448,512]{1,0:T(8,128)(2,1)S(1)}, u32[]{:S(2)}, u32[]{:S(2)}) collective-permute-start(bf16[448,512]{1,0:T(8,128)(2,1)S(1)} %get-tuple-element.52), channel_id=1, source_target_pairs={{0,16},{8,24},{16,0},{24,8},{32,48},{40,56},{48,32},{56,40},{64,80... | collective-permute-start | bytes 1376264 | tf_op jit(solution)/shard_map/ppermute | solution.py:53
  37.9 7.1 %collective-permute-start.10 = (bf16[112,512]{1,0:T(8,128)(2,1)S(1)}, bf16[112,512]{1,0:T(8,128)(2,1)S(1)}, u32[]{:S(2)}, u32[]{:S(2)}) collective-permute-start(bf16[112,512]{1,0:T(8,128)(2,1)S(1)} %get-tuple-element.44), channel_id=1, source_target_pairs={{0,64},{8,72},{16,80},{24,88},{32,96},{40,104},{48,112},{56,120},{... | collective-permute-start | bytes 344072 | tf_op jit(solution)/shard_map/ppermute | solution.py:49
  39.5 9.3 %collective-permute-start.11 = (bf16[112,512]{1,0:T(8,128)(2,1)S(1)}, bf16[112,512]{1,0:T(8,128)(2,1)S(1)}, u32[]{:S(2)}, u32[]{:S(2)}) collective-permute-start(bf16[112,512]{1,0:T(8,128)(2,1)S(1)} %get-tuple-element.45), channel_id=1, source_target_pairs={{0,128},{8,136},{16,144},{24,152},{32,160},{40,168},{48,176},{56,1... | collective-permute-start | bytes 344072 | tf_op jit(solution)/shard_map/ppermute | solution.py:49
  42.4 6.4 %collective-permute-start.12 = (bf16[112,512]{1,0:T(8,128)(2,1)S(1)}, bf16[112,512]{1,0:T(8,128)(2,1)S(1)}, u32[]{:S(2)}, u32[]{:S(2)}) collective-permute-start(bf16[112,512]{1,0:T(8,128)(2,1)S(1)} %get-tuple-element.46), channel_id=1, source_target_pairs={{0,192},{8,200},{16,208},{24,216},{32,224},{40,232},{48,240},{56,2... | collective-permute-start | bytes 344072 | tf_op jit(solution)/shard_map/ppermute | solution.py:49
  44.2 21.2 %copy-start = (f32[1,112,512]{2,1,0:T(8,128)S(1)}, f32[1,112,512]{2,1,0:T(8,128)}, u32[]{:S(2)}) copy-start(f32[1,112,512]{2,1,0:T(8,128)} %first.3) | copy-start | bytes 688132
  44.3 21.2 %copy-start.1 = (f32[1,112,512]{2,1,0:T(8,128)S(1)}, f32[1,112,512]{2,1,0:T(8,128)}, u32[]{:S(2)}) copy-start(f32[1,112,512]{2,1,0:T(8,128)} %second.3) | copy-start | bytes 688132
  44.3 7.2 %collective-permute-start.14 = (bf16[112,512]{1,0:T(8,128)(2,1)S(1)}, bf16[112,512]{1,0:T(8,128)(2,1)S(1)}, u32[]{:S(2)}, u32[]{:S(2)}) collective-permute-start(bf16[112,512]{1,0:T(8,128)(2,1)S(1)} %get-tuple-element.48), channel_id=1, source_target_pairs={{0,64},{8,72},{16,80},{24,88},{32,96},{40,104},{48,112},{56,120},{... | collective-permute-start | bytes 344072 | tf_op jit(solution)/shard_map/ppermute | solution.py:49
  45.0 8.0 %collective-permute-start.15 = (bf16[112,512]{1,0:T(8,128)(2,1)S(1)}, bf16[112,512]{1,0:T(8,128)(2,1)S(1)}, u32[]{:S(2)}, u32[]{:S(2)}) collective-permute-start(bf16[112,512]{1,0:T(8,128)(2,1)S(1)} %get-tuple-element.49), channel_id=1, source_target_pairs={{0,128},{8,136},{16,144},{24,152},{32,160},{40,168},{48,176},{56,1... | collective-permute-start | bytes 344072 | tf_op jit(solution)/shard_map/ppermute | solution.py:49
  48.9 4.8 %collective-permute-start.16 = (bf16[112,512]{1,0:T(8,128)(2,1)S(1)}, bf16[112,512]{1,0:T(8,128)(2,1)S(1)}, u32[]{:S(2)}, u32[]{:S(2)}) collective-permute-start(bf16[112,512]{1,0:T(8,128)(2,1)S(1)} %get-tuple-element.50), channel_id=1, source_target_pairs={{0,192},{8,200},{16,208},{24,216},{32,224},{40,232},{48,240},{56,2... | collective-permute-start | bytes 344072 | tf_op jit(solution)/shard_map/ppermute | solution.py:49
  48.9 12.5 %collective-permute-start.13 = (bf16[112,512]{1,0:T(8,128)(2,1)S(1)}, bf16[112,512]{1,0:T(8,128)(2,1)S(1)}, u32[]{:S(2)}, u32[]{:S(2)}) collective-permute-start(bf16[112,512]{1,0:T(8,128)(2,1)S(1)} %shard_map.82), channel_id=1, source_target_pairs={{0,48},{8,56},{16,32},{24,40},{32,16},{40,24},{48,0},{56,8},{64,11... | collective-permute-start | bytes 344072 | tf_op jit(solution)/shard_map/ppermute | solution.py:53
  53.7 7.8 %collective-permute-start.17 = (bf16[112,512]{1,0:T(8,128)(2,1)S(1)}, bf16[112,512]{1,0:T(8,128)(2,1)S(1)}, u32[]{:S(2)}, u32[]{:S(2)}) collective-permute-start(bf16[112,512]{1,0:T(8,128)(2,1)S(1)} %shard_map.84), channel_id=1, source_target_pairs={{0,32},{8,40},{16,48},{24,56},{32,0},{40,8},{48,16},{56,24},{64,96... | collective-permute-start | bytes 344072 | tf_op jit(solution)/shard_map/ppermute | solution.py:53
  57.2 6.1 %collective-permute-start.19 = (bf16[112,512]{1,0:T(8,128)(2,1)S(1)}, bf16[112,512]{1,0:T(8,128)(2,1)S(1)}, u32[]{:S(2)}, u32[]{:S(2)}) collective-permute-start(bf16[112,512]{1,0:T(8,128)(2,1)S(1)} %get-tuple-element.54), channel_id=1, source_target_pairs={{0,64},{8,72},{16,80},{24,88},{32,96},{40,104},{48,112},{56,120},{... | collective-permute-start | bytes 344072 | tf_op jit(solution)/shard_map/ppermute | solution.py:49
  57.7 6.9 %collective-permute-start.20 = (bf16[112,512]{1,0:T(8,128)(2,1)S(1)}, bf16[112,512]{1,0:T(8,128)(2,1)S(1)}, u32[]{:S(2)}, u32[]{:S(2)}) collective-permute-start(bf16[112,512]{1,0:T(8,128)(2,1)S(1)} %get-tuple-element.55), channel_id=1, source_target_pairs={{0,128},{8,136},{16,144},{24,152},{32,160},{40,168},{48,176},{56,1... | collective-permute-start | bytes 344072 | tf_op jit(solution)/shard_map/ppermute | solution.py:49
  60.6 4.8 %collective-permute-start.21 = (bf16[112,512]{1,0:T(8,128)(2,1)S(1)}, bf16[112,512]{1,0:T(8,128)(2,1)S(1)}, u32[]{:S(2)}, u32[]{:S(2)}) collective-permute-start(bf16[112,512]{1,0:T(8,128)(2,1)S(1)} %get-tuple-element.56), channel_id=1, source_target_pairs={{0,192},{8,200},{16,208},{24,216},{32,224},{40,232},{48,240},{56,2... | collective-permute-start | bytes 344072 | tf_op jit(solution)/shard_map/ppermute | solution.py:49
  65.7 10.1 %collective-permute-start.22 = (bf16[112,512]{1,0:T(8,128)(2,1)S(1)}, bf16[112,512]{1,0:T(8,128)(2,1)S(1)}, u32[]{:S(2)}, u32[]{:S(2)}) collective-permute-start(bf16[112,512]{1,0:T(8,128)(2,1)S(1)} %get-tuple-element.57.refs_0_), channel_id=1, source_target_pairs={{0,1},{1,0},{2,3},{3,2},{4,5},{5,4},{6,7},{7,6},{8,9},{9,8},{10,11... | collective-permute-start | bytes 344072 | tf_op jit(solution)/shard_map/ppermute | solution.py:61
  70.5 9.3 %collective-permute-start.26 = (bf16[112,512]{1,0:T(8,128)(2,1)S(1)}, bf16[112,512]{1,0:T(8,128)(2,1)S(1)}, u32[]{:S(2)}, u32[]{:S(2)}) collective-permute-start(bf16[112,512]{1,0:T(8,128)(2,1)S(1)} %get-tuple-element.57.refs_0_), channel_id=1, source_target_pairs={{0,2},{1,3},{2,4},{3,5},{4,6},{5,7},{6,0},{7,1},{8,10},{9,11},{10,... | collective-permute-start | bytes 344072 | tf_op jit(solution)/shard_map/ppermute | solution.py:57
  71.6 9.7 %collective-permute-start.27 = (bf16[112,512]{1,0:T(8,128)(2,1)S(1)}, bf16[112,512]{1,0:T(8,128)(2,1)S(1)}, u32[]{:S(2)}, u32[]{:S(2)}) collective-permute-start(bf16[112,512]{1,0:T(8,128)(2,1)S(1)} %get-tuple-element.57.refs_0_), channel_id=1, source_target_pairs={{0,4},{1,5},{2,6},{3,7},{4,0},{5,1},{6,2},{7,3},{8,12},{9,13},{10,... | collective-permute-start | bytes 344072 | tf_op jit(solution)/shard_map/ppermute | solution.py:57
  74.5 6.7 %collective-permute-start.28 = (bf16[112,512]{1,0:T(8,128)(2,1)S(1)}, bf16[112,512]{1,0:T(8,128)(2,1)S(1)}, u32[]{:S(2)}, u32[]{:S(2)}) collective-permute-start(bf16[112,512]{1,0:T(8,128)(2,1)S(1)} %get-tuple-element.57.refs_0_), channel_id=1, source_target_pairs={{0,6},{1,7},{2,0},{3,1},{4,2},{5,3},{6,4},{7,5},{8,14},{9,15},{10,... | collective-permute-start | bytes 344072 | tf_op jit(solution)/shard_map/ppermute | solution.py:57
  75.8 7.0 %collective-permute-start.23 = (bf16[112,512]{1,0:T(8,128)(2,1)S(1)}, bf16[112,512]{1,0:T(8,128)(2,1)S(1)}, u32[]{:S(2)}, u32[]{:S(2)}) collective-permute-start(bf16[112,512]{1,0:T(8,128)(2,1)S(1)} %collective-permute-done.22.refs_3_), channel_id=1, source_target_pairs={{0,2},{1,3},{2,4},{3,5},{4,6},{5,7},{6,0},{7,1},{8,10},{9,11},{10,... | collective-permute-start | bytes 344072 | tf_op jit(solution)/shard_map/ppermute | solution.py:57
  77.7 6.3 %collective-permute-start.24 = (bf16[112,512]{1,0:T(8,128)(2,1)S(1)}, bf16[112,512]{1,0:T(8,128)(2,1)S(1)}, u32[]{:S(2)}, u32[]{:S(2)}) collective-permute-start(bf16[112,512]{1,0:T(8,128)(2,1)S(1)} %collective-permute-done.22.refs_3_), channel_id=1, source_target_pairs={{0,4},{1,5},{2,6},{3,7},{4,0},{5,1},{6,2},{7,3},{8,12},{9,13},{10,... | collective-permute-start | bytes 344072 | tf_op jit(solution)/shard_map/ppermute | solution.py:57
  79.8 4.8 %collective-permute-start.25 = (bf16[112,512]{1,0:T(8,128)(2,1)S(1)}, bf16[112,512]{1,0:T(8,128)(2,1)S(1)}, u32[]{:S(2)}, u32[]{:S(2)}) collective-permute-start(bf16[112,512]{1,0:T(8,128)(2,1)S(1)} %collective-permute-done.22.refs_3_), channel_id=1, source_target_pairs={{0,6},{1,7},{2,0},{3,1},{4,2},{5,3},{6,4},{7,5},{8,14},{9,15},{10,... | collective-permute-start | bytes 344072 | tf_op jit(solution)/shard_map/ppermute | solution.py:57

commit v4 on v3

--- a/solution.py
+++ b/solution.py
@@ -78,26 +78,25 @@
     )
 
 
-def project_body(feat, basis, own, s1, s2, s3, fbuf, bbuf, sems):
+def project_body(feat, basis, own, s1, s2, s3, fbuf, bbuf, acc, sems):
     _, _, _, x, _ = place()
     rows = own.shape[0]
-    order = ((2, s2), (1, s1), (3, s3), (0, own))
     part = basis.shape[0] // NX
     copies = []
     for i in range(NX):
         cut = pl.ds(i * part, part)
         copies.append(pltpu.make_async_copy(basis.at[cut, :], bbuf.at[cut, :], sems.at[NX + i]))
-    for k, _ in order:
-        start = pl.multiple_of(lax.rem(x + k, NX) * rows, rows)
-        copies.append(pltpu.make_async_copy(feat.at[pl.ds(start, rows), :], fbuf.at[k], sems.at[k]))
+        copies.append(pltpu.make_async_copy(feat.at[:, cut], fbuf.at[i], sems.at[i]))
     for copy in copies:
         copy.start()
-    for copy in copies[:NX]:
-        copy.wait()
-    for (k, out), copy in zip(order, copies[NX:]):
-        copy.wait()
-        t = jnp.dot(fbuf[k], bbuf[...], preferred_element_type=f32)
-        out[...] = t.astype(out.dtype)
+    for i in range(NX):
+        copies[2 * i].wait()
+        copies[2 * i + 1].wait()
+        t = jnp.dot(fbuf[i], bbuf[i * part : (i + 1) * part, :], preferred_element_type=f32)
+        acc[...] = t if i == 0 else acc[...] + t
+    for k, out in ((1, s1), (3, s3), (2, s2), (0, own)):
+        start = pl.multiple_of(lax.rem(x + k, NX) * rows, rows)
+        out[...] = acc[pl.ds(start, rows), :].astype(out.dtype)
 
 
 def turn_body(grads, basis, _, keep, *refs):
@@ -155,14 +154,13 @@
         outs[ry][...] = t.astype(outs[ry].dtype)
 
 
-def low_near_body(acc, q, *refs):
-    other, (own, send) = refs[:SPLIT], refs[SPLIT:]
+def low_near_body(rz, acc, q, *refs):
+    other, out = refs[:SPLIT], refs[SPLIT]
     rows = other[0].shape[2]
     for ry in range(NY):
-        for rz, out in ((1, send), (0, own)):
-            t = acc[ry, rz * rows : (rz + 1) * rows, :]
-            t = t + jnp.dot(other[ry * SPLIT // NY][ry % (NY // SPLIT), rz], q[...], preferred_element_type=f32)
-            out[ry * rows : (ry + 1) * rows, :] = t.astype(out.dtype)
+        t = acc[ry, rz * rows : (rz + 1) * rows, :]
+        t = t + jnp.dot(other[ry * SPLIT // NY][ry % (NY // SPLIT), rz], q[...], preferred_element_type=f32)
+        out[ry * rows : (ry + 1) * rows, :] = t.astype(out.dtype)
 
 
 def sum_far_body(own, r1, r2, r3, out):
@@ -241,8 +239,9 @@
         [((toks, rank), f32)] + [((toks, rank), bf16)] * 3,
         2,
         scratch=[
-            pltpu.VMEM((NX, toks, width), bf16),
+            pltpu.VMEM((NX, tokens, width // NX), bf16),
             pltpu.VMEM((width, rank), bf16),
+            pltpu.VMEM((tokens, rank), f32),
             pltpu.SemaphoreType.DMA((2 * NX,)),
         ],
         in_specs=[HBM] * 2,
@@ -264,7 +263,7 @@
         ],
         in_specs=[HBM, HBM, ANY],
     )(grads_in, basis_in, own)
-    total, sent = call(sum_x_body, [((toks, rank), f32), ((toks, rank), bf16)], 4)(own, r1, r2, r3)
+    total, sent = call(sum_x_body, [((toks, rank), f32), ((toks, rank), bf16)], 4)(own, r1, r3, r2)
     half_sum = to_h(sent)
     other = [to_core(a) for a in sends]
     p0 = call(sum_h_body, [((toks, rank), bf16)], 2)(total, half_sum)[0]
@@ -285,8 +284,11 @@
 
     own3, *far3 = low_far(3)
     far3 = over_y(*far3)
-    near, send = call(low_near_body, [(four, f32), (four, bf16)], 2 + SPLIT)(acc, q, *other)
-    send = to_z(send, 1)
+    def low_near(rz, dtype):
+        return call(functools.partial(low_near_body, rz), [(four, dtype)], 2 + SPLIT)(acc, q, *other)[0]
+
+    send = to_z(low_near(1, bf16), 1)
+    near = low_near(0, f32)
     own2, *far2 = low_far(2)
     far2 = over_y(*far2)
     z3 = to_z(call(sum_far_body, [(one, bf16)], 4)(own3, *far3)[0], 3)

time: 86.2 us -> 85.2 us (0.988)
  starting transfers between devices: 49 us -> 47.8 us
    ppermute x12, starting transfers between devices: 19.2 us -> 17.6 us  [to_x(): return lax.ppermute(a, 'shard', shard_perm(lambda x, h: (x + k, h)))]
    ppermute x12, waiting for transfers between devices: 7.13 us -> 8.05 us  [to_x(): return lax.ppermute(a, 'shard', shard_perm(lambda x, h: (x + k, h)))]
  transfers between devices with their start and end apart: 29 -> 29, of which waited for: 15 -> 15; matrix products, arithmetic and copies ran while one was open for 0% -> 0% of each run, Pallas kernels for 10% -> 11%
where the time goes in v4:
time: 85.2 us; the launch traced here: 85.1 us
  starting transfers between devices  47.8 us (56%)
  waiting for transfers between devices  23.1 us (27%)
  Pallas kernels  13.1 us (15%)
  between operations  0.97 us (1%)
    ppermute x12, starting transfers between devices, to_x(): return lax.ppermute(a, 'shard', shard_perm(lambda x, h: (x + k, h)))  17.6 us
    ppermute x9, starting transfers between devices, to_y(): return lax.ppermute(a, 'dp', dp_perm(lambda y, z, c: (y + k, z, c)))  12.3 us
    ppermute x2, starting transfers between devices, to_h(): return lax.ppermute(a, 'shard', shard_perm(lambda x, h: (x, 1 - h)))  11.1 us
    ppermute x9, waiting for transfers between devices, to_y(): return lax.ppermute(a, 'dp', dp_perm(lambda y, z, c: (y + k, z, c)))  8.39 us
    ppermute x12, waiting for transfers between devices, to_x(): return lax.ppermute(a, 'shard', shard_perm(lambda x, h: (x + k, h)))  8.05 us
    ppermute x3, starting transfers between devices, to_z(): return lax.ppermute(a, 'dp', dp_perm(lambda y, z, c: (y, z ^ k, c)))  6.1 us
    ppermute x2, waiting for transfers between devices, to_h(): return lax.ppermute(a, 'shard', shard_perm(lambda x, h: (x, 1 - h)))  5.9 us
    pallas_call x3, Pallas kernels, update_part(): call(functools.partial(update_body, moves, aliased), [((NX * NH, rows, co...  3.82 us
  transfers between devices with their start and end apart: 29, of which 15 were waited for; matrix products, arithmetic and copies ran while one was open for 0% of the time, Pallas kernels for 11%

profile of v4, /device:TPU:32, one launch (start us, length us, event | category | flops | bytes accessed | tf_op | source)
XLA Modules:
  0.0 85.1 jit_solution(9381733044644582850)
XLA Ops:
  0.6 2.0 %shard_map.76 = (f32[128,512]{1,0:T(8,128)S(1)}, bf16[128,512]{1,0:T(8,128)(2,1)S(1)}, bf16[128,512]{1,0:T(8,128)(2,1)S(1)}, bf16[128,512]{1,0:T(8,128)(2,1)S(1)}) custom-call(bf16[512,1024]{1,0:T(8,128)(2,1)} %feat.1, bf16[1024,512]{1,0:T(8,128)(2,1)} %basis.3), custom_call_target="tpu_custom_call" | custom-call | tf_op jit(solution)/shard_map/pallas_call | solution.py:237
  2.6 1.6 %collective-permute-start = (bf16[128,512]{1,0:T(8,128)(2,1)S(1)}, bf16[128,512]{1,0:T(8,128)(2,1)S(1)}, u32[]{:S(2)}, u32[]{:S(2)}) collective-permute-start(bf16[128,512]{1,0:T(8,128)(2,1)S(1)} %get-tuple-element.34), channel_id=1, source_target_pairs={{0,2},{1,3},{2,4},{3,5},{4,6},{5,7},{6,0},{7,1},{8,10},{9,11},{10,... | collective-permute-start | bytes 393224 | tf_op jit(solution)/shard_map/ppermute | solution.py:57
  4.2 1.7 %collective-permute-start.1 = (bf16[128,512]{1,0:T(8,128)(2,1)S(1)}, bf16[128,512]{1,0:T(8,128)(2,1)S(1)}, u32[]{:S(2)}, u32[]{:S(2)}) collective-permute-start(bf16[128,512]{1,0:T(8,128)(2,1)S(1)} %get-tuple-element.35), channel_id=1, source_target_pairs={{0,6},{1,7},{2,0},{3,1},{4,2},{5,3},{6,4},{7,5},{8,14},{9,15},{10,... | collective-permute-start | bytes 393224 | tf_op jit(solution)/shard_map/ppermute | solution.py:57
  6.0 1.8 %collective-permute-start.2 = (bf16[128,512]{1,0:T(8,128)(2,1)S(1)}, bf16[128,512]{1,0:T(8,128)(2,1)S(1)}, u32[]{:S(2)}, u32[]{:S(2)}) collective-permute-start(bf16[128,512]{1,0:T(8,128)(2,1)S(1)} %get-tuple-element.36), channel_id=1, source_target_pairs={{0,4},{1,5},{2,6},{3,7},{4,0},{5,1},{6,2},{7,3},{8,12},{9,13},{10,... | collective-permute-start | bytes 393224 | tf_op jit(solution)/shard_map/ppermute | solution.py:57
  7.8 3.0 %shard_map.77 = (bf16[4,4,112,512]{3,2,1,0:T(8,128)(2,1)S(1)}, bf16[2,4,112,512]{3,2,1,0:T(8,128)(2,1)S(1)}, bf16[2,4,112,512]{3,2,1,0:T(8,128)(2,1)S(1)}, bf16[512,1024]{1,0:T(8,128)(2,1)S(1)}) custom-call(bf16[512,3584]{1,0:T(8,128)(2,1)} %grads.1, bf16[1024,512]{1,0:T(8,128)(2,1)} %basis.3, f32[128,512]{1,0:T(8,128)S(1)} %get-tuple-element.32._.own), custom_call_target="tpu_custom_call" | custom-call | tf_op jit(solution)/shard_map/pallas_call | solution.py:254
  11.4 1.6 %collective-permute-done.2.r3 = bf16[128,512]{1,0:T(8,128)(2,1)S(1)} collective-permute-done((bf16[128,512]{1,0:T(8,128)(2,1)S(1)}, bf16[128,512]{1,0:T(8,128)(2,1)S(1)}, u32[]{:S(2)}, u32[]{:S(2)}) %collective-permute-start.2) | collective-permute-done | bytes 131104 | tf_op jit(solution)/shard_map/ppermute | solution.py:57
  13.0 6.4 %collective-permute-start.3 = (bf16[128,512]{1,0:T(8,128)(2,1)S(1)}, bf16[128,512]{1,0:T(8,128)(2,1)S(1)}, u32[]{:S(2)}, u32[]{:S(2)}) collective-permute-start(bf16[128,512]{1,0:T(8,128)(2,1)S(1)} %get-tuple-element.38), channel_id=1, source_target_pairs={{0,1},{1,0},{2,3},{3,2},{4,5},{5,4},{6,7},{7,6},{8,9},{9,8},{10,11... | collective-permute-start | bytes 393224 | tf_op jit(solution)/shard_map/ppermute | solution.py:61
  19.4 5.7 %collective-permute-done.3.other = bf16[128,512]{1,0:T(8,128)(2,1)S(1)} collective-permute-done((bf16[128,512]{1,0:T(8,128)(2,1)S(1)}, bf16[128,512]{1,0:T(8,128)(2,1)S(1)}, u32[]{:S(2)}, u32[]{:S(2)}) %collective-permute-start.3) | collective-permute-done | bytes 131104 | tf_op jit(solution)/shard_map/ppermute | solution.py:61
  25.2 3.1 %collective-permute-start.5 = (bf16[128,512]{1,0:T(8,128)(2,1)S(1)}, bf16[128,512]{1,0:T(8,128)(2,1)S(1)}, u32[]{:S(2)}, u32[]{:S(2)}) collective-permute-start(bf16[128,512]{1,0:T(8,128)(2,1)S(1)} %shard_map.79.p0), channel_id=1, source_target_pairs={{0,4},{1,5},{2,6},{3,7},{4,0},{5,1},{6,2},{7,3},{8,12},{9,13},{10,... | collective-permute-start | bytes 393224 | tf_op jit(solution)/shard_map/ppermute | solution.py:57
  28.9 2.5 %collective-permute-done.4.p1 = bf16[128,512]{1,0:T(8,128)(2,1)S(1)} collective-permute-done((bf16[128,512]{1,0:T(8,128)(2,1)S(1)}, bf16[128,512]{1,0:T(8,128)(2,1)S(1)}, u32[]{:S(2)}, u32[]{:S(2)}) %collective-permute-start.4) | collective-permute-done | bytes 131104 | tf_op jit(solution)/shard_map/ppermute | solution.py:57
  31.4 1.4 %collective-permute-done.5.p2 = bf16[128,512]{1,0:T(8,128)(2,1)S(1)} collective-permute-done((bf16[128,512]{1,0:T(8,128)(2,1)S(1)}, bf16[128,512]{1,0:T(8,128)(2,1)S(1)}, u32[]{:S(2)}, u32[]{:S(2)}) %collective-permute-start.5) | collective-permute-done | bytes 131104 | tf_op jit(solution)/shard_map/ppermute | solution.py:57
  33.8 1.1 %shard_map.80.acc = f32[4,448,512]{2,1,0:T(8,128)S(1)} custom-call(bf16[4,4,112,512]{3,2,1,0:T(8,128)(2,1)S(1)} %get-tuple-element.33.keep, bf16[128,512]{1,0:T(8,128)(2,1)S(1)} %shard_map.79.p0, bf16[128,512]{1,0:T(8,128)(2,1)S(1)} %collective-permute-done.4.p1, bf16[128,512]{1,0:T(8,128)(2,1)S(1)} %collective-permute-done.5.p2, ...), custom_call_target="tpu_custom_call" | custom-call | tf_op jit(solution)/shard_map/pallas_call | solution.py:273
  36.7 1.7 %collective-permute-start.10 = (bf16[112,512]{1,0:T(8,128)(2,1)S(1)}, bf16[112,512]{1,0:T(8,128)(2,1)S(1)}, u32[]{:S(2)}, u32[]{:S(2)}) collective-permute-start(bf16[112,512]{1,0:T(8,128)(2,1)S(1)} %get-tuple-element.42), channel_id=1, source_target_pairs={{0,64},{8,72},{16,80},{24,88},{32,96},{40,104},{48,112},{56,120},{... | collective-permute-start | bytes 344072 | tf_op jit(solution)/shard_map/ppermute | solution.py:49
  38.4 2.9 %collective-permute-start.11 = (bf16[112,512]{1,0:T(8,128)(2,1)S(1)}, bf16[112,512]{1,0:T(8,128)(2,1)S(1)}, u32[]{:S(2)}, u32[]{:S(2)}) collective-permute-start(bf16[112,512]{1,0:T(8,128)(2,1)S(1)} %get-tuple-element.43), channel_id=1, source_target_pairs={{0,128},{8,136},{16,144},{24,152},{32,160},{40,168},{48,176},{56,1... | collective-permute-start | bytes 344072 | tf_op jit(solution)/shard_map/ppermute | solution.py:49
  41.3 1.3 %collective-permute-start.12 = (bf16[112,512]{1,0:T(8,128)(2,1)S(1)}, bf16[112,512]{1,0:T(8,128)(2,1)S(1)}, u32[]{:S(2)}, u32[]{:S(2)}) collective-permute-start(bf16[112,512]{1,0:T(8,128)(2,1)S(1)} %get-tuple-element.44), channel_id=1, source_target_pairs={{0,192},{8,200},{16,208},{24,216},{32,224},{40,232},{48,240},{56,2... | collective-permute-start | bytes 344072 | tf_op jit(solution)/shard_map/ppermute | solution.py:49
  43.8 1.3 %collective-permute-start.15 = (bf16[112,512]{1,0:T(8,128)(2,1)S(1)}, bf16[112,512]{1,0:T(8,128)(2,1)S(1)}, u32[]{:S(2)}, u32[]{:S(2)}) collective-permute-start(bf16[112,512]{1,0:T(8,128)(2,1)S(1)} %get-tuple-element.47), channel_id=1, source_target_pairs={{0,128},{8,136},{16,144},{24,152},{32,160},{40,168},{48,176},{56,1... | collective-permute-start | bytes 344072 | tf_op jit(solution)/shard_map/ppermute | solution.py:49
  45.2 2.5 %collective-permute-done.11.r2 = bf16[112,512]{1,0:T(8,128)(2,1)S(1)} collective-permute-done((bf16[112,512]{1,0:T(8,128)(2,1)S(1)}, bf16[112,512]{1,0:T(8,128)(2,1)S(1)}, u32[]{:S(2)}, u32[]{:S(2)}) %collective-permute-start.11) | collective-permute-done | bytes 114720 | tf_op jit(solution)/shard_map/ppermute | solution.py:49
  48.2 2.3 %collective-permute-start.13 = (bf16[112,512]{1,0:T(8,128)(2,1)S(1)}, bf16[112,512]{1,0:T(8,128)(2,1)S(1)}, u32[]{:S(2)}, u32[]{:S(2)}) collective-permute-start(bf16[112,512]{1,0:T(8,128)(2,1)S(1)} %shard_map.82), channel_id=1, source_target_pairs={{0,48},{8,56},{16,32},{24,40},{32,16},{40,24},{48,0},{56,8},{64,11... | collective-permute-start | bytes 344072 | tf_op jit(solution)/shard_map/ppermute | solution.py:53
  50.5 1.4 %collective-permute-done.15.r2 = bf16[112,512]{1,0:T(8,128)(2,1)S(1)} collective-permute-done((bf16[112,512]{1,0:T(8,128)(2,1)S(1)}, bf16[112,512]{1,0:T(8,128)(2,1)S(1)}, u32[]{:S(2)}, u32[]{:S(2)}) %collective-permute-start.15) | collective-permute-done | bytes 114720 | tf_op jit(solution)/shard_map/ppermute | solution.py:49
  52.5 3.7 %collective-permute-start.17 = (bf16[112,512]{1,0:T(8,128)(2,1)S(1)}, bf16[112,512]{1,0:T(8,128)(2,1)S(1)}, u32[]{:S(2)}, u32[]{:S(2)}) collective-permute-start(bf16[112,512]{1,0:T(8,128)(2,1)S(1)} %shard_map.84), channel_id=1, source_target_pairs={{0,32},{8,40},{16,48},{24,56},{32,0},{40,8},{48,16},{56,24},{64,96... | collective-permute-start | bytes 344072 | tf_op jit(solution)/shard_map/ppermute | solution.py:53
  56.9 2.9 %collective-permute-start.20 = (bf16[112,512]{1,0:T(8,128)(2,1)S(1)}, bf16[112,512]{1,0:T(8,128)(2,1)S(1)}, u32[]{:S(2)}, u32[]{:S(2)}) collective-permute-start(bf16[112,512]{1,0:T(8,128)(2,1)S(1)} %get-tuple-element.51), channel_id=1, source_target_pairs={{0,128},{8,136},{16,144},{24,152},{32,160},{40,168},{48,176},{56,1... | collective-permute-start | bytes 344072 | tf_op jit(solution)/shard_map/ppermute | solution.py:49
  59.8 0.9 %collective-permute-start.21 = (bf16[112,512]{1,0:T(8,128)(2,1)S(1)}, bf16[112,512]{1,0:T(8,128)(2,1)S(1)}, u32[]{:S(2)}, u32[]{:S(2)}) collective-permute-start(bf16[112,512]{1,0:T(8,128)(2,1)S(1)} %get-tuple-element.52), channel_id=1, source_target_pairs={{0,192},{8,200},{16,208},{24,216},{32,224},{40,232},{48,240},{56,2... | collective-permute-start | bytes 344072 | tf_op jit(solution)/shard_map/ppermute | solution.py:49
  60.7 1.8 %collective-permute-done.19.y1 = bf16[112,512]{1,0:T(8,128)(2,1)S(1)} collective-permute-done((bf16[112,512]{1,0:T(8,128)(2,1)S(1)}, bf16[112,512]{1,0:T(8,128)(2,1)S(1)}, u32[]{:S(2)}, u32[]{:S(2)}) %collective-permute-start.19) | collective-permute-done | bytes 114720 | tf_op jit(solution)/shard_map/ppermute | solution.py:49
  62.4 1.3 %collective-permute-done.20.y2 = bf16[112,512]{1,0:T(8,128)(2,1)S(1)} collective-permute-done((bf16[112,512]{1,0:T(8,128)(2,1)S(1)}, bf16[112,512]{1,0:T(8,128)(2,1)S(1)}, u32[]{:S(2)}, u32[]{:S(2)}) %collective-permute-start.20) | collective-permute-done | bytes 114720 | tf_op jit(solution)/shard_map/ppermute | solution.py:49
  64.8 4.8 %collective-permute-start.22 = (bf16[112,512]{1,0:T(8,128)(2,1)S(1)}, bf16[112,512]{1,0:T(8,128)(2,1)S(1)}, u32[]{:S(2)}, u32[]{:S(2)}) collective-permute-start(bf16[112,512]{1,0:T(8,128)(2,1)S(1)} %get-tuple-element.53.refs_0_), channel_id=1, source_target_pairs={{0,1},{1,0},{2,3},{3,2},{4,5},{5,4},{6,7},{7,6},{8,9},{9,8},{10,11... | collective-permute-start | bytes 344072 | tf_op jit(solution)/shard_map/ppermute | solution.py:61
  70.0 3.6 %collective-permute-start.27 = (bf16[112,512]{1,0:T(8,128)(2,1)S(1)}, bf16[112,512]{1,0:T(8,128)(2,1)S(1)}, u32[]{:S(2)}, u32[]{:S(2)}) collective-permute-start(bf16[112,512]{1,0:T(8,128)(2,1)S(1)} %get-tuple-element.53.refs_0_), channel_id=1, source_target_pairs={{0,4},{1,5},{2,6},{3,7},{4,0},{5,1},{6,2},{7,3},{8,12},{9,13},{10,... | collective-permute-start | bytes 344072 | tf_op jit(solution)/shard_map/ppermute | solution.py:57
  73.5 1.0 %shard_map.89.refs_5_ = bf16[8,112,1024]{2,1,0:T(8,128)(2,1)} custom-call(bf16[112,512]{1,0:T(8,128)(2,1)S(1)} %get-tuple-element.53.refs_0_, bf16[512,1024]{1,0:T(8,128)(2,1)S(1)} %get-tuple-element.54.refs_1_.refs_4_.refs_3_), custom_call_target="tpu_custom_call" | custom-call | tf_op jit(solution)/shard_map/pallas_call | solution.py:217
  74.8 1.9 %collective-permute-start.23 = (bf16[112,512]{1,0:T(8,128)(2,1)S(1)}, bf16[112,512]{1,0:T(8,128)(2,1)S(1)}, u32[]{:S(2)}, u32[]{:S(2)}) collective-permute-start(bf16[112,512]{1,0:T(8,128)(2,1)S(1)} %collective-permute-done.22.refs_3_), channel_id=1, source_target_pairs={{0,2},{1,3},{2,4},{3,5},{4,6},{5,7},{6,0},{7,1},{8,10},{9,11},{10,... | collective-permute-start | bytes 344072 | tf_op jit(solution)/shard_map/ppermute | solution.py:57
  76.7 2.1 %collective-permute-start.24 = (bf16[112,512]{1,0:T(8,128)(2,1)S(1)}, bf16[112,512]{1,0:T(8,128)(2,1)S(1)}, u32[]{:S(2)}, u32[]{:S(2)}) collective-permute-start(bf16[112,512]{1,0:T(8,128)(2,1)S(1)} %collective-permute-done.22.refs_3_), channel_id=1, source_target_pairs={{0,4},{1,5},{2,6},{3,7},{4,0},{5,1},{6,2},{7,3},{8,12},{9,13},{10,... | collective-permute-start | bytes 344072 | tf_op jit(solution)/shard_map/ppermute | solution.py:57
  80.3 1.5 %shard_map.90.refs_4_ = bf16[8,112,1024]{2,1,0:T(8,128)(2,1)} custom-call(bf16[112,512]{1,0:T(8,128)(2,1)S(1)} %collective-permute-done.26.refs_0_, bf16[112,512]{1,0:T(8,128)(2,1)S(1)} %collective-permute-done.27.refs_1_, bf16[112,512]{1,0:T(8,128)(2,1)S(1)} %collective-permute-done.28.refs_2_, ...), custom_call_target="tpu_custom_call", output_to_operand_aliasing={{}: (5, {})} | custom-call | tf_op jit(solution)/shard_map/pallas_call | solution.py:217
  81.9 1.1 %collective-permute-done.24.refs_1_ = bf16[112,512]{1,0:T(8,128)(2,1)S(1)} collective-permute-done((bf16[112,512]{1,0:T(8,128)(2,1)S(1)}, bf16[112,512]{1,0:T(8,128)(2,1)S(1)}, u32[]{:S(2)}, u32[]{:S(2)}) %collective-permute-start.24) | collective-permute-done | bytes 114720 | tf_op jit(solution)/shard_map/ppermute | solution.py:57
  83.6 1.3 %shard_map.91 = bf16[8,112,1024]{2,1,0:T(8,128)(2,1)} custom-call(bf16[112,512]{1,0:T(8,128)(2,1)S(1)} %collective-permute-done.23.refs_0_, bf16[112,512]{1,0:T(8,128)(2,1)S(1)} %collective-permute-done.24.refs_1_, bf16[112,512]{1,0:T(8,128)(2,1)S(1)} %collective-permute-done.25.refs_2_, ...), custom_call_target="tpu_custom_call", output_to_operand_aliasing={{}: (4, {})} | custom-call | tf_op jit(solution)/shard_map/pallas_call | solution.py:217
  (48 shorter events, 11.0 us)
Async XLA Ops:
  2.6 8.7 %collective-permute-start = (bf16[128,512]{1,0:T(8,128)(2,1)S(1)}, bf16[128,512]{1,0:T(8,128)(2,1)S(1)}, u32[]{:S(2)}, u32[]{:S(2)}) collective-permute-start(bf16[128,512]{1,0:T(8,128)(2,1)S(1)} %get-tuple-element.34), channel_id=1, source_target_pairs={{0,2},{1,3},{2,4},{3,5},{4,6},{5,7},{6,0},{7,1},{8,10},{9,11},{10,... | collective-permute-start | bytes 393224 | tf_op jit(solution)/shard_map/ppermute | solution.py:57
  4.2 7.2 %collective-permute-start.1 = (bf16[128,512]{1,0:T(8,128)(2,1)S(1)}, bf16[128,512]{1,0:T(8,128)(2,1)S(1)}, u32[]{:S(2)}, u32[]{:S(2)}) collective-permute-start(bf16[128,512]{1,0:T(8,128)(2,1)S(1)} %get-tuple-element.35), channel_id=1, source_target_pairs={{0,6},{1,7},{2,0},{3,1},{4,2},{5,3},{6,4},{7,5},{8,14},{9,15},{10,... | collective-permute-start | bytes 393224 | tf_op jit(solution)/shard_map/ppermute | solution.py:57
  6.0 7.0 %collective-permute-start.2 = (bf16[128,512]{1,0:T(8,128)(2,1)S(1)}, bf16[128,512]{1,0:T(8,128)(2,1)S(1)}, u32[]{:S(2)}, u32[]{:S(2)}) collective-permute-start(bf16[128,512]{1,0:T(8,128)(2,1)S(1)} %get-tuple-element.36), channel_id=1, source_target_pairs={{0,4},{1,5},{2,6},{3,7},{4,0},{5,1},{6,2},{7,3},{8,12},{9,13},{10,... | collective-permute-start | bytes 393224 | tf_op jit(solution)/shard_map/ppermute | solution.py:57
  10.8 24.9 %collective-permute-start.8 = (bf16[2,4,112,512]{3,2,1,0:T(8,128)(2,1)S(1)}, bf16[2,4,112,512]{3,2,1,0:T(8,128)(2,1)S(1)}, u32[]{:S(2)}, u32[]{:S(2)}) collective-permute-start(bf16[2,4,112,512]{3,2,1,0:T(8,128)(2,1)S(1)} %get-tuple-element.39), channel_id=1, source_target_pairs={{0,8},{8,0},{16,24},{24,16},{32,40},{40,32},{48,56},{56,48},{64,72... | collective-permute-start | bytes 2752520 | tf_op jit(solution)/shard_map/ppermute | solution.py:45
  10.9 24.8 %collective-permute-start.9 = (bf16[2,4,112,512]{3,2,1,0:T(8,128)(2,1)S(1)}, bf16[2,4,112,512]{3,2,1,0:T(8,128)(2,1)S(1)}, u32[]{:S(2)}, u32[]{:S(2)}) collective-permute-start(bf16[2,4,112,512]{3,2,1,0:T(8,128)(2,1)S(1)} %get-tuple-element.40), channel_id=1, source_target_pairs={{0,8},{8,0},{16,24},{24,16},{32,40},{40,32},{48,56},{56,48},{64,72... | collective-permute-start | bytes 2752520 | tf_op jit(solution)/shard_map/ppermute | solution.py:45
  13.0 12.0 %collective-permute-start.3 = (bf16[128,512]{1,0:T(8,128)(2,1)S(1)}, bf16[128,512]{1,0:T(8,128)(2,1)S(1)}, u32[]{:S(2)}, u32[]{:S(2)}) collective-permute-start(bf16[128,512]{1,0:T(8,128)(2,1)S(1)} %get-tuple-element.38), channel_id=1, source_target_pairs={{0,1},{1,0},{2,3},{3,2},{4,5},{5,4},{6,7},{7,6},{8,9},{9,8},{10,11... | collective-permute-start | bytes 393224 | tf_op jit(solution)/shard_map/ppermute | solution.py:61
  25.1 6.3 %collective-permute-start.4 = (bf16[128,512]{1,0:T(8,128)(2,1)S(1)}, bf16[128,512]{1,0:T(8,128)(2,1)S(1)}, u32[]{:S(2)}, u32[]{:S(2)}) collective-permute-start(bf16[128,512]{1,0:T(8,128)(2,1)S(1)} %shard_map.79.p0), channel_id=1, source_target_pairs={{0,2},{1,3},{2,4},{3,5},{4,6},{5,7},{6,0},{7,1},{8,10},{9,11},{10,... | collective-permute-start | bytes 393224 | tf_op jit(solution)/shard_map/ppermute | solution.py:57
  25.2 7.5 %collective-permute-start.5 = (bf16[128,512]{1,0:T(8,128)(2,1)S(1)}, bf16[128,512]{1,0:T(8,128)(2,1)S(1)}, u32[]{:S(2)}, u32[]{:S(2)}) collective-permute-start(bf16[128,512]{1,0:T(8,128)(2,1)S(1)} %shard_map.79.p0), channel_id=1, source_target_pairs={{0,4},{1,5},{2,6},{3,7},{4,0},{5,1},{6,2},{7,3},{8,12},{9,13},{10,... | collective-permute-start | bytes 393224 | tf_op jit(solution)/shard_map/ppermute | solution.py:57
  28.3 5.3 %collective-permute-start.6 = (bf16[128,512]{1,0:T(8,128)(2,1)S(1)}, bf16[128,512]{1,0:T(8,128)(2,1)S(1)}, u32[]{:S(2)}, u32[]{:S(2)}) collective-permute-start(bf16[128,512]{1,0:T(8,128)(2,1)S(1)} %shard_map.79.p0), channel_id=1, source_target_pairs={{0,6},{1,7},{2,0},{3,1},{4,2},{5,3},{6,4},{7,5},{8,14},{9,15},{10,... | collective-permute-start | bytes 393224 | tf_op jit(solution)/shard_map/ppermute | solution.py:57
  33.7 2.0 %collective-permute-start.7 = (bf16[512,512]{1,0:T(8,128)(2,1)S(1)}, bf16[512,512]{1,0:T(8,128)(2,1)S(1)}, u32[]{:S(2)}, u32[]{:S(2)}) collective-permute-start(bf16[512,512]{1,0:T(8,128)(2,1)S(1)} %pad_maximum_fusion), channel_id=1, source_target_pairs={{0,8},{8,0},{16,24},{24,16},{32,40},{40,32},{48,56},{56,48},{64,72... | collective-permute-start | bytes 1572872 | tf_op jit(solution)/shard_map/ppermute | solution.py:45
  36.1 20.1 %collective-permute-start.18 = (bf16[448,512]{1,0:T(8,128)(2,1)S(1)}, bf16[448,512]{1,0:T(8,128)(2,1)S(1)}, u32[]{:S(2)}, u32[]{:S(2)}) collective-permute-start(bf16[448,512]{1,0:T(8,128)(2,1)S(1)} %shard_map.86), channel_id=1, source_target_pairs={{0,16},{8,24},{16,0},{24,8},{32,48},{40,56},{48,32},{56,40},{64,80... | collective-permute-start | bytes 1376264 | tf_op jit(solution)/shard_map/ppermute | solution.py:53
  36.7 7.1 %collective-permute-start.10 = (bf16[112,512]{1,0:T(8,128)(2,1)S(1)}, bf16[112,512]{1,0:T(8,128)(2,1)S(1)}, u32[]{:S(2)}, u32[]{:S(2)}) collective-permute-start(bf16[112,512]{1,0:T(8,128)(2,1)S(1)} %get-tuple-element.42), channel_id=1, source_target_pairs={{0,64},{8,72},{16,80},{24,88},{32,96},{40,104},{48,112},{56,120},{... | collective-permute-start | bytes 344072 | tf_op jit(solution)/shard_map/ppermute | solution.py:49
  38.4 9.3 %collective-permute-start.11 = (bf16[112,512]{1,0:T(8,128)(2,1)S(1)}, bf16[112,512]{1,0:T(8,128)(2,1)S(1)}, u32[]{:S(2)}, u32[]{:S(2)}) collective-permute-start(bf16[112,512]{1,0:T(8,128)(2,1)S(1)} %get-tuple-element.43), channel_id=1, source_target_pairs={{0,128},{8,136},{16,144},{24,152},{32,160},{40,168},{48,176},{56,1... | collective-permute-start | bytes 344072 | tf_op jit(solution)/shard_map/ppermute | solution.py:49
  41.3 6.9 %collective-permute-start.12 = (bf16[112,512]{1,0:T(8,128)(2,1)S(1)}, bf16[112,512]{1,0:T(8,128)(2,1)S(1)}, u32[]{:S(2)}, u32[]{:S(2)}) collective-permute-start(bf16[112,512]{1,0:T(8,128)(2,1)S(1)} %get-tuple-element.44), channel_id=1, source_target_pairs={{0,192},{8,200},{16,208},{24,216},{32,224},{40,232},{48,240},{56,2... | collective-permute-start | bytes 344072 | tf_op jit(solution)/shard_map/ppermute | solution.py:49
  43.1 7.4 %collective-permute-start.14 = (bf16[112,512]{1,0:T(8,128)(2,1)S(1)}, bf16[112,512]{1,0:T(8,128)(2,1)S(1)}, u32[]{:S(2)}, u32[]{:S(2)}) collective-permute-start(bf16[112,512]{1,0:T(8,128)(2,1)S(1)} %get-tuple-element.46), channel_id=1, source_target_pairs={{0,64},{8,72},{16,80},{24,88},{32,96},{40,104},{48,112},{56,120},{... | collective-permute-start | bytes 344072 | tf_op jit(solution)/shard_map/ppermute | solution.py:49
  43.8 8.1 %collective-permute-start.15 = (bf16[112,512]{1,0:T(8,128)(2,1)S(1)}, bf16[112,512]{1,0:T(8,128)(2,1)S(1)}, u32[]{:S(2)}, u32[]{:S(2)}) collective-permute-start(bf16[112,512]{1,0:T(8,128)(2,1)S(1)} %get-tuple-element.47), channel_id=1, source_target_pairs={{0,128},{8,136},{16,144},{24,152},{32,160},{40,168},{48,176},{56,1... | collective-permute-start | bytes 344072 | tf_op jit(solution)/shard_map/ppermute | solution.py:49
  47.7 4.8 %collective-permute-start.16 = (bf16[112,512]{1,0:T(8,128)(2,1)S(1)}, bf16[112,512]{1,0:T(8,128)(2,1)S(1)}, u32[]{:S(2)}, u32[]{:S(2)}) collective-permute-start(bf16[112,512]{1,0:T(8,128)(2,1)S(1)} %get-tuple-element.48), channel_id=1, source_target_pairs={{0,192},{8,200},{16,208},{24,216},{32,224},{40,232},{48,240},{56,2... | collective-permute-start | bytes 344072 | tf_op jit(solution)/shard_map/ppermute | solution.py:49
  48.1 16.4 %copy-start = (f32[1,112,512]{2,1,0:T(8,128)S(1)}, f32[1,112,512]{2,1,0:T(8,128)}, u32[]{:S(2)}) copy-start(f32[1,112,512]{2,1,0:T(8,128)} %first.3) | copy-start | bytes 688132
  48.2 16.4 %copy-start.1 = (f32[1,112,512]{2,1,0:T(8,128)S(1)}, f32[1,112,512]{2,1,0:T(8,128)}, u32[]{:S(2)}) copy-start(f32[1,112,512]{2,1,0:T(8,128)} %second.3) | copy-start | bytes 688132
  48.2 12.4 %collective-permute-start.13 = (bf16[112,512]{1,0:T(8,128)(2,1)S(1)}, bf16[112,512]{1,0:T(8,128)(2,1)S(1)}, u32[]{:S(2)}, u32[]{:S(2)}) collective-permute-start(bf16[112,512]{1,0:T(8,128)(2,1)S(1)} %shard_map.82), channel_id=1, source_target_pairs={{0,48},{8,56},{16,32},{24,40},{32,16},{40,24},{48,0},{56,8},{64,11... | collective-permute-start | bytes 344072 | tf_op jit(solution)/shard_map/ppermute | solution.py:53
  52.5 8.1 %collective-permute-start.17 = (bf16[112,512]{1,0:T(8,128)(2,1)S(1)}, bf16[112,512]{1,0:T(8,128)(2,1)S(1)}, u32[]{:S(2)}, u32[]{:S(2)}) collective-permute-start(bf16[112,512]{1,0:T(8,128)(2,1)S(1)} %shard_map.84), channel_id=1, source_target_pairs={{0,32},{8,40},{16,48},{24,56},{32,0},{40,8},{48,16},{56,24},{64,96... | collective-permute-start | bytes 344072 | tf_op jit(solution)/shard_map/ppermute | solution.py:53
  56.3 6.1 %collective-permute-start.19 = (bf16[112,512]{1,0:T(8,128)(2,1)S(1)}, bf16[112,512]{1,0:T(8,128)(2,1)S(1)}, u32[]{:S(2)}, u32[]{:S(2)}) collective-permute-start(bf16[112,512]{1,0:T(8,128)(2,1)S(1)} %get-tuple-element.50), channel_id=1, source_target_pairs={{0,64},{8,72},{16,80},{24,88},{32,96},{40,104},{48,112},{56,120},{... | collective-permute-start | bytes 344072 | tf_op jit(solution)/shard_map/ppermute | solution.py:49
  56.9 6.9 %collective-permute-start.20 = (bf16[112,512]{1,0:T(8,128)(2,1)S(1)}, bf16[112,512]{1,0:T(8,128)(2,1)S(1)}, u32[]{:S(2)}, u32[]{:S(2)}) collective-permute-start(bf16[112,512]{1,0:T(8,128)(2,1)S(1)} %get-tuple-element.51), channel_id=1, source_target_pairs={{0,128},{8,136},{16,144},{24,152},{32,160},{40,168},{48,176},{56,1... | collective-permute-start | bytes 344072 | tf_op jit(solution)/shard_map/ppermute | solution.py:49
  59.8 4.8 %collective-permute-start.21 = (bf16[112,512]{1,0:T(8,128)(2,1)S(1)}, bf16[112,512]{1,0:T(8,128)(2,1)S(1)}, u32[]{:S(2)}, u32[]{:S(2)}) collective-permute-start(bf16[112,512]{1,0:T(8,128)(2,1)S(1)} %get-tuple-element.52), channel_id=1, source_target_pairs={{0,192},{8,200},{16,208},{24,216},{32,224},{40,232},{48,240},{56,2... | collective-permute-start | bytes 344072 | tf_op jit(solution)/shard_map/ppermute | solution.py:49
  64.8 10.0 %collective-permute-start.22 = (bf16[112,512]{1,0:T(8,128)(2,1)S(1)}, bf16[112,512]{1,0:T(8,128)(2,1)S(1)}, u32[]{:S(2)}, u32[]{:S(2)}) collective-permute-start(bf16[112,512]{1,0:T(8,128)(2,1)S(1)} %get-tuple-element.53.refs_0_), channel_id=1, source_target_pairs={{0,1},{1,0},{2,3},{3,2},{4,5},{5,4},{6,7},{7,6},{8,9},{9,8},{10,11... | collective-permute-start | bytes 344072 | tf_op jit(solution)/shard_map/ppermute | solution.py:61
  69.6 9.2 %collective-permute-start.26 = (bf16[112,512]{1,0:T(8,128)(2,1)S(1)}, bf16[112,512]{1,0:T(8,128)(2,1)S(1)}, u32[]{:S(2)}, u32[]{:S(2)}) collective-permute-start(bf16[112,512]{1,0:T(8,128)(2,1)S(1)} %get-tuple-element.53.refs_0_), channel_id=1, source_target_pairs={{0,2},{1,3},{2,4},{3,5},{4,6},{5,7},{6,0},{7,1},{8,10},{9,11},{10,... | collective-permute-start | bytes 344072 | tf_op jit(solution)/shard_map/ppermute | solution.py:57
  70.0 10.4 %collective-permute-start.27 = (bf16[112,512]{1,0:T(8,128)(2,1)S(1)}, bf16[112,512]{1,0:T(8,128)(2,1)S(1)}, u32[]{:S(2)}, u32[]{:S(2)}) collective-permute-start(bf16[112,512]{1,0:T(8,128)(2,1)S(1)} %get-tuple-element.53.refs_0_), channel_id=1, source_target_pairs={{0,4},{1,5},{2,6},{3,7},{4,0},{5,1},{6,2},{7,3},{8,12},{9,13},{10,... | collective-permute-start | bytes 344072 | tf_op jit(solution)/shard_map/ppermute | solution.py:57
  73.5 6.8 %collective-permute-start.28 = (bf16[112,512]{1,0:T(8,128)(2,1)S(1)}, bf16[112,512]{1,0:T(8,128)(2,1)S(1)}, u32[]{:S(2)}, u32[]{:S(2)}) collective-permute-start(bf16[112,512]{1,0:T(8,128)(2,1)S(1)} %get-tuple-element.53.refs_0_), channel_id=1, source_target_pairs={{0,6},{1,7},{2,0},{3,1},{4,2},{5,3},{6,4},{7,5},{8,14},{9,15},{10,... | collective-permute-start | bytes 344072 | tf_op jit(solution)/shard_map/ppermute | solution.py:57
  74.8 7.0 %collective-permute-start.23 = (bf16[112,512]{1,0:T(8,128)(2,1)S(1)}, bf16[112,512]{1,0:T(8,128)(2,1)S(1)}, u32[]{:S(2)}, u32[]{:S(2)}) collective-permute-start(bf16[112,512]{1,0:T(8,128)(2,1)S(1)} %collective-permute-done.22.refs_3_), channel_id=1, source_target_pairs={{0,2},{1,3},{2,4},{3,5},{4,6},{5,7},{6,0},{7,1},{8,10},{9,11},{10,... | collective-permute-start | bytes 344072 | tf_op jit(solution)/shard_map/ppermute | solution.py:57
  76.7 6.3 %collective-permute-start.24 = (bf16[112,512]{1,0:T(8,128)(2,1)S(1)}, bf16[112,512]{1,0:T(8,128)(2,1)S(1)}, u32[]{:S(2)}, u32[]{:S(2)}) collective-permute-start(bf16[112,512]{1,0:T(8,128)(2,1)S(1)} %collective-permute-done.22.refs_3_), channel_id=1, source_target_pairs={{0,4},{1,5},{2,6},{3,7},{4,0},{5,1},{6,2},{7,3},{8,12},{9,13},{10,... | collective-permute-start | bytes 344072 | tf_op jit(solution)/shard_map/ppermute | solution.py:57
  78.8 4.8 %collective-permute-start.25 = (bf16[112,512]{1,0:T(8,128)(2,1)S(1)}, bf16[112,512]{1,0:T(8,128)(2,1)S(1)}, u32[]{:S(2)}, u32[]{:S(2)}) collective-permute-start(bf16[112,512]{1,0:T(8,128)(2,1)S(1)} %collective-permute-done.22.refs_3_), channel_id=1, source_target_pairs={{0,6},{1,7},{2,0},{3,1},{4,2},{5,3},{6,4},{7,5},{8,14},{9,15},{10,... | collective-permute-start | bytes 344072 | tf_op jit(solution)/shard_map/ppermute | solution.py:57

commit v5 on v4

--- a/solution.py
+++ b/solution.py
@@ -163,7 +163,13 @@
         out[ry * rows : (ry + 1) * rows, :] = t.astype(out.dtype)
 
 
-def sum_far_body(own, r1, r2, r3, out):
+def low_rest_body(rz, acc, q, *refs):
+    low_near_body(0, acc, q, *refs[: SPLIT + 1])
+    low_far_body(rz, acc, q, *refs[:SPLIT], *refs[SPLIT + 1 :])
+
+
+def sum_far_body(own, r1, r2, r3, *refs):
+    out = refs[-1]
     t = own[...] + r1[...].astype(f32) + r2[...].astype(f32) + r3[...].astype(f32)
     out[...] = t.astype(out.dtype)
 
@@ -175,7 +181,7 @@
         out[...] = (own[part, :] + near[part, :].astype(f32)).astype(out.dtype)
 
 
-def direction_body(z3, z2, own, y1, y2, y3, first, second, grad, direction):
+def direction_body(z3, own, y1, y2, y3, z2, first, second, grad, direction):
     g = own[...] + y1[...].astype(f32) + y2[...].astype(f32) + y3[...].astype(f32)
     g = g + z2[...].astype(f32) + z3[...].astype(f32)
     grad[...] = g
@@ -196,14 +202,21 @@
     dirs, basis_t = refs[:n], refs[n]
     out, buf, sems = refs[n + 1 + aliased :]
     _, _, _, x, h = place()
+    rows, cols = buf.shape[1], buf.shape[2] // 2
+    cat = jnp.concatenate([d[...] for d in dirs], axis=0)
     copies = []
-    for i, (k, flip) in enumerate(moves):
-        t = galore_scale * jnp.dot(dirs[i][...], basis_t[...], preferred_element_type=f32)
-        buf[i] = t.astype(bf16)
-        block = lax.rem(x + NX - k, NX) * NH + (h ^ flip)
-        copy = pltpu.make_async_copy(buf.at[i], out.at[block], sems.at[i])
-        copy.start()
-        copies.append(copy)
+    for half in range(2):
+        part = slice(half * cols, (half + 1) * cols)
+        t = galore_scale * jnp.dot(cat, basis_t[:, part], preferred_element_type=f32)
+        for i, (k, flip) in enumerate(moves):
+            buf[i, :, part] = t[i * rows : (i + 1) * rows, :].astype(bf16)
+            block = lax.rem(x + NX - k, NX) * NH + (h ^ flip)
+            cut = pl.ds(half * cols, cols)
+            copy = pltpu.make_async_copy(
+                buf.at[i, :, cut], out.at[block, :, cut], sems.at[half * n + i]
+            )
+            copy.start()
+            copies.append(copy)
     for copy in copies:
         copy.wait()
 
@@ -218,7 +231,7 @@
         functools.partial(update_body, moves, aliased),
         [((NX * NH, rows, cols), bf16)],
         len(args),
-        scratch=[pltpu.VMEM((n, rows, cols), bf16), pltpu.SemaphoreType.DMA((n,))],
+        scratch=[pltpu.VMEM((n, rows, cols), bf16), pltpu.SemaphoreType.DMA((2 * n,))],
         in_specs=[VMEM] * (n + 1) + [ANY] * aliased,
         out_specs=[ANY],
         input_output_aliases={n + 1: 0} if aliased else {},
@@ -284,19 +297,19 @@
 
     own3, *far3 = low_far(3)
     far3 = over_y(*far3)
-    def low_near(rz, dtype):
-        return call(functools.partial(low_near_body, rz), [(four, dtype)], 2 + SPLIT)(acc, q, *other)[0]
-
-    send = to_z(low_near(1, bf16), 1)
-    near = low_near(0, f32)
-    own2, *far2 = low_far(2)
+    send = call(functools.partial(low_near_body, 1), [(four, bf16)], 2 + SPLIT)(acc, q, *other)[0]
+    send = to_z(send, 1)
+    near, own2, *far2 = call(
+        functools.partial(low_rest_body, 2), [(four, f32), (one, f32)] + [(one, bf16)] * 3, 2 + SPLIT
+    )(acc, q, *other)
     far2 = over_y(*far2)
     z3 = to_z(call(sum_far_body, [(one, bf16)], 4)(own3, *far3)[0], 3)
-    z2 = to_z(call(sum_far_body, [(one, bf16)], 4)(own2, *far2)[0], 2)
+    z2 = call(sum_far_body, [(one, bf16)], 5, in_specs=[VMEM] * 4 + [ANY])(own2, *far2, send)[0]
+    z2 = to_z(z2, 2)
     own, y1, y2, y3 = call(sum_near_body, [(one, f32)] + [(one, bf16)] * 3, 2)(near, send)
     y1, y2, y3 = over_y(y1, y2, y3)
     grad, d0 = call(direction_body, [(one, f32), (one, bf16)], 8)(
-        z3, z2, own, y1, y2, y3, first_moment, second_moment
+        z3, own, y1, y2, y3, z2, first_moment, second_moment
     )
     e0 = to_h(d0)
     d2, d1, d3 = to_x(d0, 2), to_x(d0, 1), to_x(d0, 3)

time: 85.2 us -> 84.9 us (level)
  the two profiles are of different devices: /device:TPU:32 before, /device:TPU:6 now
where the time goes in v5:
time: 84.9 us; the launch traced here: 84.8 us
  starting transfers between devices  45.1 us (53%)
  waiting for transfers between devices  26 us (31%)
  Pallas kernels  12.7 us (15%)
  between operations  0.95 us (1%)
    ppermute x12, starting transfers between devices, to_x(): return lax.ppermute(a, 'shard', shard_perm(lambda x, h: (x + k, h)))  14.3 us
    ppermute x12, waiting for transfers between devices, to_x(): return lax.ppermute(a, 'shard', shard_perm(lambda x, h: (x + k, h)))  13 us
    ppermute x9, starting transfers between devices, to_y(): return lax.ppermute(a, 'dp', dp_perm(lambda y, z, c: (y + k, z, c)))  12.8 us
    ppermute x2, starting transfers between devices, to_h(): return lax.ppermute(a, 'shard', shard_perm(lambda x, h: (x, 1 - h)))  11.7 us
    ppermute x3, starting transfers between devices, to_z(): return lax.ppermute(a, 'dp', dp_perm(lambda y, z, c: (y, z ^ k, c)))  5.71 us
    ppermute x9, waiting for transfers between devices, to_y(): return lax.ppermute(a, 'dp', dp_perm(lambda y, z, c: (y + k, z, c)))  5.29 us
    ppermute x2, waiting for transfers between devices, to_h(): return lax.ppermute(a, 'shard', shard_perm(lambda x, h: (x, 1 - h)))  4.18 us
    pallas_call x3, Pallas kernels, update_part(): call(functools.partial(update_body, moves, aliased), [((NX * NH, rows, co...  3.6 us
  transfers between devices with their start and end apart: 29, of which 13 were waited for; matrix products, arithmetic and copies ran while one was open for 0% of the time, Pallas kernels for 10%

profile of v5, /device:TPU:6, one launch (start us, length us, event | category | flops | bytes accessed | tf_op | source)
XLA Modules:
  0.0 84.8 jit_solution(14497591755469690079)
XLA Ops:
  0.6 2.0 %shard_map.76 = (f32[128,512]{1,0:T(8,128)S(1)}, bf16[128,512]{1,0:T(8,128)(2,1)S(1)}, bf16[128,512]{1,0:T(8,128)(2,1)S(1)}, bf16[128,512]{1,0:T(8,128)(2,1)S(1)}) custom-call(bf16[512,1024]{1,0:T(8,128)(2,1)} %feat.1, bf16[1024,512]{1,0:T(8,128)(2,1)} %basis.3), custom_call_target="tpu_custom_call" | custom-call | tf_op jit(solution)/shard_map/pallas_call | solution.py:250
  2.7 2.3 %collective-permute-start = (bf16[128,512]{1,0:T(8,128)(2,1)S(1)}, bf16[128,512]{1,0:T(8,128)(2,1)S(1)}, u32[]{:S(2)}, u32[]{:S(2)}) collective-permute-start(bf16[128,512]{1,0:T(8,128)(2,1)S(1)} %get-tuple-element.35), channel_id=1, source_target_pairs={{0,2},{1,3},{2,4},{3,5},{4,6},{5,7},{6,0},{7,1},{8,10},{9,11},{10,... | collective-permute-start | bytes 393224 | tf_op jit(solution)/shard_map/ppermute | solution.py:57
  5.0 1.6 %collective-permute-start.2 = (bf16[128,512]{1,0:T(8,128)(2,1)S(1)}, bf16[128,512]{1,0:T(8,128)(2,1)S(1)}, u32[]{:S(2)}, u32[]{:S(2)}) collective-permute-start(bf16[128,512]{1,0:T(8,128)(2,1)S(1)} %get-tuple-element.37), channel_id=1, source_target_pairs={{0,4},{1,5},{2,6},{3,7},{4,0},{5,1},{6,2},{7,3},{8,12},{9,13},{10,... | collective-permute-start | bytes 393224 | tf_op jit(solution)/shard_map/ppermute | solution.py:57
  6.5 3.0 %shard_map.77 = (bf16[4,4,112,512]{3,2,1,0:T(8,128)(2,1)S(1)}, bf16[2,4,112,512]{3,2,1,0:T(8,128)(2,1)S(1)}, bf16[2,4,112,512]{3,2,1,0:T(8,128)(2,1)S(1)}, bf16[512,1024]{1,0:T(8,128)(2,1)S(1)}) custom-call(bf16[512,3584]{1,0:T(8,128)(2,1)} %grads.1, bf16[1024,512]{1,0:T(8,128)(2,1)} %basis.3, f32[128,512]{1,0:T(8,128)S(1)} %get-tuple-element.33._.own), custom_call_target="tpu_custom_call" | custom-call | tf_op jit(solution)/shard_map/pallas_call | solution.py:267
  10.1 3.0 %collective-permute-done.1.r2 = bf16[128,512]{1,0:T(8,128)(2,1)S(1)} collective-permute-done((bf16[128,512]{1,0:T(8,128)(2,1)S(1)}, bf16[128,512]{1,0:T(8,128)(2,1)S(1)}, u32[]{:S(2)}, u32[]{:S(2)}) %collective-permute-start.1) | collective-permute-done | bytes 131104 | tf_op jit(solution)/shard_map/ppermute | solution.py:57
  13.2 6.3 %collective-permute-start.3 = (bf16[128,512]{1,0:T(8,128)(2,1)S(1)}, bf16[128,512]{1,0:T(8,128)(2,1)S(1)}, u32[]{:S(2)}, u32[]{:S(2)}) collective-permute-start(bf16[128,512]{1,0:T(8,128)(2,1)S(1)} %get-tuple-element.39), channel_id=1, source_target_pairs={{0,1},{1,0},{2,3},{3,2},{4,5},{5,4},{6,7},{7,6},{8,9},{9,8},{10,11... | collective-permute-start | bytes 393224 | tf_op jit(solution)/shard_map/ppermute | solution.py:61
  19.5 4.2 %collective-permute-done.3.other = bf16[128,512]{1,0:T(8,128)(2,1)S(1)} collective-permute-done((bf16[128,512]{1,0:T(8,128)(2,1)S(1)}, bf16[128,512]{1,0:T(8,128)(2,1)S(1)}, u32[]{:S(2)}, u32[]{:S(2)}) %collective-permute-start.3) | collective-permute-done | bytes 131104 | tf_op jit(solution)/shard_map/ppermute | solution.py:61
  23.7 1.7 %collective-permute-start.4 = (bf16[128,512]{1,0:T(8,128)(2,1)S(1)}, bf16[128,512]{1,0:T(8,128)(2,1)S(1)}, u32[]{:S(2)}, u32[]{:S(2)}) collective-permute-start(bf16[128,512]{1,0:T(8,128)(2,1)S(1)} %shard_map.79.p0), channel_id=1, source_target_pairs={{0,2},{1,3},{2,4},{3,5},{4,6},{5,7},{6,0},{7,1},{8,10},{9,11},{10,... | collective-permute-start | bytes 393224 | tf_op jit(solution)/shard_map/ppermute | solution.py:57
  26.5 2.3 %collective-permute-done.4.p1 = bf16[128,512]{1,0:T(8,128)(2,1)S(1)} collective-permute-done((bf16[128,512]{1,0:T(8,128)(2,1)S(1)}, bf16[128,512]{1,0:T(8,128)(2,1)S(1)}, u32[]{:S(2)}, u32[]{:S(2)}) %collective-permute-start.4) | collective-permute-done | bytes 131104 | tf_op jit(solution)/shard_map/ppermute | solution.py:57
  28.8 3.3 %collective-permute-done.5.p2 = bf16[128,512]{1,0:T(8,128)(2,1)S(1)} collective-permute-done((bf16[128,512]{1,0:T(8,128)(2,1)S(1)}, bf16[128,512]{1,0:T(8,128)(2,1)S(1)}, u32[]{:S(2)}, u32[]{:S(2)}) %collective-permute-start.5) | collective-permute-done | bytes 131104 | tf_op jit(solution)/shard_map/ppermute | solution.py:57
  32.0 1.3 %collective-permute-done.6.p3 = bf16[128,512]{1,0:T(8,128)(2,1)S(1)} collective-permute-done((bf16[128,512]{1,0:T(8,128)(2,1)S(1)}, bf16[128,512]{1,0:T(8,128)(2,1)S(1)}, u32[]{:S(2)}, u32[]{:S(2)}) %collective-permute-start.6) | collective-permute-done | bytes 131104 | tf_op jit(solution)/shard_map/ppermute | solution.py:57
  33.5 1.1 %shard_map.80.acc = f32[4,448,512]{2,1,0:T(8,128)S(1)} custom-call(bf16[4,4,112,512]{3,2,1,0:T(8,128)(2,1)S(1)} %get-tuple-element.34.keep, bf16[128,512]{1,0:T(8,128)(2,1)S(1)} %shard_map.79.p0, bf16[128,512]{1,0:T(8,128)(2,1)S(1)} %collective-permute-done.4.p1, bf16[128,512]{1,0:T(8,128)(2,1)S(1)} %collective-permute-done.5.p2, ...), custom_call_target="tpu_custom_call" | custom-call | tf_op jit(solution)/shard_map/pallas_call | solution.py:286
  35.9 2.2 %collective-permute-start.14 = (bf16[448,512]{1,0:T(8,128)(2,1)S(1)}, bf16[448,512]{1,0:T(8,128)(2,1)S(1)}, u32[]{:S(2)}, u32[]{:S(2)}) collective-permute-start(bf16[448,512]{1,0:T(8,128)(2,1)S(1)} %shard_map.84), channel_id=1, source_target_pairs={{0,16},{8,24},{16,0},{24,8},{32,48},{40,56},{48,32},{56,40},{64,80... | collective-permute-start | bytes 1376264 | tf_op jit(solution)/shard_map/ppermute | solution.py:53
  38.5 1.7 %collective-permute-start.10 = (bf16[112,512]{1,0:T(8,128)(2,1)S(1)}, bf16[112,512]{1,0:T(8,128)(2,1)S(1)}, u32[]{:S(2)}, u32[]{:S(2)}) collective-permute-start(bf16[112,512]{1,0:T(8,128)(2,1)S(1)} %get-tuple-element.43), channel_id=1, source_target_pairs={{0,64},{8,72},{16,80},{24,88},{32,96},{40,104},{48,112},{56,120},{... | collective-permute-start | bytes 344072 | tf_op jit(solution)/shard_map/ppermute | solution.py:49
  40.2 2.9 %collective-permute-start.11 = (bf16[112,512]{1,0:T(8,128)(2,1)S(1)}, bf16[112,512]{1,0:T(8,128)(2,1)S(1)}, u32[]{:S(2)}, u32[]{:S(2)}) collective-permute-start(bf16[112,512]{1,0:T(8,128)(2,1)S(1)} %get-tuple-element.44), channel_id=1, source_target_pairs={{0,128},{8,136},{16,144},{24,152},{32,160},{40,168},{48,176},{56,1... | collective-permute-start | bytes 344072 | tf_op jit(solution)/shard_map/ppermute | solution.py:49
  43.1 1.3 %collective-permute-start.12 = (bf16[112,512]{1,0:T(8,128)(2,1)S(1)}, bf16[112,512]{1,0:T(8,128)(2,1)S(1)}, u32[]{:S(2)}, u32[]{:S(2)}) collective-permute-start(bf16[112,512]{1,0:T(8,128)(2,1)S(1)} %get-tuple-element.45), channel_id=1, source_target_pairs={{0,192},{8,200},{16,208},{24,216},{32,224},{40,232},{48,240},{56,2... | collective-permute-start | bytes 344072 | tf_op jit(solution)/shard_map/ppermute | solution.py:49
  46.8 2.8 %collective-permute-done.11.r2 = bf16[112,512]{1,0:T(8,128)(2,1)S(1)} collective-permute-done((bf16[112,512]{1,0:T(8,128)(2,1)S(1)}, bf16[112,512]{1,0:T(8,128)(2,1)S(1)}, u32[]{:S(2)}, u32[]{:S(2)}) %collective-permute-start.11) | collective-permute-done | bytes 114720 | tf_op jit(solution)/shard_map/ppermute | solution.py:49
  49.6 3.0 %collective-permute-start.13 = (bf16[112,512]{1,0:T(8,128)(2,1)S(1)}, bf16[112,512]{1,0:T(8,128)(2,1)S(1)}, u32[]{:S(2)}, u32[]{:S(2)}) collective-permute-start(bf16[112,512]{1,0:T(8,128)(2,1)S(1)} %shard_map.82), channel_id=1, source_target_pairs={{0,48},{8,56},{16,32},{24,40},{32,16},{40,24},{48,0},{56,8},{64,11... | collective-permute-start | bytes 344072 | tf_op jit(solution)/shard_map/ppermute | solution.py:53
  52.7 2.1 %collective-permute-start.15 = (bf16[112,512]{1,0:T(8,128)(2,1)S(1)}, bf16[112,512]{1,0:T(8,128)(2,1)S(1)}, u32[]{:S(2)}, u32[]{:S(2)}) collective-permute-start(bf16[112,512]{1,0:T(8,128)(2,1)S(1)} %get-tuple-element.48), channel_id=1, source_target_pairs={{0,64},{8,72},{16,80},{24,88},{32,96},{40,104},{48,112},{56,120},{... | collective-permute-start | bytes 344072 | tf_op jit(solution)/shard_map/ppermute | solution.py:49
  55.4 2.5 %collective-permute-start.17 = (bf16[112,512]{1,0:T(8,128)(2,1)S(1)}, bf16[112,512]{1,0:T(8,128)(2,1)S(1)}, u32[]{:S(2)}, u32[]{:S(2)}) collective-permute-start(bf16[112,512]{1,0:T(8,128)(2,1)S(1)} %get-tuple-element.50), channel_id=1, source_target_pairs={{0,192},{8,200},{16,208},{24,216},{32,224},{40,232},{48,240},{56,2... | collective-permute-start | bytes 344072 | tf_op jit(solution)/shard_map/ppermute | solution.py:49
  58.7 2.3 %collective-permute-done.16.y2 = bf16[112,512]{1,0:T(8,128)(2,1)S(1)} collective-permute-done((bf16[112,512]{1,0:T(8,128)(2,1)S(1)}, bf16[112,512]{1,0:T(8,128)(2,1)S(1)}, u32[]{:S(2)}, u32[]{:S(2)}) %collective-permute-start.16) | collective-permute-done | bytes 114720 | tf_op jit(solution)/shard_map/ppermute | solution.py:49
  61.1 2.8 %collective-permute-done.21.z2 = bf16[112,512]{1,0:T(8,128)(2,1)S(1)} collective-permute-done((bf16[112,512]{1,0:T(8,128)(2,1)S(1)}, bf16[112,512]{1,0:T(8,128)(2,1)S(1)}, u32[]{:S(2)}, u32[]{:S(2)}) %collective-permute-start.21) | collective-permute-done | bytes 114720 | tf_op jit(solution)/shard_map/ppermute | solution.py:53
  64.1 5.3 %collective-permute-start.22 = (bf16[112,512]{1,0:T(8,128)(2,1)S(1)}, bf16[112,512]{1,0:T(8,128)(2,1)S(1)}, u32[]{:S(2)}, u32[]{:S(2)}) collective-permute-start(bf16[112,512]{1,0:T(8,128)(2,1)S(1)} %get-tuple-element.55.refs_0_), channel_id=1, source_target_pairs={{0,1},{1,0},{2,3},{3,2},{4,5},{5,4},{6,7},{7,6},{8,9},{9,8},{10,11... | collective-permute-start | bytes 344072 | tf_op jit(solution)/shard_map/ppermute | solution.py:61
  70.0 1.6 %collective-permute-start.27 = (bf16[112,512]{1,0:T(8,128)(2,1)S(1)}, bf16[112,512]{1,0:T(8,128)(2,1)S(1)}, u32[]{:S(2)}, u32[]{:S(2)}) collective-permute-start(bf16[112,512]{1,0:T(8,128)(2,1)S(1)} %get-tuple-element.55.refs_0_), channel_id=1, source_target_pairs={{0,4},{1,5},{2,6},{3,7},{4,0},{5,1},{6,2},{7,3},{8,12},{9,13},{10,... | collective-permute-start | bytes 344072 | tf_op jit(solution)/shard_map/ppermute | solution.py:57
  71.6 1.1 %collective-permute-start.28 = (bf16[112,512]{1,0:T(8,128)(2,1)S(1)}, bf16[112,512]{1,0:T(8,128)(2,1)S(1)}, u32[]{:S(2)}, u32[]{:S(2)}) collective-permute-start(bf16[112,512]{1,0:T(8,128)(2,1)S(1)} %get-tuple-element.55.refs_0_), channel_id=1, source_target_pairs={{0,6},{1,7},{2,0},{3,1},{4,2},{5,3},{6,4},{7,5},{8,14},{9,15},{10,... | collective-permute-start | bytes 344072 | tf_op jit(solution)/shard_map/ppermute | solution.py:57
  72.7 1.0 %shard_map.88.refs_5_ = bf16[8,112,1024]{2,1,0:T(8,128)(2,1)} custom-call(bf16[112,512]{1,0:T(8,128)(2,1)S(1)} %get-tuple-element.55.refs_0_, bf16[512,1024]{1,0:T(8,128)(2,1)S(1)} %get-tuple-element.56.refs_1_.refs_4_.refs_3_), custom_call_target="tpu_custom_call" | custom-call | tf_op jit(solution)/shard_map/pallas_call | solution.py:230
  73.7 2.2 %collective-permute-start.23 = (bf16[112,512]{1,0:T(8,128)(2,1)S(1)}, bf16[112,512]{1,0:T(8,128)(2,1)S(1)}, u32[]{:S(2)}, u32[]{:S(2)}) collective-permute-start(bf16[112,512]{1,0:T(8,128)(2,1)S(1)} %collective-permute-done.22.refs_3_), channel_id=1, source_target_pairs={{0,2},{1,3},{2,4},{3,5},{4,6},{5,7},{6,0},{7,1},{8,10},{9,11},{10,... | collective-permute-start | bytes 344072 | tf_op jit(solution)/shard_map/ppermute | solution.py:57
  76.8 1.3 %collective-permute-start.25 = (bf16[112,512]{1,0:T(8,128)(2,1)S(1)}, bf16[112,512]{1,0:T(8,128)(2,1)S(1)}, u32[]{:S(2)}, u32[]{:S(2)}) collective-permute-start(bf16[112,512]{1,0:T(8,128)(2,1)S(1)} %collective-permute-done.22.refs_3_), channel_id=1, source_target_pairs={{0,6},{1,7},{2,0},{3,1},{4,2},{5,3},{6,4},{7,5},{8,14},{9,15},{10,... | collective-permute-start | bytes 344072 | tf_op jit(solution)/shard_map/ppermute | solution.py:57
  79.6 1.4 %shard_map.89.refs_4_ = bf16[8,112,1024]{2,1,0:T(8,128)(2,1)} custom-call(bf16[112,512]{1,0:T(8,128)(2,1)S(1)} %collective-permute-done.26.refs_0_, bf16[112,512]{1,0:T(8,128)(2,1)S(1)} %collective-permute-done.27.refs_1_, bf16[112,512]{1,0:T(8,128)(2,1)S(1)} %collective-permute-done.28.refs_2_, ...), custom_call_target="tpu_custom_call", output_to_operand_aliasing={{}: (5, {})} | custom-call | tf_op jit(solution)/shard_map/pallas_call | solution.py:230
  81.0 1.3 %collective-permute-done.24.refs_1_ = bf16[112,512]{1,0:T(8,128)(2,1)S(1)} collective-permute-done((bf16[112,512]{1,0:T(8,128)(2,1)S(1)}, bf16[112,512]{1,0:T(8,128)(2,1)S(1)}, u32[]{:S(2)}, u32[]{:S(2)}) %collective-permute-start.24) | collective-permute-done | bytes 114720 | tf_op jit(solution)/shard_map/ppermute | solution.py:57
  82.3 1.2 %collective-permute-done.25.refs_2_ = bf16[112,512]{1,0:T(8,128)(2,1)S(1)} collective-permute-done((bf16[112,512]{1,0:T(8,128)(2,1)S(1)}, bf16[112,512]{1,0:T(8,128)(2,1)S(1)}, u32[]{:S(2)}, u32[]{:S(2)}) %collective-permute-start.25) | collective-permute-done | bytes 114720 | tf_op jit(solution)/shard_map/ppermute | solution.py:57
  83.4 1.2 %shard_map.90 = bf16[8,112,1024]{2,1,0:T(8,128)(2,1)} custom-call(bf16[112,512]{1,0:T(8,128)(2,1)S(1)} %collective-permute-done.23.refs_0_, bf16[112,512]{1,0:T(8,128)(2,1)S(1)} %collective-permute-done.24.refs_1_, bf16[112,512]{1,0:T(8,128)(2,1)S(1)} %collective-permute-done.25.refs_2_, ...), custom_call_target="tpu_custom_call", output_to_operand_aliasing={{}: (4, {})} | custom-call | tf_op jit(solution)/shard_map/pallas_call | solution.py:230
  (47 shorter events, 10.6 us)
Async XLA Ops:
  2.7 7.4 %collective-permute-start = (bf16[128,512]{1,0:T(8,128)(2,1)S(1)}, bf16[128,512]{1,0:T(8,128)(2,1)S(1)}, u32[]{:S(2)}, u32[]{:S(2)}) collective-permute-start(bf16[128,512]{1,0:T(8,128)(2,1)S(1)} %get-tuple-element.35), channel_id=1, source_target_pairs={{0,2},{1,3},{2,4},{3,5},{4,6},{5,7},{6,0},{7,1},{8,10},{9,11},{10,... | collective-permute-start | bytes 393224 | tf_op jit(solution)/shard_map/ppermute | solution.py:57
  5.0 8.2 %collective-permute-start.1 = (bf16[128,512]{1,0:T(8,128)(2,1)S(1)}, bf16[128,512]{1,0:T(8,128)(2,1)S(1)}, u32[]{:S(2)}, u32[]{:S(2)}) collective-permute-start(bf16[128,512]{1,0:T(8,128)(2,1)S(1)} %get-tuple-element.36), channel_id=1, source_target_pairs={{0,6},{1,7},{2,0},{3,1},{4,2},{5,3},{6,4},{7,5},{8,14},{9,15},{10,... | collective-permute-start | bytes 393224 | tf_op jit(solution)/shard_map/ppermute | solution.py:57
  5.0 8.2 %collective-permute-start.2 = (bf16[128,512]{1,0:T(8,128)(2,1)S(1)}, bf16[128,512]{1,0:T(8,128)(2,1)S(1)}, u32[]{:S(2)}, u32[]{:S(2)}) collective-permute-start(bf16[128,512]{1,0:T(8,128)(2,1)S(1)} %get-tuple-element.37), channel_id=1, source_target_pairs={{0,4},{1,5},{2,6},{3,7},{4,0},{5,1},{6,2},{7,3},{8,12},{9,13},{10,... | collective-permute-start | bytes 393224 | tf_op jit(solution)/shard_map/ppermute | solution.py:57
  9.5 25.9 %collective-permute-start.8 = (bf16[2,4,112,512]{3,2,1,0:T(8,128)(2,1)S(1)}, bf16[2,4,112,512]{3,2,1,0:T(8,128)(2,1)S(1)}, u32[]{:S(2)}, u32[]{:S(2)}) collective-permute-start(bf16[2,4,112,512]{3,2,1,0:T(8,128)(2,1)S(1)} %get-tuple-element.40), channel_id=1, source_target_pairs={{0,8},{8,0},{16,24},{24,16},{32,40},{40,32},{48,56},{56,48},{64,72... | collective-permute-start | bytes 2752520 | tf_op jit(solution)/shard_map/ppermute | solution.py:45
  9.6 25.8 %collective-permute-start.9 = (bf16[2,4,112,512]{3,2,1,0:T(8,128)(2,1)S(1)}, bf16[2,4,112,512]{3,2,1,0:T(8,128)(2,1)S(1)}, u32[]{:S(2)}, u32[]{:S(2)}) collective-permute-start(bf16[2,4,112,512]{3,2,1,0:T(8,128)(2,1)S(1)} %get-tuple-element.41), channel_id=1, source_target_pairs={{0,8},{8,0},{16,24},{24,16},{32,40},{40,32},{48,56},{56,48},{64,72... | collective-permute-start | bytes 2752520 | tf_op jit(solution)/shard_map/ppermute | solution.py:45
  13.2 10.5 %collective-permute-start.3 = (bf16[128,512]{1,0:T(8,128)(2,1)S(1)}, bf16[128,512]{1,0:T(8,128)(2,1)S(1)}, u32[]{:S(2)}, u32[]{:S(2)}) collective-permute-start(bf16[128,512]{1,0:T(8,128)(2,1)S(1)} %get-tuple-element.39), channel_id=1, source_target_pairs={{0,1},{1,0},{2,3},{3,2},{4,5},{5,4},{6,7},{7,6},{8,9},{9,8},{10,11... | collective-permute-start | bytes 393224 | tf_op jit(solution)/shard_map/ppermute | solution.py:61
  23.7 5.0 %collective-permute-start.4 = (bf16[128,512]{1,0:T(8,128)(2,1)S(1)}, bf16[128,512]{1,0:T(8,128)(2,1)S(1)}, u32[]{:S(2)}, u32[]{:S(2)}) collective-permute-start(bf16[128,512]{1,0:T(8,128)(2,1)S(1)} %shard_map.79.p0), channel_id=1, source_target_pairs={{0,2},{1,3},{2,4},{3,5},{4,6},{5,7},{6,0},{7,1},{8,10},{9,11},{10,... | collective-permute-start | bytes 393224 | tf_op jit(solution)/shard_map/ppermute | solution.py:57
  25.5 6.6 %collective-permute-start.5 = (bf16[128,512]{1,0:T(8,128)(2,1)S(1)}, bf16[128,512]{1,0:T(8,128)(2,1)S(1)}, u32[]{:S(2)}, u32[]{:S(2)}) collective-permute-start(bf16[128,512]{1,0:T(8,128)(2,1)S(1)} %shard_map.79.p0), channel_id=1, source_target_pairs={{0,4},{1,5},{2,6},{3,7},{4,0},{5,1},{6,2},{7,3},{8,12},{9,13},{10,... | collective-permute-start | bytes 393224 | tf_op jit(solution)/shard_map/ppermute | solution.py:57
  25.9 7.4 %collective-permute-start.6 = (bf16[128,512]{1,0:T(8,128)(2,1)S(1)}, bf16[128,512]{1,0:T(8,128)(2,1)S(1)}, u32[]{:S(2)}, u32[]{:S(2)}) collective-permute-start(bf16[128,512]{1,0:T(8,128)(2,1)S(1)} %shard_map.79.p0), channel_id=1, source_target_pairs={{0,6},{1,7},{2,0},{3,1},{4,2},{5,3},{6,4},{7,5},{8,14},{9,15},{10,... | collective-permute-start | bytes 393224 | tf_op jit(solution)/shard_map/ppermute | solution.py:57
  33.4 2.0 %collective-permute-start.7 = (bf16[512,512]{1,0:T(8,128)(2,1)S(1)}, bf16[512,512]{1,0:T(8,128)(2,1)S(1)}, u32[]{:S(2)}, u32[]{:S(2)}) collective-permute-start(bf16[512,512]{1,0:T(8,128)(2,1)S(1)} %pad_maximum_fusion), channel_id=1, source_target_pairs={{0,8},{8,0},{16,24},{24,16},{32,40},{40,32},{48,56},{56,48},{64,72... | collective-permute-start | bytes 1572872 | tf_op jit(solution)/shard_map/ppermute | solution.py:45
  35.9 16.7 %collective-permute-start.14 = (bf16[448,512]{1,0:T(8,128)(2,1)S(1)}, bf16[448,512]{1,0:T(8,128)(2,1)S(1)}, u32[]{:S(2)}, u32[]{:S(2)}) collective-permute-start(bf16[448,512]{1,0:T(8,128)(2,1)S(1)} %shard_map.84), channel_id=1, source_target_pairs={{0,16},{8,24},{16,0},{24,8},{32,48},{40,56},{48,32},{56,40},{64,80... | collective-permute-start | bytes 1376264 | tf_op jit(solution)/shard_map/ppermute | solution.py:53
  38.5 7.5 %collective-permute-start.10 = (bf16[112,512]{1,0:T(8,128)(2,1)S(1)}, bf16[112,512]{1,0:T(8,128)(2,1)S(1)}, u32[]{:S(2)}, u32[]{:S(2)}) collective-permute-start(bf16[112,512]{1,0:T(8,128)(2,1)S(1)} %get-tuple-element.43), channel_id=1, source_target_pairs={{0,64},{8,72},{16,80},{24,88},{32,96},{40,104},{48,112},{56,120},{... | collective-permute-start | bytes 344072 | tf_op jit(solution)/shard_map/ppermute | solution.py:49
  40.2 9.4 %collective-permute-start.11 = (bf16[112,512]{1,0:T(8,128)(2,1)S(1)}, bf16[112,512]{1,0:T(8,128)(2,1)S(1)}, u32[]{:S(2)}, u32[]{:S(2)}) collective-permute-start(bf16[112,512]{1,0:T(8,128)(2,1)S(1)} %get-tuple-element.44), channel_id=1, source_target_pairs={{0,128},{8,136},{16,144},{24,152},{32,160},{40,168},{48,176},{56,1... | collective-permute-start | bytes 344072 | tf_op jit(solution)/shard_map/ppermute | solution.py:49
  43.1 6.5 %collective-permute-start.12 = (bf16[112,512]{1,0:T(8,128)(2,1)S(1)}, bf16[112,512]{1,0:T(8,128)(2,1)S(1)}, u32[]{:S(2)}, u32[]{:S(2)}) collective-permute-start(bf16[112,512]{1,0:T(8,128)(2,1)S(1)} %get-tuple-element.45), channel_id=1, source_target_pairs={{0,192},{8,200},{16,208},{24,216},{32,224},{40,232},{48,240},{56,2... | collective-permute-start | bytes 344072 | tf_op jit(solution)/shard_map/ppermute | solution.py:49
  45.2 18.7 %copy-start = (f32[1,112,512]{2,1,0:T(8,128)S(1)}, f32[1,112,512]{2,1,0:T(8,128)}, u32[]{:S(2)}) copy-start(f32[1,112,512]{2,1,0:T(8,128)} %first.3) | copy-start | bytes 688132
  45.2 18.6 %copy-start.1 = (f32[1,112,512]{2,1,0:T(8,128)S(1)}, f32[1,112,512]{2,1,0:T(8,128)}, u32[]{:S(2)}) copy-start(f32[1,112,512]{2,1,0:T(8,128)} %second.3) | copy-start | bytes 688132
  45.2 9.5 %collective-permute-start.18 = (bf16[112,512]{1,0:T(8,128)(2,1)S(1)}, bf16[112,512]{1,0:T(8,128)(2,1)S(1)}, u32[]{:S(2)}, u32[]{:S(2)}) collective-permute-start(bf16[112,512]{1,0:T(8,128)(2,1)S(1)} %get-tuple-element.52), channel_id=1, source_target_pairs={{0,64},{8,72},{16,80},{24,88},{32,96},{40,104},{48,112},{56,120},{... | collective-permute-start | bytes 344072 | tf_op jit(solution)/shard_map/ppermute | solution.py:49
  46.0 9.4 %collective-permute-start.19 = (bf16[112,512]{1,0:T(8,128)(2,1)S(1)}, bf16[112,512]{1,0:T(8,128)(2,1)S(1)}, u32[]{:S(2)}, u32[]{:S(2)}) collective-permute-start(bf16[112,512]{1,0:T(8,128)(2,1)S(1)} %get-tuple-element.53), channel_id=1, source_target_pairs={{0,128},{8,136},{16,144},{24,152},{32,160},{40,168},{48,176},{56,1... | collective-permute-start | bytes 344072 | tf_op jit(solution)/shard_map/ppermute | solution.py:49
  49.5 8.4 %collective-permute-start.20 = (bf16[112,512]{1,0:T(8,128)(2,1)S(1)}, bf16[112,512]{1,0:T(8,128)(2,1)S(1)}, u32[]{:S(2)}, u32[]{:S(2)}) collective-permute-start(bf16[112,512]{1,0:T(8,128)(2,1)S(1)} %get-tuple-element.54), channel_id=1, source_target_pairs={{0,192},{8,200},{16,208},{24,216},{32,224},{40,232},{48,240},{56,2... | collective-permute-start | bytes 344072 | tf_op jit(solution)/shard_map/ppermute | solution.py:49
  49.6 9.0 %collective-permute-start.13 = (bf16[112,512]{1,0:T(8,128)(2,1)S(1)}, bf16[112,512]{1,0:T(8,128)(2,1)S(1)}, u32[]{:S(2)}, u32[]{:S(2)}) collective-permute-start(bf16[112,512]{1,0:T(8,128)(2,1)S(1)} %shard_map.82), channel_id=1, source_target_pairs={{0,48},{8,56},{16,32},{24,40},{32,16},{40,24},{48,0},{56,8},{64,11... | collective-permute-start | bytes 344072 | tf_op jit(solution)/shard_map/ppermute | solution.py:53
  52.7 6.1 %collective-permute-start.15 = (bf16[112,512]{1,0:T(8,128)(2,1)S(1)}, bf16[112,512]{1,0:T(8,128)(2,1)S(1)}, u32[]{:S(2)}, u32[]{:S(2)}) collective-permute-start(bf16[112,512]{1,0:T(8,128)(2,1)S(1)} %get-tuple-element.48), channel_id=1, source_target_pairs={{0,64},{8,72},{16,80},{24,88},{32,96},{40,104},{48,112},{56,120},{... | collective-permute-start | bytes 344072 | tf_op jit(solution)/shard_map/ppermute | solution.py:49
  54.8 6.3 %collective-permute-start.16 = (bf16[112,512]{1,0:T(8,128)(2,1)S(1)}, bf16[112,512]{1,0:T(8,128)(2,1)S(1)}, u32[]{:S(2)}, u32[]{:S(2)}) collective-permute-start(bf16[112,512]{1,0:T(8,128)(2,1)S(1)} %get-tuple-element.49), channel_id=1, source_target_pairs={{0,128},{8,136},{16,144},{24,152},{32,160},{40,168},{48,176},{56,1... | collective-permute-start | bytes 344072 | tf_op jit(solution)/shard_map/ppermute | solution.py:49
  55.4 5.6 %collective-permute-start.17 = (bf16[112,512]{1,0:T(8,128)(2,1)S(1)}, bf16[112,512]{1,0:T(8,128)(2,1)S(1)}, u32[]{:S(2)}, u32[]{:S(2)}) collective-permute-start(bf16[112,512]{1,0:T(8,128)(2,1)S(1)} %get-tuple-element.50), channel_id=1, source_target_pairs={{0,192},{8,200},{16,208},{24,216},{32,224},{40,232},{48,240},{56,2... | collective-permute-start | bytes 344072 | tf_op jit(solution)/shard_map/ppermute | solution.py:49
  58.0 5.8 %collective-permute-start.21 = (bf16[112,512]{1,0:T(8,128)(2,1)S(1)}, bf16[112,512]{1,0:T(8,128)(2,1)S(1)}, u32[]{:S(2)}, u32[]{:S(2)}) collective-permute-start(bf16[112,512]{1,0:T(8,128)(2,1)S(1)} %shard_map.86), channel_id=1, source_target_pairs={{0,32},{8,40},{16,48},{24,56},{32,0},{40,8},{48,16},{56,24},{64,96... | collective-permute-start | bytes 344072 | tf_op jit(solution)/shard_map/ppermute | solution.py:53
  64.1 9.6 %collective-permute-start.22 = (bf16[112,512]{1,0:T(8,128)(2,1)S(1)}, bf16[112,512]{1,0:T(8,128)(2,1)S(1)}, u32[]{:S(2)}, u32[]{:S(2)}) collective-permute-start(bf16[112,512]{1,0:T(8,128)(2,1)S(1)} %get-tuple-element.55.refs_0_), channel_id=1, source_target_pairs={{0,1},{1,0},{2,3},{3,2},{4,5},{5,4},{6,7},{7,6},{8,9},{9,8},{10,11... | collective-permute-start | bytes 344072 | tf_op jit(solution)/shard_map/ppermute | solution.py:61
  69.4 7.3 %collective-permute-start.26 = (bf16[112,512]{1,0:T(8,128)(2,1)S(1)}, bf16[112,512]{1,0:T(8,128)(2,1)S(1)}, u32[]{:S(2)}, u32[]{:S(2)}) collective-permute-start(bf16[112,512]{1,0:T(8,128)(2,1)S(1)} %get-tuple-element.55.refs_0_), channel_id=1, source_target_pairs={{0,2},{1,3},{2,4},{3,5},{4,6},{5,7},{6,0},{7,1},{8,10},{9,11},{10,... | collective-permute-start | bytes 344072 | tf_op jit(solution)/shard_map/ppermute | solution.py:57
  70.0 8.9 %collective-permute-start.27 = (bf16[112,512]{1,0:T(8,128)(2,1)S(1)}, bf16[112,512]{1,0:T(8,128)(2,1)S(1)}, u32[]{:S(2)}, u32[]{:S(2)}) collective-permute-start(bf16[112,512]{1,0:T(8,128)(2,1)S(1)} %get-tuple-element.55.refs_0_), channel_id=1, source_target_pairs={{0,4},{1,5},{2,6},{3,7},{4,0},{5,1},{6,2},{7,3},{8,12},{9,13},{10,... | collective-permute-start | bytes 344072 | tf_op jit(solution)/shard_map/ppermute | solution.py:57
  71.6 8.0 %collective-permute-start.28 = (bf16[112,512]{1,0:T(8,128)(2,1)S(1)}, bf16[112,512]{1,0:T(8,128)(2,1)S(1)}, u32[]{:S(2)}, u32[]{:S(2)}) collective-permute-start(bf16[112,512]{1,0:T(8,128)(2,1)S(1)} %get-tuple-element.55.refs_0_), channel_id=1, source_target_pairs={{0,6},{1,7},{2,0},{3,1},{4,2},{5,3},{6,4},{7,5},{8,14},{9,15},{10,... | collective-permute-start | bytes 344072 | tf_op jit(solution)/shard_map/ppermute | solution.py:57
  73.7 7.3 %collective-permute-start.23 = (bf16[112,512]{1,0:T(8,128)(2,1)S(1)}, bf16[112,512]{1,0:T(8,128)(2,1)S(1)}, u32[]{:S(2)}, u32[]{:S(2)}) collective-permute-start(bf16[112,512]{1,0:T(8,128)(2,1)S(1)} %collective-permute-done.22.refs_3_), channel_id=1, source_target_pairs={{0,2},{1,3},{2,4},{3,5},{4,6},{5,7},{6,0},{7,1},{8,10},{9,11},{10,... | collective-permute-start | bytes 344072 | tf_op jit(solution)/shard_map/ppermute | solution.py:57
  75.9 6.4 %collective-permute-start.24 = (bf16[112,512]{1,0:T(8,128)(2,1)S(1)}, bf16[112,512]{1,0:T(8,128)(2,1)S(1)}, u32[]{:S(2)}, u32[]{:S(2)}) collective-permute-start(bf16[112,512]{1,0:T(8,128)(2,1)S(1)} %collective-permute-done.22.refs_3_), channel_id=1, source_target_pairs={{0,4},{1,5},{2,6},{3,7},{4,0},{5,1},{6,2},{7,3},{8,12},{9,13},{10,... | collective-permute-start | bytes 344072 | tf_op jit(solution)/shard_map/ppermute | solution.py:57
  76.8 6.7 %collective-permute-start.25 = (bf16[112,512]{1,0:T(8,128)(2,1)S(1)}, bf16[112,512]{1,0:T(8,128)(2,1)S(1)}, u32[]{:S(2)}, u32[]{:S(2)}) collective-permute-start(bf16[112,512]{1,0:T(8,128)(2,1)S(1)} %collective-permute-done.22.refs_3_), channel_id=1, source_target_pairs={{0,6},{1,7},{2,0},{3,1},{4,2},{5,3},{6,4},{7,5},{8,14},{9,15},{10,... | collective-permute-start | bytes 344072 | tf_op jit(solution)/shard_map/ppermute | solution.py:57

commit v6 on v5

--- a/solution.py
+++ b/solution.py
@@ -174,14 +174,14 @@
     out[...] = t.astype(out.dtype)
 
 
-def sum_near_body(own, near, total, s1, s2, s3):
-    rows = total.shape[0]
-    for ry, out in ((2, s2), (1, s1), (3, s3), (0, total)):
+def sum_near_body(parts, own, near, *refs):
+    rows = refs[-1].shape[0]
+    for ry, out in zip(parts, refs[-len(parts) :]):
         part = slice(ry * rows, (ry + 1) * rows)
         out[...] = (own[part, :] + near[part, :].astype(f32)).astype(out.dtype)
 
 
-def direction_body(z3, own, y1, y2, y3, z2, first, second, grad, direction):
+def direction_body(z3, own, y1, y3, z2, y2, first, second, grad, direction):
     g = own[...] + y1[...].astype(f32) + y2[...].astype(f32) + y3[...].astype(f32)
     g = g + z2[...].astype(f32) + z3[...].astype(f32)
     grad[...] = g
@@ -305,11 +305,17 @@
     far2 = over_y(*far2)
     z3 = to_z(call(sum_far_body, [(one, bf16)], 4)(own3, *far3)[0], 3)
     z2 = call(sum_far_body, [(one, bf16)], 5, in_specs=[VMEM] * 4 + [ANY])(own2, *far2, send)[0]
+    own, y1, y3 = call(
+        functools.partial(sum_near_body, (0, 1, 3)), [(one, f32)] + [(one, bf16)] * 2, 2
+    )(near, send)
+    y1, y3 = to_y(y1, 1), to_y(y3, 3)
+    y2 = call(
+        functools.partial(sum_near_body, (2,)), [(one, bf16)], 3, in_specs=[VMEM] * 2 + [ANY]
+    )(near, send, z2)[0]
+    y2 = to_y(y2, 2)
     z2 = to_z(z2, 2)
-    own, y1, y2, y3 = call(sum_near_body, [(one, f32)] + [(one, bf16)] * 3, 2)(near, send)
-    y1, y2, y3 = over_y(y1, y2, y3)
     grad, d0 = call(direction_body, [(one, f32), (one, bf16)], 8)(
-        z3, own, y1, y2, y3, z2, first_moment, second_moment
+        z3, own, y1, y3, z2, y2, first_moment, second_moment
     )
     e0 = to_h(d0)
     d2, d1, d3 = to_x(d0, 2), to_x(d0, 1), to_x(d0, 3)

time: 84.9 us -> 84.1 us (level)
  the two profiles are of different devices: /device:TPU:6 before, /device:TPU:32 now
where the time goes in v6:
time: 84.1 us; the launch traced here: 84 us
  starting transfers between devices  47.3 us (56%)
  waiting for transfers between devices  23 us (27%)
  Pallas kernels  12.7 us (15%)
  between operations  0.94 us (1%)
    ppermute x12, starting transfers between devices, to_x(): return lax.ppermute(a, 'shard', shard_perm(lambda x, h: (x + k, h)))  17.5 us
    ppermute x9, starting transfers between devices, to_y(): return lax.ppermute(a, 'dp', dp_perm(lambda y, z, c: (y + k, z, c)))  12 us
    ppermute x2, starting transfers between devices, to_h(): return lax.ppermute(a, 'shard', shard_perm(lambda x, h: (x, 1 - h)))  10.9 us
    ppermute x12, waiting for transfers between devices, to_x(): return lax.ppermute(a, 'shard', shard_perm(lambda x, h: (x + k, h)))  8.22 us
    ppermute x3, starting transfers between devices, to_z(): return lax.ppermute(a, 'dp', dp_perm(lambda y, z, c: (y, z ^ k, c)))  6.29 us
    ppermute x9, waiting for transfers between devices, to_y(): return lax.ppermute(a, 'dp', dp_perm(lambda y, z, c: (y + k, z, c)))  6.1 us
    ppermute x2, waiting for transfers between devices, to_h(): return lax.ppermute(a, 'shard', shard_perm(lambda x, h: (x, 1 - h)))  6 us
    pallas_call x3, Pallas kernels, update_part(): call(functools.partial(update_body, moves, aliased), [((NX * NH, rows, co...  3.6 us
  transfers between devices with their start and end apart: 29, of which 12 were waited for; matrix products, arithmetic and copies ran while one was open for 0% of the time, Pallas kernels for 10%

profile of v6, /device:TPU:32, one launch (start us, length us, event | category | flops | bytes accessed | tf_op | source)
XLA Modules:
  0.0 84.0 jit_solution(17532081773359413211)
XLA Ops:
  0.6 2.0 %shard_map.76 = (f32[128,512]{1,0:T(8,128)S(1)}, bf16[128,512]{1,0:T(8,128)(2,1)S(1)}, bf16[128,512]{1,0:T(8,128)(2,1)S(1)}, bf16[128,512]{1,0:T(8,128)(2,1)S(1)}) custom-call(bf16[512,1024]{1,0:T(8,128)(2,1)} %feat.1, bf16[1024,512]{1,0:T(8,128)(2,1)} %basis.3), custom_call_target="tpu_custom_call" | custom-call | tf_op jit(solution)/shard_map/pallas_call | solution.py:250
  2.6 1.6 %collective-permute-start = (bf16[128,512]{1,0:T(8,128)(2,1)S(1)}, bf16[128,512]{1,0:T(8,128)(2,1)S(1)}, u32[]{:S(2)}, u32[]{:S(2)}) collective-permute-start(bf16[128,512]{1,0:T(8,128)(2,1)S(1)} %get-tuple-element.34), channel_id=1, source_target_pairs={{0,2},{1,3},{2,4},{3,5},{4,6},{5,7},{6,0},{7,1},{8,10},{9,11},{10,... | collective-permute-start | bytes 393224 | tf_op jit(solution)/shard_map/ppermute | solution.py:57
  4.2 1.7 %collective-permute-start.1 = (bf16[128,512]{1,0:T(8,128)(2,1)S(1)}, bf16[128,512]{1,0:T(8,128)(2,1)S(1)}, u32[]{:S(2)}, u32[]{:S(2)}) collective-permute-start(bf16[128,512]{1,0:T(8,128)(2,1)S(1)} %get-tuple-element.35), channel_id=1, source_target_pairs={{0,6},{1,7},{2,0},{3,1},{4,2},{5,3},{6,4},{7,5},{8,14},{9,15},{10,... | collective-permute-start | bytes 393224 | tf_op jit(solution)/shard_map/ppermute | solution.py:57
  6.0 1.8 %collective-permute-start.2 = (bf16[128,512]{1,0:T(8,128)(2,1)S(1)}, bf16[128,512]{1,0:T(8,128)(2,1)S(1)}, u32[]{:S(2)}, u32[]{:S(2)}) collective-permute-start(bf16[128,512]{1,0:T(8,128)(2,1)S(1)} %get-tuple-element.36), channel_id=1, source_target_pairs={{0,4},{1,5},{2,6},{3,7},{4,0},{5,1},{6,2},{7,3},{8,12},{9,13},{10,... | collective-permute-start | bytes 393224 | tf_op jit(solution)/shard_map/ppermute | solution.py:57
  7.8 3.0 %shard_map.77 = (bf16[4,4,112,512]{3,2,1,0:T(8,128)(2,1)S(1)}, bf16[2,4,112,512]{3,2,1,0:T(8,128)(2,1)S(1)}, bf16[2,4,112,512]{3,2,1,0:T(8,128)(2,1)S(1)}, bf16[512,1024]{1,0:T(8,128)(2,1)S(1)}) custom-call(bf16[512,3584]{1,0:T(8,128)(2,1)} %grads.1, bf16[1024,512]{1,0:T(8,128)(2,1)} %basis.3, f32[128,512]{1,0:T(8,128)S(1)} %get-tuple-element.32._.own), custom_call_target="tpu_custom_call" | custom-call | tf_op jit(solution)/shard_map/pallas_call | solution.py:267
  11.4 1.6 %collective-permute-done.2.r3 = bf16[128,512]{1,0:T(8,128)(2,1)S(1)} collective-permute-done((bf16[128,512]{1,0:T(8,128)(2,1)S(1)}, bf16[128,512]{1,0:T(8,128)(2,1)S(1)}, u32[]{:S(2)}, u32[]{:S(2)}) %collective-permute-start.2) | collective-permute-done | bytes 131104 | tf_op jit(solution)/shard_map/ppermute | solution.py:57
  13.0 6.4 %collective-permute-start.3 = (bf16[128,512]{1,0:T(8,128)(2,1)S(1)}, bf16[128,512]{1,0:T(8,128)(2,1)S(1)}, u32[]{:S(2)}, u32[]{:S(2)}) collective-permute-start(bf16[128,512]{1,0:T(8,128)(2,1)S(1)} %get-tuple-element.38), channel_id=1, source_target_pairs={{0,1},{1,0},{2,3},{3,2},{4,5},{5,4},{6,7},{7,6},{8,9},{9,8},{10,11... | collective-permute-start | bytes 393224 | tf_op jit(solution)/shard_map/ppermute | solution.py:61
  19.4 5.7 %collective-permute-done.3.other = bf16[128,512]{1,0:T(8,128)(2,1)S(1)} collective-permute-done((bf16[128,512]{1,0:T(8,128)(2,1)S(1)}, bf16[128,512]{1,0:T(8,128)(2,1)S(1)}, u32[]{:S(2)}, u32[]{:S(2)}) %collective-permute-start.3) | collective-permute-done | bytes 131104 | tf_op jit(solution)/shard_map/ppermute | solution.py:61
  25.2 3.1 %collective-permute-start.5 = (bf16[128,512]{1,0:T(8,128)(2,1)S(1)}, bf16[128,512]{1,0:T(8,128)(2,1)S(1)}, u32[]{:S(2)}, u32[]{:S(2)}) collective-permute-start(bf16[128,512]{1,0:T(8,128)(2,1)S(1)} %shard_map.79.p0), channel_id=1, source_target_pairs={{0,4},{1,5},{2,6},{3,7},{4,0},{5,1},{6,2},{7,3},{8,12},{9,13},{10,... | collective-permute-start | bytes 393224 | tf_op jit(solution)/shard_map/ppermute | solution.py:57
  28.9 2.5 %collective-permute-done.4.p1 = bf16[128,512]{1,0:T(8,128)(2,1)S(1)} collective-permute-done((bf16[128,512]{1,0:T(8,128)(2,1)S(1)}, bf16[128,512]{1,0:T(8,128)(2,1)S(1)}, u32[]{:S(2)}, u32[]{:S(2)}) %collective-permute-start.4) | collective-permute-done | bytes 131104 | tf_op jit(solution)/shard_map/ppermute | solution.py:57
  31.4 1.4 %collective-permute-done.5.p2 = bf16[128,512]{1,0:T(8,128)(2,1)S(1)} collective-permute-done((bf16[128,512]{1,0:T(8,128)(2,1)S(1)}, bf16[128,512]{1,0:T(8,128)(2,1)S(1)}, u32[]{:S(2)}, u32[]{:S(2)}) %collective-permute-start.5) | collective-permute-done | bytes 131104 | tf_op jit(solution)/shard_map/ppermute | solution.py:57
  33.8 1.1 %shard_map.80.acc = f32[4,448,512]{2,1,0:T(8,128)S(1)} custom-call(bf16[4,4,112,512]{3,2,1,0:T(8,128)(2,1)S(1)} %get-tuple-element.33.keep, bf16[128,512]{1,0:T(8,128)(2,1)S(1)} %shard_map.79.p0, bf16[128,512]{1,0:T(8,128)(2,1)S(1)} %collective-permute-done.4.p1, bf16[128,512]{1,0:T(8,128)(2,1)S(1)} %collective-permute-done.5.p2, ...), custom_call_target="tpu_custom_call" | custom-call | tf_op jit(solution)/shard_map/pallas_call | solution.py:286
  36.7 1.7 %collective-permute-start.10 = (bf16[112,512]{1,0:T(8,128)(2,1)S(1)}, bf16[112,512]{1,0:T(8,128)(2,1)S(1)}, u32[]{:S(2)}, u32[]{:S(2)}) collective-permute-start(bf16[112,512]{1,0:T(8,128)(2,1)S(1)} %get-tuple-element.42), channel_id=1, source_target_pairs={{0,64},{8,72},{16,80},{24,88},{32,96},{40,104},{48,112},{56,120},{... | collective-permute-start | bytes 344072 | tf_op jit(solution)/shard_map/ppermute | solution.py:49
  38.4 2.9 %collective-permute-start.11 = (bf16[112,512]{1,0:T(8,128)(2,1)S(1)}, bf16[112,512]{1,0:T(8,128)(2,1)S(1)}, u32[]{:S(2)}, u32[]{:S(2)}) collective-permute-start(bf16[112,512]{1,0:T(8,128)(2,1)S(1)} %get-tuple-element.43), channel_id=1, source_target_pairs={{0,128},{8,136},{16,144},{24,152},{32,160},{40,168},{48,176},{56,1... | collective-permute-start | bytes 344072 | tf_op jit(solution)/shard_map/ppermute | solution.py:49
  41.3 1.3 %collective-permute-start.12 = (bf16[112,512]{1,0:T(8,128)(2,1)S(1)}, bf16[112,512]{1,0:T(8,128)(2,1)S(1)}, u32[]{:S(2)}, u32[]{:S(2)}) collective-permute-start(bf16[112,512]{1,0:T(8,128)(2,1)S(1)} %get-tuple-element.44), channel_id=1, source_target_pairs={{0,192},{8,200},{16,208},{24,216},{32,224},{40,232},{48,240},{56,2... | collective-permute-start | bytes 344072 | tf_op jit(solution)/shard_map/ppermute | solution.py:49
  44.1 1.0 %collective-permute-start.18 = (bf16[112,512]{1,0:T(8,128)(2,1)S(1)}, bf16[112,512]{1,0:T(8,128)(2,1)S(1)}, u32[]{:S(2)}, u32[]{:S(2)}) collective-permute-start(bf16[112,512]{1,0:T(8,128)(2,1)S(1)} %get-tuple-element.51), channel_id=1, source_target_pairs={{0,128},{8,136},{16,144},{24,152},{32,160},{40,168},{48,176},{56,1... | collective-permute-start | bytes 344072 | tf_op jit(solution)/shard_map/ppermute | solution.py:49
  45.2 2.5 %collective-permute-done.11.r2 = bf16[112,512]{1,0:T(8,128)(2,1)S(1)} collective-permute-done((bf16[112,512]{1,0:T(8,128)(2,1)S(1)}, bf16[112,512]{1,0:T(8,128)(2,1)S(1)}, u32[]{:S(2)}, u32[]{:S(2)}) %collective-permute-start.11) | collective-permute-done | bytes 114720 | tf_op jit(solution)/shard_map/ppermute | solution.py:49
  47.8 2.3 %collective-permute-start.13 = (bf16[112,512]{1,0:T(8,128)(2,1)S(1)}, bf16[112,512]{1,0:T(8,128)(2,1)S(1)}, u32[]{:S(2)}, u32[]{:S(2)}) collective-permute-start(bf16[112,512]{1,0:T(8,128)(2,1)S(1)} %shard_map.82), channel_id=1, source_target_pairs={{0,48},{8,56},{16,32},{24,40},{32,16},{40,24},{48,0},{56,8},{64,11... | collective-permute-start | bytes 344072 | tf_op jit(solution)/shard_map/ppermute | solution.py:53
  50.1 2.1 %collective-permute-start.15 = (bf16[112,512]{1,0:T(8,128)(2,1)S(1)}, bf16[112,512]{1,0:T(8,128)(2,1)S(1)}, u32[]{:S(2)}, u32[]{:S(2)}) collective-permute-start(bf16[112,512]{1,0:T(8,128)(2,1)S(1)} %get-tuple-element.47), channel_id=1, source_target_pairs={{0,64},{8,72},{16,80},{24,88},{32,96},{40,104},{48,112},{56,120},{... | collective-permute-start | bytes 344072 | tf_op jit(solution)/shard_map/ppermute | solution.py:49
  52.2 1.2 %collective-permute-start.16 = (bf16[112,512]{1,0:T(8,128)(2,1)S(1)}, bf16[112,512]{1,0:T(8,128)(2,1)S(1)}, u32[]{:S(2)}, u32[]{:S(2)}) collective-permute-start(bf16[112,512]{1,0:T(8,128)(2,1)S(1)} %get-tuple-element.48), channel_id=1, source_target_pairs={{0,192},{8,200},{16,208},{24,216},{32,224},{40,232},{48,240},{56,2... | collective-permute-start | bytes 344072 | tf_op jit(solution)/shard_map/ppermute | solution.py:49
  53.5 3.9 %collective-permute-start.20 = (bf16[112,512]{1,0:T(8,128)(2,1)S(1)}, bf16[112,512]{1,0:T(8,128)(2,1)S(1)}, u32[]{:S(2)}, u32[]{:S(2)}) collective-permute-start(bf16[112,512]{1,0:T(8,128)(2,1)S(1)} %shard_map.86.refs_0_), channel_id=1, source_target_pairs={{0,32},{8,40},{16,48},{24,56},{32,0},{40,8},{48,16},{56,24},{64,96... | collective-permute-start | bytes 344072 | tf_op jit(solution)/shard_map/ppermute | solution.py:53
  57.4 0.9 %collective-permute-start.21 = (bf16[112,512]{1,0:T(8,128)(2,1)S(1)}, bf16[112,512]{1,0:T(8,128)(2,1)S(1)}, u32[]{:S(2)}, u32[]{:S(2)}) collective-permute-start(bf16[112,512]{1,0:T(8,128)(2,1)S(1)} %shard_map.87), channel_id=1, source_target_pairs={{0,128},{8,136},{16,144},{24,152},{32,160},{40,168},{48,176},{56,1... | collective-permute-start | bytes 344072 | tf_op jit(solution)/shard_map/ppermute | solution.py:49
  58.4 1.9 %collective-permute-done.20.z2 = bf16[112,512]{1,0:T(8,128)(2,1)S(1)} collective-permute-done((bf16[112,512]{1,0:T(8,128)(2,1)S(1)}, bf16[112,512]{1,0:T(8,128)(2,1)S(1)}, u32[]{:S(2)}, u32[]{:S(2)}) %collective-permute-start.20) | collective-permute-done | bytes 114720 | tf_op jit(solution)/shard_map/ppermute | solution.py:53
  60.3 3.6 %collective-permute-done.21.y2 = bf16[112,512]{1,0:T(8,128)(2,1)S(1)} collective-permute-done((bf16[112,512]{1,0:T(8,128)(2,1)S(1)}, bf16[112,512]{1,0:T(8,128)(2,1)S(1)}, u32[]{:S(2)}, u32[]{:S(2)}) %collective-permute-start.21) | collective-permute-done | bytes 114720 | tf_op jit(solution)/shard_map/ppermute | solution.py:49
  64.1 4.5 %collective-permute-start.22 = (bf16[112,512]{1,0:T(8,128)(2,1)S(1)}, bf16[112,512]{1,0:T(8,128)(2,1)S(1)}, u32[]{:S(2)}, u32[]{:S(2)}) collective-permute-start(bf16[112,512]{1,0:T(8,128)(2,1)S(1)} %get-tuple-element.53.refs_0_), channel_id=1, source_target_pairs={{0,1},{1,0},{2,3},{3,2},{4,5},{5,4},{6,7},{7,6},{8,9},{9,8},{10,11... | collective-permute-start | bytes 344072 | tf_op jit(solution)/shard_map/ppermute | solution.py:61
  69.1 3.5 %collective-permute-start.27 = (bf16[112,512]{1,0:T(8,128)(2,1)S(1)}, bf16[112,512]{1,0:T(8,128)(2,1)S(1)}, u32[]{:S(2)}, u32[]{:S(2)}) collective-permute-start(bf16[112,512]{1,0:T(8,128)(2,1)S(1)} %get-tuple-element.53.refs_0_), channel_id=1, source_target_pairs={{0,4},{1,5},{2,6},{3,7},{4,0},{5,1},{6,2},{7,3},{8,12},{9,13},{10,... | collective-permute-start | bytes 344072 | tf_op jit(solution)/shard_map/ppermute | solution.py:57
  72.6 1.0 %shard_map.89.refs_5_ = bf16[8,112,1024]{2,1,0:T(8,128)(2,1)} custom-call(bf16[112,512]{1,0:T(8,128)(2,1)S(1)} %get-tuple-element.53.refs_0_, bf16[512,1024]{1,0:T(8,128)(2,1)S(1)} %get-tuple-element.54.refs_1_.refs_4_.refs_3_), custom_call_target="tpu_custom_call" | custom-call | tf_op jit(solution)/shard_map/pallas_call | solution.py:230
  73.9 1.8 %collective-permute-start.23 = (bf16[112,512]{1,0:T(8,128)(2,1)S(1)}, bf16[112,512]{1,0:T(8,128)(2,1)S(1)}, u32[]{:S(2)}, u32[]{:S(2)}) collective-permute-start(bf16[112,512]{1,0:T(8,128)(2,1)S(1)} %collective-permute-done.22.refs_3_), channel_id=1, source_target_pairs={{0,2},{1,3},{2,4},{3,5},{4,6},{5,7},{6,0},{7,1},{8,10},{9,11},{10,... | collective-permute-start | bytes 344072 | tf_op jit(solution)/shard_map/ppermute | solution.py:57
  75.7 2.2 %collective-permute-start.24 = (bf16[112,512]{1,0:T(8,128)(2,1)S(1)}, bf16[112,512]{1,0:T(8,128)(2,1)S(1)}, u32[]{:S(2)}, u32[]{:S(2)}) collective-permute-start(bf16[112,512]{1,0:T(8,128)(2,1)S(1)} %collective-permute-done.22.refs_3_), channel_id=1, source_target_pairs={{0,4},{1,5},{2,6},{3,7},{4,0},{5,1},{6,2},{7,3},{8,12},{9,13},{10,... | collective-permute-start | bytes 344072 | tf_op jit(solution)/shard_map/ppermute | solution.py:57
  79.3 1.4 %shard_map.90.refs_4_ = bf16[8,112,1024]{2,1,0:T(8,128)(2,1)} custom-call(bf16[112,512]{1,0:T(8,128)(2,1)S(1)} %collective-permute-done.26.refs_0_, bf16[112,512]{1,0:T(8,128)(2,1)S(1)} %collective-permute-done.27.refs_1_, bf16[112,512]{1,0:T(8,128)(2,1)S(1)} %collective-permute-done.28.refs_2_, ...), custom_call_target="tpu_custom_call", output_to_operand_aliasing={{}: (5, {})} | custom-call | tf_op jit(solution)/shard_map/pallas_call | solution.py:230
  80.7 1.2 %collective-permute-done.24.refs_1_ = bf16[112,512]{1,0:T(8,128)(2,1)S(1)} collective-permute-done((bf16[112,512]{1,0:T(8,128)(2,1)S(1)}, bf16[112,512]{1,0:T(8,128)(2,1)S(1)}, u32[]{:S(2)}, u32[]{:S(2)}) %collective-permute-start.24) | collective-permute-done | bytes 114720 | tf_op jit(solution)/shard_map/ppermute | solution.py:57
  82.6 1.2 %shard_map.91 = bf16[8,112,1024]{2,1,0:T(8,128)(2,1)} custom-call(bf16[112,512]{1,0:T(8,128)(2,1)S(1)} %collective-permute-done.23.refs_0_, bf16[112,512]{1,0:T(8,128)(2,1)S(1)} %collective-permute-done.24.refs_1_, bf16[112,512]{1,0:T(8,128)(2,1)S(1)} %collective-permute-done.25.refs_2_, ...), custom_call_target="tpu_custom_call", output_to_operand_aliasing={{}: (4, {})} | custom-call | tf_op jit(solution)/shard_map/pallas_call | solution.py:230
  (48 shorter events, 9.1 us)
Async XLA Ops:
  2.6 8.7 %collective-permute-start = (bf16[128,512]{1,0:T(8,128)(2,1)S(1)}, bf16[128,512]{1,0:T(8,128)(2,1)S(1)}, u32[]{:S(2)}, u32[]{:S(2)}) collective-permute-start(bf16[128,512]{1,0:T(8,128)(2,1)S(1)} %get-tuple-element.34), channel_id=1, source_target_pairs={{0,2},{1,3},{2,4},{3,5},{4,6},{5,7},{6,0},{7,1},{8,10},{9,11},{10,... | collective-permute-start | bytes 393224 | tf_op jit(solution)/shard_map/ppermute | solution.py:57
  4.2 7.2 %collective-permute-start.1 = (bf16[128,512]{1,0:T(8,128)(2,1)S(1)}, bf16[128,512]{1,0:T(8,128)(2,1)S(1)}, u32[]{:S(2)}, u32[]{:S(2)}) collective-permute-start(bf16[128,512]{1,0:T(8,128)(2,1)S(1)} %get-tuple-element.35), channel_id=1, source_target_pairs={{0,6},{1,7},{2,0},{3,1},{4,2},{5,3},{6,4},{7,5},{8,14},{9,15},{10,... | collective-permute-start | bytes 393224 | tf_op jit(solution)/shard_map/ppermute | solution.py:57
  6.0 7.0 %collective-permute-start.2 = (bf16[128,512]{1,0:T(8,128)(2,1)S(1)}, bf16[128,512]{1,0:T(8,128)(2,1)S(1)}, u32[]{:S(2)}, u32[]{:S(2)}) collective-permute-start(bf16[128,512]{1,0:T(8,128)(2,1)S(1)} %get-tuple-element.36), channel_id=1, source_target_pairs={{0,4},{1,5},{2,6},{3,7},{4,0},{5,1},{6,2},{7,3},{8,12},{9,13},{10,... | collective-permute-start | bytes 393224 | tf_op jit(solution)/shard_map/ppermute | solution.py:57
  10.8 24.9 %collective-permute-start.8 = (bf16[2,4,112,512]{3,2,1,0:T(8,128)(2,1)S(1)}, bf16[2,4,112,512]{3,2,1,0:T(8,128)(2,1)S(1)}, u32[]{:S(2)}, u32[]{:S(2)}) collective-permute-start(bf16[2,4,112,512]{3,2,1,0:T(8,128)(2,1)S(1)} %get-tuple-element.39), channel_id=1, source_target_pairs={{0,8},{8,0},{16,24},{24,16},{32,40},{40,32},{48,56},{56,48},{64,72... | collective-permute-start | bytes 2752520 | tf_op jit(solution)/shard_map/ppermute | solution.py:45
  10.9 24.8 %collective-permute-start.9 = (bf16[2,4,112,512]{3,2,1,0:T(8,128)(2,1)S(1)}, bf16[2,4,112,512]{3,2,1,0:T(8,128)(2,1)S(1)}, u32[]{:S(2)}, u32[]{:S(2)}) collective-permute-start(bf16[2,4,112,512]{3,2,1,0:T(8,128)(2,1)S(1)} %get-tuple-element.40), channel_id=1, source_target_pairs={{0,8},{8,0},{16,24},{24,16},{32,40},{40,32},{48,56},{56,48},{64,72... | collective-permute-start | bytes 2752520 | tf_op jit(solution)/shard_map/ppermute | solution.py:45
  13.0 12.0 %collective-permute-start.3 = (bf16[128,512]{1,0:T(8,128)(2,1)S(1)}, bf16[128,512]{1,0:T(8,128)(2,1)S(1)}, u32[]{:S(2)}, u32[]{:S(2)}) collective-permute-start(bf16[128,512]{1,0:T(8,128)(2,1)S(1)} %get-tuple-element.38), channel_id=1, source_target_pairs={{0,1},{1,0},{2,3},{3,2},{4,5},{5,4},{6,7},{7,6},{8,9},{9,8},{10,11... | collective-permute-start | bytes 393224 | tf_op jit(solution)/shard_map/ppermute | solution.py:61
  25.1 6.3 %collective-permute-start.4 = (bf16[128,512]{1,0:T(8,128)(2,1)S(1)}, bf16[128,512]{1,0:T(8,128)(2,1)S(1)}, u32[]{:S(2)}, u32[]{:S(2)}) collective-permute-start(bf16[128,512]{1,0:T(8,128)(2,1)S(1)} %shard_map.79.p0), channel_id=1, source_target_pairs={{0,2},{1,3},{2,4},{3,5},{4,6},{5,7},{6,0},{7,1},{8,10},{9,11},{10,... | collective-permute-start | bytes 393224 | tf_op jit(solution)/shard_map/ppermute | solution.py:57
  25.2 7.5 %collective-permute-start.5 = (bf16[128,512]{1,0:T(8,128)(2,1)S(1)}, bf16[128,512]{1,0:T(8,128)(2,1)S(1)}, u32[]{:S(2)}, u32[]{:S(2)}) collective-permute-start(bf16[128,512]{1,0:T(8,128)(2,1)S(1)} %shard_map.79.p0), channel_id=1, source_target_pairs={{0,4},{1,5},{2,6},{3,7},{4,0},{5,1},{6,2},{7,3},{8,12},{9,13},{10,... | collective-permute-start | bytes 393224 | tf_op jit(solution)/shard_map/ppermute | solution.py:57
  28.3 5.3 %collective-permute-start.6 = (bf16[128,512]{1,0:T(8,128)(2,1)S(1)}, bf16[128,512]{1,0:T(8,128)(2,1)S(1)}, u32[]{:S(2)}, u32[]{:S(2)}) collective-permute-start(bf16[128,512]{1,0:T(8,128)(2,1)S(1)} %shard_map.79.p0), channel_id=1, source_target_pairs={{0,6},{1,7},{2,0},{3,1},{4,2},{5,3},{6,4},{7,5},{8,14},{9,15},{10,... | collective-permute-start | bytes 393224 | tf_op jit(solution)/shard_map/ppermute | solution.py:57
  33.7 2.0 %collective-permute-start.7 = (bf16[512,512]{1,0:T(8,128)(2,1)S(1)}, bf16[512,512]{1,0:T(8,128)(2,1)S(1)}, u32[]{:S(2)}, u32[]{:S(2)}) collective-permute-start(bf16[512,512]{1,0:T(8,128)(2,1)S(1)} %pad_maximum_fusion), channel_id=1, source_target_pairs={{0,8},{8,0},{16,24},{24,16},{32,40},{40,32},{48,56},{56,48},{64,72... | collective-permute-start | bytes 1572872 | tf_op jit(solution)/shard_map/ppermute | solution.py:45
  36.1 13.9 %collective-permute-start.14 = (bf16[448,512]{1,0:T(8,128)(2,1)S(1)}, bf16[448,512]{1,0:T(8,128)(2,1)S(1)}, u32[]{:S(2)}, u32[]{:S(2)}) collective-permute-start(bf16[448,512]{1,0:T(8,128)(2,1)S(1)} %shard_map.84), channel_id=1, source_target_pairs={{0,16},{8,24},{16,0},{24,8},{32,48},{40,56},{48,32},{56,40},{64,80... | collective-permute-start | bytes 1376264 | tf_op jit(solution)/shard_map/ppermute | solution.py:53
  36.7 7.5 %collective-permute-start.10 = (bf16[112,512]{1,0:T(8,128)(2,1)S(1)}, bf16[112,512]{1,0:T(8,128)(2,1)S(1)}, u32[]{:S(2)}, u32[]{:S(2)}) collective-permute-start(bf16[112,512]{1,0:T(8,128)(2,1)S(1)} %get-tuple-element.42), channel_id=1, source_target_pairs={{0,64},{8,72},{16,80},{24,88},{32,96},{40,104},{48,112},{56,120},{... | collective-permute-start | bytes 344072 | tf_op jit(solution)/shard_map/ppermute | solution.py:49
  38.4 9.3 %collective-permute-start.11 = (bf16[112,512]{1,0:T(8,128)(2,1)S(1)}, bf16[112,512]{1,0:T(8,128)(2,1)S(1)}, u32[]{:S(2)}, u32[]{:S(2)}) collective-permute-start(bf16[112,512]{1,0:T(8,128)(2,1)S(1)} %get-tuple-element.43), channel_id=1, source_target_pairs={{0,128},{8,136},{16,144},{24,152},{32,160},{40,168},{48,176},{56,1... | collective-permute-start | bytes 344072 | tf_op jit(solution)/shard_map/ppermute | solution.py:49
  41.3 6.4 %collective-permute-start.12 = (bf16[112,512]{1,0:T(8,128)(2,1)S(1)}, bf16[112,512]{1,0:T(8,128)(2,1)S(1)}, u32[]{:S(2)}, u32[]{:S(2)}) collective-permute-start(bf16[112,512]{1,0:T(8,128)(2,1)S(1)} %get-tuple-element.44), channel_id=1, source_target_pairs={{0,192},{8,200},{16,208},{24,216},{32,224},{40,232},{48,240},{56,2... | collective-permute-start | bytes 344072 | tf_op jit(solution)/shard_map/ppermute | solution.py:49
  43.4 8.8 %collective-permute-start.17 = (bf16[112,512]{1,0:T(8,128)(2,1)S(1)}, bf16[112,512]{1,0:T(8,128)(2,1)S(1)}, u32[]{:S(2)}, u32[]{:S(2)}) collective-permute-start(bf16[112,512]{1,0:T(8,128)(2,1)S(1)} %get-tuple-element.50), channel_id=1, source_target_pairs={{0,64},{8,72},{16,80},{24,88},{32,96},{40,104},{48,112},{56,120},{... | collective-permute-start | bytes 344072 | tf_op jit(solution)/shard_map/ppermute | solution.py:49
  44.1 9.3 %collective-permute-start.18 = (bf16[112,512]{1,0:T(8,128)(2,1)S(1)}, bf16[112,512]{1,0:T(8,128)(2,1)S(1)}, u32[]{:S(2)}, u32[]{:S(2)}) collective-permute-start(bf16[112,512]{1,0:T(8,128)(2,1)S(1)} %get-tuple-element.51), channel_id=1, source_target_pairs={{0,128},{8,136},{16,144},{24,152},{32,160},{40,168},{48,176},{56,1... | collective-permute-start | bytes 344072 | tf_op jit(solution)/shard_map/ppermute | solution.py:49
  47.7 5.7 %collective-permute-start.19 = (bf16[112,512]{1,0:T(8,128)(2,1)S(1)}, bf16[112,512]{1,0:T(8,128)(2,1)S(1)}, u32[]{:S(2)}, u32[]{:S(2)}) collective-permute-start(bf16[112,512]{1,0:T(8,128)(2,1)S(1)} %get-tuple-element.52), channel_id=1, source_target_pairs={{0,192},{8,200},{16,208},{24,216},{32,224},{40,232},{48,240},{56,2... | collective-permute-start | bytes 344072 | tf_op jit(solution)/shard_map/ppermute | solution.py:49
  47.8 10.6 %collective-permute-start.13 = (bf16[112,512]{1,0:T(8,128)(2,1)S(1)}, bf16[112,512]{1,0:T(8,128)(2,1)S(1)}, u32[]{:S(2)}, u32[]{:S(2)}) collective-permute-start(bf16[112,512]{1,0:T(8,128)(2,1)S(1)} %shard_map.82), channel_id=1, source_target_pairs={{0,48},{8,56},{16,32},{24,40},{32,16},{40,24},{48,0},{56,8},{64,11... | collective-permute-start | bytes 344072 | tf_op jit(solution)/shard_map/ppermute | solution.py:53
  50.0 13.8 %copy-start = (f32[1,112,512]{2,1,0:T(8,128)S(1)}, f32[1,112,512]{2,1,0:T(8,128)}, u32[]{:S(2)}) copy-start(f32[1,112,512]{2,1,0:T(8,128)} %first.3) | copy-start | bytes 688132
  50.0 13.8 %copy-start.1 = (f32[1,112,512]{2,1,0:T(8,128)S(1)}, f32[1,112,512]{2,1,0:T(8,128)}, u32[]{:S(2)}) copy-start(f32[1,112,512]{2,1,0:T(8,128)} %second.3) | copy-start | bytes 688132
  50.1 8.3 %collective-permute-start.15 = (bf16[112,512]{1,0:T(8,128)(2,1)S(1)}, bf16[112,512]{1,0:T(8,128)(2,1)S(1)}, u32[]{:S(2)}, u32[]{:S(2)}) collective-permute-start(bf16[112,512]{1,0:T(8,128)(2,1)S(1)} %get-tuple-element.47), channel_id=1, source_target_pairs={{0,64},{8,72},{16,80},{24,88},{32,96},{40,104},{48,112},{56,120},{... | collective-permute-start | bytes 344072 | tf_op jit(solution)/shard_map/ppermute | solution.py:49
  52.2 6.2 %collective-permute-start.16 = (bf16[112,512]{1,0:T(8,128)(2,1)S(1)}, bf16[112,512]{1,0:T(8,128)(2,1)S(1)}, u32[]{:S(2)}, u32[]{:S(2)}) collective-permute-start(bf16[112,512]{1,0:T(8,128)(2,1)S(1)} %get-tuple-element.48), channel_id=1, source_target_pairs={{0,192},{8,200},{16,208},{24,216},{32,224},{40,232},{48,240},{56,2... | collective-permute-start | bytes 344072 | tf_op jit(solution)/shard_map/ppermute | solution.py:49
  53.5 6.8 %collective-permute-start.20 = (bf16[112,512]{1,0:T(8,128)(2,1)S(1)}, bf16[112,512]{1,0:T(8,128)(2,1)S(1)}, u32[]{:S(2)}, u32[]{:S(2)}) collective-permute-start(bf16[112,512]{1,0:T(8,128)(2,1)S(1)} %shard_map.86.refs_0_), channel_id=1, source_target_pairs={{0,32},{8,40},{16,48},{24,56},{32,0},{40,8},{48,16},{56,24},{64,96... | collective-permute-start | bytes 344072 | tf_op jit(solution)/shard_map/ppermute | solution.py:53
  57.4 6.4 %collective-permute-start.21 = (bf16[112,512]{1,0:T(8,128)(2,1)S(1)}, bf16[112,512]{1,0:T(8,128)(2,1)S(1)}, u32[]{:S(2)}, u32[]{:S(2)}) collective-permute-start(bf16[112,512]{1,0:T(8,128)(2,1)S(1)} %shard_map.87), channel_id=1, source_target_pairs={{0,128},{8,136},{16,144},{24,152},{32,160},{40,168},{48,176},{56,1... | collective-permute-start | bytes 344072 | tf_op jit(solution)/shard_map/ppermute | solution.py:49
  64.1 9.8 %collective-permute-start.22 = (bf16[112,512]{1,0:T(8,128)(2,1)S(1)}, bf16[112,512]{1,0:T(8,128)(2,1)S(1)}, u32[]{:S(2)}, u32[]{:S(2)}) collective-permute-start(bf16[112,512]{1,0:T(8,128)(2,1)S(1)} %get-tuple-element.53.refs_0_), channel_id=1, source_target_pairs={{0,1},{1,0},{2,3},{3,2},{4,5},{5,4},{6,7},{7,6},{8,9},{9,8},{10,11... | collective-permute-start | bytes 344072 | tf_op jit(solution)/shard_map/ppermute | solution.py:61
  68.6 9.2 %collective-permute-start.26 = (bf16[112,512]{1,0:T(8,128)(2,1)S(1)}, bf16[112,512]{1,0:T(8,128)(2,1)S(1)}, u32[]{:S(2)}, u32[]{:S(2)}) collective-permute-start(bf16[112,512]{1,0:T(8,128)(2,1)S(1)} %get-tuple-element.53.refs_0_), channel_id=1, source_target_pairs={{0,2},{1,3},{2,4},{3,5},{4,6},{5,7},{6,0},{7,1},{8,10},{9,11},{10,... | collective-permute-start | bytes 344072 | tf_op jit(solution)/shard_map/ppermute | solution.py:57
  69.1 10.2 %collective-permute-start.27 = (bf16[112,512]{1,0:T(8,128)(2,1)S(1)}, bf16[112,512]{1,0:T(8,128)(2,1)S(1)}, u32[]{:S(2)}, u32[]{:S(2)}) collective-permute-start(bf16[112,512]{1,0:T(8,128)(2,1)S(1)} %get-tuple-element.53.refs_0_), channel_id=1, source_target_pairs={{0,4},{1,5},{2,6},{3,7},{4,0},{5,1},{6,2},{7,3},{8,12},{9,13},{10,... | collective-permute-start | bytes 344072 | tf_op jit(solution)/shard_map/ppermute | solution.py:57
  72.6 6.8 %collective-permute-start.28 = (bf16[112,512]{1,0:T(8,128)(2,1)S(1)}, bf16[112,512]{1,0:T(8,128)(2,1)S(1)}, u32[]{:S(2)}, u32[]{:S(2)}) collective-permute-start(bf16[112,512]{1,0:T(8,128)(2,1)S(1)} %get-tuple-element.53.refs_0_), channel_id=1, source_target_pairs={{0,6},{1,7},{2,0},{3,1},{4,2},{5,3},{6,4},{7,5},{8,14},{9,15},{10,... | collective-permute-start | bytes 344072 | tf_op jit(solution)/shard_map/ppermute | solution.py:57
  73.9 6.8 %collective-permute-start.23 = (bf16[112,512]{1,0:T(8,128)(2,1)S(1)}, bf16[112,512]{1,0:T(8,128)(2,1)S(1)}, u32[]{:S(2)}, u32[]{:S(2)}) collective-permute-start(bf16[112,512]{1,0:T(8,128)(2,1)S(1)} %collective-permute-done.22.refs_3_), channel_id=1, source_target_pairs={{0,2},{1,3},{2,4},{3,5},{4,6},{5,7},{6,0},{7,1},{8,10},{9,11},{10,... | collective-permute-start | bytes 344072 | tf_op jit(solution)/shard_map/ppermute | solution.py:57
  75.7 6.3 %collective-permute-start.24 = (bf16[112,512]{1,0:T(8,128)(2,1)S(1)}, bf16[112,512]{1,0:T(8,128)(2,1)S(1)}, u32[]{:S(2)}, u32[]{:S(2)}) collective-permute-start(bf16[112,512]{1,0:T(8,128)(2,1)S(1)} %collective-permute-done.22.refs_3_), channel_id=1, source_target_pairs={{0,4},{1,5},{2,6},{3,7},{4,0},{5,1},{6,2},{7,3},{8,12},{9,13},{10,... | collective-permute-start | bytes 344072 | tf_op jit(solution)/shard_map/ppermute | solution.py:57
  77.8 4.8 %collective-permute-start.25 = (bf16[112,512]{1,0:T(8,128)(2,1)S(1)}, bf16[112,512]{1,0:T(8,128)(2,1)S(1)}, u32[]{:S(2)}, u32[]{:S(2)}) collective-permute-start(bf16[112,512]{1,0:T(8,128)(2,1)S(1)} %collective-permute-done.22.refs_3_), channel_id=1, source_target_pairs={{0,6},{1,7},{2,0},{3,1},{4,2},{5,3},{6,4},{7,5},{8,14},{9,15},{10,... | collective-permute-start | bytes 344072 | tf_op jit(solution)/shard_map/ppermute | solution.py:57

commit v7 on v6

--- a/solution.py
+++ b/solution.py
@@ -181,7 +181,7 @@
         out[...] = (own[part, :] + near[part, :].astype(f32)).astype(out.dtype)
 
 
-def direction_body(z3, own, y1, y3, z2, y2, first, second, grad, direction):
+def direction_body(z3, own, y1, y2, z2, y3, first, second, grad, direction):
     g = own[...] + y1[...].astype(f32) + y2[...].astype(f32) + y3[...].astype(f32)
     g = g + z2[...].astype(f32) + z3[...].astype(f32)
     grad[...] = g
@@ -292,8 +292,7 @@
         )
 
     def over_y(s1, s2, s3):
-        r2, r1, r3 = to_y(s2, 2), to_y(s1, 1), to_y(s3, 3)
-        return r1, r2, r3
+        return to_y(s1, 1), to_y(s3, 3), to_y(s2, 2)
 
     own3, *far3 = low_far(3)
     far3 = over_y(*far3)
@@ -305,17 +304,17 @@
     far2 = over_y(*far2)
     z3 = to_z(call(sum_far_body, [(one, bf16)], 4)(own3, *far3)[0], 3)
     z2 = call(sum_far_body, [(one, bf16)], 5, in_specs=[VMEM] * 4 + [ANY])(own2, *far2, send)[0]
-    own, y1, y3 = call(
-        functools.partial(sum_near_body, (0, 1, 3)), [(one, f32)] + [(one, bf16)] * 2, 2
+    own, y1, y2 = call(
+        functools.partial(sum_near_body, (0, 1, 2)), [(one, f32)] + [(one, bf16)] * 2, 2
     )(near, send)
-    y1, y3 = to_y(y1, 1), to_y(y3, 3)
-    y2 = call(
-        functools.partial(sum_near_body, (2,)), [(one, bf16)], 3, in_specs=[VMEM] * 2 + [ANY]
+    y1, y2 = to_y(y1, 1), to_y(y2, 2)
+    y3 = call(
+        functools.partial(sum_near_body, (3,)), [(one, bf16)], 3, in_specs=[VMEM] * 2 + [ANY]
     )(near, send, z2)[0]
-    y2 = to_y(y2, 2)
+    y3 = to_y(y3, 3)
     z2 = to_z(z2, 2)
     grad, d0 = call(direction_body, [(one, f32), (one, bf16)], 8)(
-        z3, own, y1, y3, z2, y2, first_moment, second_moment
+        z3, own, y1, y2, z2, y3, first_moment, second_moment
     )
     e0 = to_h(d0)
     d2, d1, d3 = to_x(d0, 2), to_x(d0, 1), to_x(d0, 3)

time: 84.1 us -> 83 us (0.987); the launches traced: 84 us -> 81.5 us
  waiting for transfers between devices: 23 us -> 17.5 us
  starting transfers between devices: 47.3 us -> 50.2 us
    ppermute x9, waiting for transfers between devices: 6.1 us -> 1.6 us  [to_y(): return lax.ppermute(a, 'dp', dp_perm(lambda y, z, c: (y + k, z, c)))]
    ppermute x9, starting transfers between devices: 12 us -> 15 us  [to_y(): return lax.ppermute(a, 'dp', dp_perm(lambda y, z, c: (y + k, z, c)))]
  transfers between devices with their start and end apart: 29 -> 29, of which waited for: 12 -> 10; matrix products, arithmetic and copies ran while one was open for 0% -> 0% of each run, Pallas kernels for 10% -> 11%
where the time goes in v7:
time: 83 us; the launch traced here: 81.5 us
  starting transfers between devices  50.2 us (60%)
  waiting for transfers between devices  17.5 us (21%)
  Pallas kernels  12.7 us (15%)
  between operations  0.95 us (1%)
    ppermute x12, starting transfers between devices, to_x(): return lax.ppermute(a, 'shard', shard_perm(lambda x, h: (x + k, h)))  17.9 us
    ppermute x9, starting transfers between devices, to_y(): return lax.ppermute(a, 'dp', dp_perm(lambda y, z, c: (y + k, z, c)))  15 us
    ppermute x2, starting transfers between devices, to_h(): return lax.ppermute(a, 'shard', shard_perm(lambda x, h: (x, 1 - h)))  11.1 us
    ppermute x12, waiting for transfers between devices, to_x(): return lax.ppermute(a, 'shard', shard_perm(lambda x, h: (x + k, h)))  7.62 us
    ppermute x2, waiting for transfers between devices, to_h(): return lax.ppermute(a, 'shard', shard_perm(lambda x, h: (x, 1 - h)))  5.66 us
    ppermute x3, starting transfers between devices, to_z(): return lax.ppermute(a, 'dp', dp_perm(lambda y, z, c: (y, z ^ k, c)))  5.54 us
    pallas_call x3, Pallas kernels, update_part(): call(functools.partial(update_body, moves, aliased), [((NX * NH, rows, co...  3.6 us
    pallas_call x1, Pallas kernels, per_device(): call(turn_body, [(block, bf16)] + [((NY // SPLIT, NZ, rows, tokens), bf16...  2.98 us
  transfers between devices with their start and end apart: 29, of which 10 were waited for; matrix products, arithmetic and copies ran while one was open for 0% of the time, Pallas kernels for 11%

profile of v7, /device:TPU:32, one launch (start us, length us, event | category | flops | bytes accessed | tf_op | source)
XLA Modules:
  0.0 81.5 jit_solution(15307842440886068933)
XLA Ops:
  0.6 2.0 %shard_map.76 = (f32[128,512]{1,0:T(8,128)S(1)}, bf16[128,512]{1,0:T(8,128)(2,1)S(1)}, bf16[128,512]{1,0:T(8,128)(2,1)S(1)}, bf16[128,512]{1,0:T(8,128)(2,1)S(1)}) custom-call(bf16[512,1024]{1,0:T(8,128)(2,1)} %feat.1, bf16[1024,512]{1,0:T(8,128)(2,1)} %basis.3), custom_call_target="tpu_custom_call" | custom-call | tf_op jit(solution)/shard_map/pallas_call | solution.py:250
  2.6 1.6 %collective-permute-start = (bf16[128,512]{1,0:T(8,128)(2,1)S(1)}, bf16[128,512]{1,0:T(8,128)(2,1)S(1)}, u32[]{:S(2)}, u32[]{:S(2)}) collective-permute-start(bf16[128,512]{1,0:T(8,128)(2,1)S(1)} %get-tuple-element.34), channel_id=1, source_target_pairs={{0,2},{1,3},{2,4},{3,5},{4,6},{5,7},{6,0},{7,1},{8,10},{9,11},{10,... | collective-permute-start | bytes 393224 | tf_op jit(solution)/shard_map/ppermute | solution.py:57
  4.2 1.7 %collective-permute-start.1 = (bf16[128,512]{1,0:T(8,128)(2,1)S(1)}, bf16[128,512]{1,0:T(8,128)(2,1)S(1)}, u32[]{:S(2)}, u32[]{:S(2)}) collective-permute-start(bf16[128,512]{1,0:T(8,128)(2,1)S(1)} %get-tuple-element.35), channel_id=1, source_target_pairs={{0,6},{1,7},{2,0},{3,1},{4,2},{5,3},{6,4},{7,5},{8,14},{9,15},{10,... | collective-permute-start | bytes 393224 | tf_op jit(solution)/shard_map/ppermute | solution.py:57
  6.0 1.8 %collective-permute-start.2 = (bf16[128,512]{1,0:T(8,128)(2,1)S(1)}, bf16[128,512]{1,0:T(8,128)(2,1)S(1)}, u32[]{:S(2)}, u32[]{:S(2)}) collective-permute-start(bf16[128,512]{1,0:T(8,128)(2,1)S(1)} %get-tuple-element.36), channel_id=1, source_target_pairs={{0,4},{1,5},{2,6},{3,7},{4,0},{5,1},{6,2},{7,3},{8,12},{9,13},{10,... | collective-permute-start | bytes 393224 | tf_op jit(solution)/shard_map/ppermute | solution.py:57
  7.8 3.0 %shard_map.77 = (bf16[4,4,112,512]{3,2,1,0:T(8,128)(2,1)S(1)}, bf16[2,4,112,512]{3,2,1,0:T(8,128)(2,1)S(1)}, bf16[2,4,112,512]{3,2,1,0:T(8,128)(2,1)S(1)}, bf16[512,1024]{1,0:T(8,128)(2,1)S(1)}) custom-call(bf16[512,3584]{1,0:T(8,128)(2,1)} %grads.1, bf16[1024,512]{1,0:T(8,128)(2,1)} %basis.3, f32[128,512]{1,0:T(8,128)S(1)} %get-tuple-element.32._.own), custom_call_target="tpu_custom_call" | custom-call | tf_op jit(solution)/shard_map/pallas_call | solution.py:267
  11.4 1.6 %collective-permute-done.2.r3 = bf16[128,512]{1,0:T(8,128)(2,1)S(1)} collective-permute-done((bf16[128,512]{1,0:T(8,128)(2,1)S(1)}, bf16[128,512]{1,0:T(8,128)(2,1)S(1)}, u32[]{:S(2)}, u32[]{:S(2)}) %collective-permute-start.2) | collective-permute-done | bytes 131104 | tf_op jit(solution)/shard_map/ppermute | solution.py:57
  13.0 6.4 %collective-permute-start.3 = (bf16[128,512]{1,0:T(8,128)(2,1)S(1)}, bf16[128,512]{1,0:T(8,128)(2,1)S(1)}, u32[]{:S(2)}, u32[]{:S(2)}) collective-permute-start(bf16[128,512]{1,0:T(8,128)(2,1)S(1)} %get-tuple-element.38), channel_id=1, source_target_pairs={{0,1},{1,0},{2,3},{3,2},{4,5},{5,4},{6,7},{7,6},{8,9},{9,8},{10,11... | collective-permute-start | bytes 393224 | tf_op jit(solution)/shard_map/ppermute | solution.py:61
  19.4 5.7 %collective-permute-done.3.other = bf16[128,512]{1,0:T(8,128)(2,1)S(1)} collective-permute-done((bf16[128,512]{1,0:T(8,128)(2,1)S(1)}, bf16[128,512]{1,0:T(8,128)(2,1)S(1)}, u32[]{:S(2)}, u32[]{:S(2)}) %collective-permute-start.3) | collective-permute-done | bytes 131104 | tf_op jit(solution)/shard_map/ppermute | solution.py:61
  25.2 3.1 %collective-permute-start.5 = (bf16[128,512]{1,0:T(8,128)(2,1)S(1)}, bf16[128,512]{1,0:T(8,128)(2,1)S(1)}, u32[]{:S(2)}, u32[]{:S(2)}) collective-permute-start(bf16[128,512]{1,0:T(8,128)(2,1)S(1)} %shard_map.79.p0), channel_id=1, source_target_pairs={{0,4},{1,5},{2,6},{3,7},{4,0},{5,1},{6,2},{7,3},{8,12},{9,13},{10,... | collective-permute-start | bytes 393224 | tf_op jit(solution)/shard_map/ppermute | solution.py:57
  28.9 2.5 %collective-permute-done.4.p1 = bf16[128,512]{1,0:T(8,128)(2,1)S(1)} collective-permute-done((bf16[128,512]{1,0:T(8,128)(2,1)S(1)}, bf16[128,512]{1,0:T(8,128)(2,1)S(1)}, u32[]{:S(2)}, u32[]{:S(2)}) %collective-permute-start.4) | collective-permute-done | bytes 131104 | tf_op jit(solution)/shard_map/ppermute | solution.py:57
  31.4 1.4 %collective-permute-done.5.p2 = bf16[128,512]{1,0:T(8,128)(2,1)S(1)} collective-permute-done((bf16[128,512]{1,0:T(8,128)(2,1)S(1)}, bf16[128,512]{1,0:T(8,128)(2,1)S(1)}, u32[]{:S(2)}, u32[]{:S(2)}) %collective-permute-start.5) | collective-permute-done | bytes 131104 | tf_op jit(solution)/shard_map/ppermute | solution.py:57
  33.8 1.1 %shard_map.80.acc = f32[4,448,512]{2,1,0:T(8,128)S(1)} custom-call(bf16[4,4,112,512]{3,2,1,0:T(8,128)(2,1)S(1)} %get-tuple-element.33.keep, bf16[128,512]{1,0:T(8,128)(2,1)S(1)} %shard_map.79.p0, bf16[128,512]{1,0:T(8,128)(2,1)S(1)} %collective-permute-done.4.p1, bf16[128,512]{1,0:T(8,128)(2,1)S(1)} %collective-permute-done.5.p2, ...), custom_call_target="tpu_custom_call" | custom-call | tf_op jit(solution)/shard_map/pallas_call | solution.py:286
  36.7 1.7 %collective-permute-start.10 = (bf16[112,512]{1,0:T(8,128)(2,1)S(1)}, bf16[112,512]{1,0:T(8,128)(2,1)S(1)}, u32[]{:S(2)}, u32[]{:S(2)}) collective-permute-start(bf16[112,512]{1,0:T(8,128)(2,1)S(1)} %get-tuple-element.42), channel_id=1, source_target_pairs={{0,64},{8,72},{16,80},{24,88},{32,96},{40,104},{48,112},{56,120},{... | collective-permute-start | bytes 344072 | tf_op jit(solution)/shard_map/ppermute | solution.py:49
  38.4 1.6 %collective-permute-start.11 = (bf16[112,512]{1,0:T(8,128)(2,1)S(1)}, bf16[112,512]{1,0:T(8,128)(2,1)S(1)}, u32[]{:S(2)}, u32[]{:S(2)}) collective-permute-start(bf16[112,512]{1,0:T(8,128)(2,1)S(1)} %get-tuple-element.43), channel_id=1, source_target_pairs={{0,192},{8,200},{16,208},{24,216},{32,224},{40,232},{48,240},{56,2... | collective-permute-start | bytes 344072 | tf_op jit(solution)/shard_map/ppermute | solution.py:49
  40.0 2.0 %collective-permute-start.12 = (bf16[112,512]{1,0:T(8,128)(2,1)S(1)}, bf16[112,512]{1,0:T(8,128)(2,1)S(1)}, u32[]{:S(2)}, u32[]{:S(2)}) collective-permute-start(bf16[112,512]{1,0:T(8,128)(2,1)S(1)} %get-tuple-element.44), channel_id=1, source_target_pairs={{0,128},{8,136},{16,144},{24,152},{32,160},{40,168},{48,176},{56,1... | collective-permute-start | bytes 344072 | tf_op jit(solution)/shard_map/ppermute | solution.py:49
  43.5 2.6 %collective-permute-start.18 = (bf16[112,512]{1,0:T(8,128)(2,1)S(1)}, bf16[112,512]{1,0:T(8,128)(2,1)S(1)}, u32[]{:S(2)}, u32[]{:S(2)}) collective-permute-start(bf16[112,512]{1,0:T(8,128)(2,1)S(1)} %get-tuple-element.51), channel_id=1, source_target_pairs={{0,192},{8,200},{16,208},{24,216},{32,224},{40,232},{48,240},{56,2... | collective-permute-start | bytes 344072 | tf_op jit(solution)/shard_map/ppermute | solution.py:49
  46.1 1.2 %collective-permute-start.19 = (bf16[112,512]{1,0:T(8,128)(2,1)S(1)}, bf16[112,512]{1,0:T(8,128)(2,1)S(1)}, u32[]{:S(2)}, u32[]{:S(2)}) collective-permute-start(bf16[112,512]{1,0:T(8,128)(2,1)S(1)} %get-tuple-element.52), channel_id=1, source_target_pairs={{0,128},{8,136},{16,144},{24,152},{32,160},{40,168},{48,176},{56,1... | collective-permute-start | bytes 344072 | tf_op jit(solution)/shard_map/ppermute | solution.py:49
  47.6 2.3 %collective-permute-start.13 = (bf16[112,512]{1,0:T(8,128)(2,1)S(1)}, bf16[112,512]{1,0:T(8,128)(2,1)S(1)}, u32[]{:S(2)}, u32[]{:S(2)}) collective-permute-start(bf16[112,512]{1,0:T(8,128)(2,1)S(1)} %shard_map.82), channel_id=1, source_target_pairs={{0,48},{8,56},{16,32},{24,40},{32,16},{40,24},{48,0},{56,8},{64,11... | collective-permute-start | bytes 344072 | tf_op jit(solution)/shard_map/ppermute | solution.py:53
  49.9 2.1 %collective-permute-start.15 = (bf16[112,512]{1,0:T(8,128)(2,1)S(1)}, bf16[112,512]{1,0:T(8,128)(2,1)S(1)}, u32[]{:S(2)}, u32[]{:S(2)}) collective-permute-start(bf16[112,512]{1,0:T(8,128)(2,1)S(1)} %get-tuple-element.47), channel_id=1, source_target_pairs={{0,64},{8,72},{16,80},{24,88},{32,96},{40,104},{48,112},{56,120},{... | collective-permute-start | bytes 344072 | tf_op jit(solution)/shard_map/ppermute | solution.py:49
  52.1 1.3 %collective-permute-start.16 = (bf16[112,512]{1,0:T(8,128)(2,1)S(1)}, bf16[112,512]{1,0:T(8,128)(2,1)S(1)}, u32[]{:S(2)}, u32[]{:S(2)}) collective-permute-start(bf16[112,512]{1,0:T(8,128)(2,1)S(1)} %get-tuple-element.48), channel_id=1, source_target_pairs={{0,128},{8,136},{16,144},{24,152},{32,160},{40,168},{48,176},{56,1... | collective-permute-start | bytes 344072 | tf_op jit(solution)/shard_map/ppermute | solution.py:49
  53.5 3.2 %collective-permute-start.20 = (bf16[112,512]{1,0:T(8,128)(2,1)S(1)}, bf16[112,512]{1,0:T(8,128)(2,1)S(1)}, u32[]{:S(2)}, u32[]{:S(2)}) collective-permute-start(bf16[112,512]{1,0:T(8,128)(2,1)S(1)} %shard_map.86.refs_0_), channel_id=1, source_target_pairs={{0,32},{8,40},{16,48},{24,56},{32,0},{40,8},{48,16},{56,24},{64,96... | collective-permute-start | bytes 344072 | tf_op jit(solution)/shard_map/ppermute | solution.py:53
  56.7 1.7 %collective-permute-start.21 = (bf16[112,512]{1,0:T(8,128)(2,1)S(1)}, bf16[112,512]{1,0:T(8,128)(2,1)S(1)}, u32[]{:S(2)}, u32[]{:S(2)}) collective-permute-start(bf16[112,512]{1,0:T(8,128)(2,1)S(1)} %shard_map.87), channel_id=1, source_target_pairs={{0,192},{8,200},{16,208},{24,216},{32,224},{40,232},{48,240},{56,2... | collective-permute-start | bytes 344072 | tf_op jit(solution)/shard_map/ppermute | solution.py:49
  58.4 1.9 %collective-permute-done.20.z2 = bf16[112,512]{1,0:T(8,128)(2,1)S(1)} collective-permute-done((bf16[112,512]{1,0:T(8,128)(2,1)S(1)}, bf16[112,512]{1,0:T(8,128)(2,1)S(1)}, u32[]{:S(2)}, u32[]{:S(2)}) %collective-permute-start.20) | collective-permute-done | bytes 114720 | tf_op jit(solution)/shard_map/ppermute | solution.py:53
  60.2 1.3 %collective-permute-done.21.y3 = bf16[112,512]{1,0:T(8,128)(2,1)S(1)} collective-permute-done((bf16[112,512]{1,0:T(8,128)(2,1)S(1)}, bf16[112,512]{1,0:T(8,128)(2,1)S(1)}, u32[]{:S(2)}, u32[]{:S(2)}) %collective-permute-start.21) | collective-permute-done | bytes 114720 | tf_op jit(solution)/shard_map/ppermute | solution.py:49
  61.8 4.8 %collective-permute-start.22 = (bf16[112,512]{1,0:T(8,128)(2,1)S(1)}, bf16[112,512]{1,0:T(8,128)(2,1)S(1)}, u32[]{:S(2)}, u32[]{:S(2)}) collective-permute-start(bf16[112,512]{1,0:T(8,128)(2,1)S(1)} %get-tuple-element.53.refs_0_), channel_id=1, source_target_pairs={{0,1},{1,0},{2,3},{3,2},{4,5},{5,4},{6,7},{7,6},{8,9},{9,8},{10,11... | collective-permute-start | bytes 344072 | tf_op jit(solution)/shard_map/ppermute | solution.py:61
  67.1 3.5 %collective-permute-start.27 = (bf16[112,512]{1,0:T(8,128)(2,1)S(1)}, bf16[112,512]{1,0:T(8,128)(2,1)S(1)}, u32[]{:S(2)}, u32[]{:S(2)}) collective-permute-start(bf16[112,512]{1,0:T(8,128)(2,1)S(1)} %get-tuple-element.53.refs_0_), channel_id=1, source_target_pairs={{0,4},{1,5},{2,6},{3,7},{4,0},{5,1},{6,2},{7,3},{8,12},{9,13},{10,... | collective-permute-start | bytes 344072 | tf_op jit(solution)/shard_map/ppermute | solution.py:57
  71.7 2.1 %collective-permute-start.23 = (bf16[112,512]{1,0:T(8,128)(2,1)S(1)}, bf16[112,512]{1,0:T(8,128)(2,1)S(1)}, u32[]{:S(2)}, u32[]{:S(2)}) collective-permute-start(bf16[112,512]{1,0:T(8,128)(2,1)S(1)} %collective-permute-done.22.refs_3_), channel_id=1, source_target_pairs={{0,2},{1,3},{2,4},{3,5},{4,6},{5,7},{6,0},{7,1},{8,10},{9,11},{10,... | collective-permute-start | bytes 344072 | tf_op jit(solution)/shard_map/ppermute | solution.py:57
  73.8 1.1 %collective-permute-start.24 = (bf16[112,512]{1,0:T(8,128)(2,1)S(1)}, bf16[112,512]{1,0:T(8,128)(2,1)S(1)}, u32[]{:S(2)}, u32[]{:S(2)}) collective-permute-start(bf16[112,512]{1,0:T(8,128)(2,1)S(1)} %collective-permute-done.22.refs_3_), channel_id=1, source_target_pairs={{0,4},{1,5},{2,6},{3,7},{4,0},{5,1},{6,2},{7,3},{8,12},{9,13},{10,... | collective-permute-start | bytes 344072 | tf_op jit(solution)/shard_map/ppermute | solution.py:57
  74.9 1.7 %collective-permute-start.25 = (bf16[112,512]{1,0:T(8,128)(2,1)S(1)}, bf16[112,512]{1,0:T(8,128)(2,1)S(1)}, u32[]{:S(2)}, u32[]{:S(2)}) collective-permute-start(bf16[112,512]{1,0:T(8,128)(2,1)S(1)} %collective-permute-done.22.refs_3_), channel_id=1, source_target_pairs={{0,6},{1,7},{2,0},{3,1},{4,2},{5,3},{6,4},{7,5},{8,14},{9,15},{10,... | collective-permute-start | bytes 344072 | tf_op jit(solution)/shard_map/ppermute | solution.py:57
  77.4 1.4 %shard_map.90.refs_4_ = bf16[8,112,1024]{2,1,0:T(8,128)(2,1)} custom-call(bf16[112,512]{1,0:T(8,128)(2,1)S(1)} %collective-permute-done.26.refs_0_, bf16[112,512]{1,0:T(8,128)(2,1)S(1)} %collective-permute-done.27.refs_1_, bf16[112,512]{1,0:T(8,128)(2,1)S(1)} %collective-permute-done.28.refs_2_, ...), custom_call_target="tpu_custom_call", output_to_operand_aliasing={{}: (5, {})} | custom-call | tf_op jit(solution)/shard_map/pallas_call | solution.py:230
  78.8 1.3 %collective-permute-done.24.refs_1_ = bf16[112,512]{1,0:T(8,128)(2,1)S(1)} collective-permute-done((bf16[112,512]{1,0:T(8,128)(2,1)S(1)}, bf16[112,512]{1,0:T(8,128)(2,1)S(1)}, u32[]{:S(2)}, u32[]{:S(2)}) %collective-permute-start.24) | collective-permute-done | bytes 114720 | tf_op jit(solution)/shard_map/ppermute | solution.py:57
  80.1 1.2 %shard_map.91 = bf16[8,112,1024]{2,1,0:T(8,128)(2,1)} custom-call(bf16[112,512]{1,0:T(8,128)(2,1)S(1)} %collective-permute-done.23.refs_0_, bf16[112,512]{1,0:T(8,128)(2,1)S(1)} %collective-permute-done.24.refs_1_, bf16[112,512]{1,0:T(8,128)(2,1)S(1)} %collective-permute-done.25.refs_2_, ...), custom_call_target="tpu_custom_call", output_to_operand_aliasing={{}: (4, {})} | custom-call | tf_op jit(solution)/shard_map/pallas_call | solution.py:230
  (48 shorter events, 8.7 us)
Async XLA Ops:
  2.6 8.7 %collective-permute-start = (bf16[128,512]{1,0:T(8,128)(2,1)S(1)}, bf16[128,512]{1,0:T(8,128)(2,1)S(1)}, u32[]{:S(2)}, u32[]{:S(2)}) collective-permute-start(bf16[128,512]{1,0:T(8,128)(2,1)S(1)} %get-tuple-element.34), channel_id=1, source_target_pairs={{0,2},{1,3},{2,4},{3,5},{4,6},{5,7},{6,0},{7,1},{8,10},{9,11},{10,... | collective-permute-start | bytes 393224 | tf_op jit(solution)/shard_map/ppermute | solution.py:57
  4.2 7.2 %collective-permute-start.1 = (bf16[128,512]{1,0:T(8,128)(2,1)S(1)}, bf16[128,512]{1,0:T(8,128)(2,1)S(1)}, u32[]{:S(2)}, u32[]{:S(2)}) collective-permute-start(bf16[128,512]{1,0:T(8,128)(2,1)S(1)} %get-tuple-element.35), channel_id=1, source_target_pairs={{0,6},{1,7},{2,0},{3,1},{4,2},{5,3},{6,4},{7,5},{8,14},{9,15},{10,... | collective-permute-start | bytes 393224 | tf_op jit(solution)/shard_map/ppermute | solution.py:57
  6.0 7.0 %collective-permute-start.2 = (bf16[128,512]{1,0:T(8,128)(2,1)S(1)}, bf16[128,512]{1,0:T(8,128)(2,1)S(1)}, u32[]{:S(2)}, u32[]{:S(2)}) collective-permute-start(bf16[128,512]{1,0:T(8,128)(2,1)S(1)} %get-tuple-element.36), channel_id=1, source_target_pairs={{0,4},{1,5},{2,6},{3,7},{4,0},{5,1},{6,2},{7,3},{8,12},{9,13},{10,... | collective-permute-start | bytes 393224 | tf_op jit(solution)/shard_map/ppermute | solution.py:57
  10.8 24.9 %collective-permute-start.8 = (bf16[2,4,112,512]{3,2,1,0:T(8,128)(2,1)S(1)}, bf16[2,4,112,512]{3,2,1,0:T(8,128)(2,1)S(1)}, u32[]{:S(2)}, u32[]{:S(2)}) collective-permute-start(bf16[2,4,112,512]{3,2,1,0:T(8,128)(2,1)S(1)} %get-tuple-element.39), channel_id=1, source_target_pairs={{0,8},{8,0},{16,24},{24,16},{32,40},{40,32},{48,56},{56,48},{64,72... | collective-permute-start | bytes 2752520 | tf_op jit(solution)/shard_map/ppermute | solution.py:45
  10.9 24.8 %collective-permute-start.9 = (bf16[2,4,112,512]{3,2,1,0:T(8,128)(2,1)S(1)}, bf16[2,4,112,512]{3,2,1,0:T(8,128)(2,1)S(1)}, u32[]{:S(2)}, u32[]{:S(2)}) collective-permute-start(bf16[2,4,112,512]{3,2,1,0:T(8,128)(2,1)S(1)} %get-tuple-element.40), channel_id=1, source_target_pairs={{0,8},{8,0},{16,24},{24,16},{32,40},{40,32},{48,56},{56,48},{64,72... | collective-permute-start | bytes 2752520 | tf_op jit(solution)/shard_map/ppermute | solution.py:45
  13.0 12.0 %collective-permute-start.3 = (bf16[128,512]{1,0:T(8,128)(2,1)S(1)}, bf16[128,512]{1,0:T(8,128)(2,1)S(1)}, u32[]{:S(2)}, u32[]{:S(2)}) collective-permute-start(bf16[128,512]{1,0:T(8,128)(2,1)S(1)} %get-tuple-element.38), channel_id=1, source_target_pairs={{0,1},{1,0},{2,3},{3,2},{4,5},{5,4},{6,7},{7,6},{8,9},{9,8},{10,11... | collective-permute-start | bytes 393224 | tf_op jit(solution)/shard_map/ppermute | solution.py:61
  25.1 6.3 %collective-permute-start.4 = (bf16[128,512]{1,0:T(8,128)(2,1)S(1)}, bf16[128,512]{1,0:T(8,128)(2,1)S(1)}, u32[]{:S(2)}, u32[]{:S(2)}) collective-permute-start(bf16[128,512]{1,0:T(8,128)(2,1)S(1)} %shard_map.79.p0), channel_id=1, source_target_pairs={{0,2},{1,3},{2,4},{3,5},{4,6},{5,7},{6,0},{7,1},{8,10},{9,11},{10,... | collective-permute-start | bytes 393224 | tf_op jit(solution)/shard_map/ppermute | solution.py:57
  25.2 7.5 %collective-permute-start.5 = (bf16[128,512]{1,0:T(8,128)(2,1)S(1)}, bf16[128,512]{1,0:T(8,128)(2,1)S(1)}, u32[]{:S(2)}, u32[]{:S(2)}) collective-permute-start(bf16[128,512]{1,0:T(8,128)(2,1)S(1)} %shard_map.79.p0), channel_id=1, source_target_pairs={{0,4},{1,5},{2,6},{3,7},{4,0},{5,1},{6,2},{7,3},{8,12},{9,13},{10,... | collective-permute-start | bytes 393224 | tf_op jit(solution)/shard_map/ppermute | solution.py:57
  28.3 5.3 %collective-permute-start.6 = (bf16[128,512]{1,0:T(8,128)(2,1)S(1)}, bf16[128,512]{1,0:T(8,128)(2,1)S(1)}, u32[]{:S(2)}, u32[]{:S(2)}) collective-permute-start(bf16[128,512]{1,0:T(8,128)(2,1)S(1)} %shard_map.79.p0), channel_id=1, source_target_pairs={{0,6},{1,7},{2,0},{3,1},{4,2},{5,3},{6,4},{7,5},{8,14},{9,15},{10,... | collective-permute-start | bytes 393224 | tf_op jit(solution)/shard_map/ppermute | solution.py:57
  33.7 2.0 %collective-permute-start.7 = (bf16[512,512]{1,0:T(8,128)(2,1)S(1)}, bf16[512,512]{1,0:T(8,128)(2,1)S(1)}, u32[]{:S(2)}, u32[]{:S(2)}) collective-permute-start(bf16[512,512]{1,0:T(8,128)(2,1)S(1)} %pad_maximum_fusion), channel_id=1, source_target_pairs={{0,8},{8,0},{16,24},{24,16},{32,40},{40,32},{48,56},{56,48},{64,72... | collective-permute-start | bytes 1572872 | tf_op jit(solution)/shard_map/ppermute | solution.py:45
  36.1 13.7 %collective-permute-start.14 = (bf16[448,512]{1,0:T(8,128)(2,1)S(1)}, bf16[448,512]{1,0:T(8,128)(2,1)S(1)}, u32[]{:S(2)}, u32[]{:S(2)}) collective-permute-start(bf16[448,512]{1,0:T(8,128)(2,1)S(1)} %shard_map.84), channel_id=1, source_target_pairs={{0,16},{8,24},{16,0},{24,8},{32,48},{40,56},{48,32},{56,40},{64,80... | collective-permute-start | bytes 1376264 | tf_op jit(solution)/shard_map/ppermute | solution.py:53
  36.7 6.8 %collective-permute-start.10 = (bf16[112,512]{1,0:T(8,128)(2,1)S(1)}, bf16[112,512]{1,0:T(8,128)(2,1)S(1)}, u32[]{:S(2)}, u32[]{:S(2)}) collective-permute-start(bf16[112,512]{1,0:T(8,128)(2,1)S(1)} %get-tuple-element.42), channel_id=1, source_target_pairs={{0,64},{8,72},{16,80},{24,88},{32,96},{40,104},{48,112},{56,120},{... | collective-permute-start | bytes 344072 | tf_op jit(solution)/shard_map/ppermute | solution.py:49
  38.4 7.7 %collective-permute-start.11 = (bf16[112,512]{1,0:T(8,128)(2,1)S(1)}, bf16[112,512]{1,0:T(8,128)(2,1)S(1)}, u32[]{:S(2)}, u32[]{:S(2)}) collective-permute-start(bf16[112,512]{1,0:T(8,128)(2,1)S(1)} %get-tuple-element.43), channel_id=1, source_target_pairs={{0,192},{8,200},{16,208},{24,216},{32,224},{40,232},{48,240},{56,2... | collective-permute-start | bytes 344072 | tf_op jit(solution)/shard_map/ppermute | solution.py:49
  40.0 7.5 %collective-permute-start.12 = (bf16[112,512]{1,0:T(8,128)(2,1)S(1)}, bf16[112,512]{1,0:T(8,128)(2,1)S(1)}, u32[]{:S(2)}, u32[]{:S(2)}) collective-permute-start(bf16[112,512]{1,0:T(8,128)(2,1)S(1)} %get-tuple-element.44), channel_id=1, source_target_pairs={{0,128},{8,136},{16,144},{24,152},{32,160},{40,168},{48,176},{56,1... | collective-permute-start | bytes 344072 | tf_op jit(solution)/shard_map/ppermute | solution.py:49
  42.8 9.3 %collective-permute-start.17 = (bf16[112,512]{1,0:T(8,128)(2,1)S(1)}, bf16[112,512]{1,0:T(8,128)(2,1)S(1)}, u32[]{:S(2)}, u32[]{:S(2)}) collective-permute-start(bf16[112,512]{1,0:T(8,128)(2,1)S(1)} %get-tuple-element.50), channel_id=1, source_target_pairs={{0,64},{8,72},{16,80},{24,88},{32,96},{40,104},{48,112},{56,120},{... | collective-permute-start | bytes 344072 | tf_op jit(solution)/shard_map/ppermute | solution.py:49
  43.5 9.9 %collective-permute-start.18 = (bf16[112,512]{1,0:T(8,128)(2,1)S(1)}, bf16[112,512]{1,0:T(8,128)(2,1)S(1)}, u32[]{:S(2)}, u32[]{:S(2)}) collective-permute-start(bf16[112,512]{1,0:T(8,128)(2,1)S(1)} %get-tuple-element.51), channel_id=1, source_target_pairs={{0,192},{8,200},{16,208},{24,216},{32,224},{40,232},{48,240},{56,2... | collective-permute-start | bytes 344072 | tf_op jit(solution)/shard_map/ppermute | solution.py:49
  46.1 7.3 %collective-permute-start.19 = (bf16[112,512]{1,0:T(8,128)(2,1)S(1)}, bf16[112,512]{1,0:T(8,128)(2,1)S(1)}, u32[]{:S(2)}, u32[]{:S(2)}) collective-permute-start(bf16[112,512]{1,0:T(8,128)(2,1)S(1)} %get-tuple-element.52), channel_id=1, source_target_pairs={{0,128},{8,136},{16,144},{24,152},{32,160},{40,168},{48,176},{56,1... | collective-permute-start | bytes 344072 | tf_op jit(solution)/shard_map/ppermute | solution.py:49
  47.6 10.8 %collective-permute-start.13 = (bf16[112,512]{1,0:T(8,128)(2,1)S(1)}, bf16[112,512]{1,0:T(8,128)(2,1)S(1)}, u32[]{:S(2)}, u32[]{:S(2)}) collective-permute-start(bf16[112,512]{1,0:T(8,128)(2,1)S(1)} %shard_map.82), channel_id=1, source_target_pairs={{0,48},{8,56},{16,32},{24,40},{32,16},{40,24},{48,0},{56,8},{64,11... | collective-permute-start | bytes 344072 | tf_op jit(solution)/shard_map/ppermute | solution.py:53
  49.9 11.7 %copy-start = (f32[1,112,512]{2,1,0:T(8,128)S(1)}, f32[1,112,512]{2,1,0:T(8,128)}, u32[]{:S(2)}) copy-start(f32[1,112,512]{2,1,0:T(8,128)} %first.3) | copy-start | bytes 688132
  49.9 11.7 %copy-start.1 = (f32[1,112,512]{2,1,0:T(8,128)S(1)}, f32[1,112,512]{2,1,0:T(8,128)}, u32[]{:S(2)}) copy-start(f32[1,112,512]{2,1,0:T(8,128)} %second.3) | copy-start | bytes 688132
  49.9 8.4 %collective-permute-start.15 = (bf16[112,512]{1,0:T(8,128)(2,1)S(1)}, bf16[112,512]{1,0:T(8,128)(2,1)S(1)}, u32[]{:S(2)}, u32[]{:S(2)}) collective-permute-start(bf16[112,512]{1,0:T(8,128)(2,1)S(1)} %get-tuple-element.47), channel_id=1, source_target_pairs={{0,64},{8,72},{16,80},{24,88},{32,96},{40,104},{48,112},{56,120},{... | collective-permute-start | bytes 344072 | tf_op jit(solution)/shard_map/ppermute | solution.py:49
  52.1 6.3 %collective-permute-start.16 = (bf16[112,512]{1,0:T(8,128)(2,1)S(1)}, bf16[112,512]{1,0:T(8,128)(2,1)S(1)}, u32[]{:S(2)}, u32[]{:S(2)}) collective-permute-start(bf16[112,512]{1,0:T(8,128)(2,1)S(1)} %get-tuple-element.48), channel_id=1, source_target_pairs={{0,128},{8,136},{16,144},{24,152},{32,160},{40,168},{48,176},{56,1... | collective-permute-start | bytes 344072 | tf_op jit(solution)/shard_map/ppermute | solution.py:49
  53.5 6.8 %collective-permute-start.20 = (bf16[112,512]{1,0:T(8,128)(2,1)S(1)}, bf16[112,512]{1,0:T(8,128)(2,1)S(1)}, u32[]{:S(2)}, u32[]{:S(2)}) collective-permute-start(bf16[112,512]{1,0:T(8,128)(2,1)S(1)} %shard_map.86.refs_0_), channel_id=1, source_target_pairs={{0,32},{8,40},{16,48},{24,56},{32,0},{40,8},{48,16},{56,24},{64,96... | collective-permute-start | bytes 344072 | tf_op jit(solution)/shard_map/ppermute | solution.py:53
  56.7 4.9 %collective-permute-start.21 = (bf16[112,512]{1,0:T(8,128)(2,1)S(1)}, bf16[112,512]{1,0:T(8,128)(2,1)S(1)}, u32[]{:S(2)}, u32[]{:S(2)}) collective-permute-start(bf16[112,512]{1,0:T(8,128)(2,1)S(1)} %shard_map.87), channel_id=1, source_target_pairs={{0,192},{8,200},{16,208},{24,216},{32,224},{40,232},{48,240},{56,2... | collective-permute-start | bytes 344072 | tf_op jit(solution)/shard_map/ppermute | solution.py:49
  61.8 9.8 %collective-permute-start.22 = (bf16[112,512]{1,0:T(8,128)(2,1)S(1)}, bf16[112,512]{1,0:T(8,128)(2,1)S(1)}, u32[]{:S(2)}, u32[]{:S(2)}) collective-permute-start(bf16[112,512]{1,0:T(8,128)(2,1)S(1)} %get-tuple-element.53.refs_0_), channel_id=1, source_target_pairs={{0,1},{1,0},{2,3},{3,2},{4,5},{5,4},{6,7},{7,6},{8,9},{9,8},{10,11... | collective-permute-start | bytes 344072 | tf_op jit(solution)/shard_map/ppermute | solution.py:61
  66.6 8.3 %collective-permute-start.26 = (bf16[112,512]{1,0:T(8,128)(2,1)S(1)}, bf16[112,512]{1,0:T(8,128)(2,1)S(1)}, u32[]{:S(2)}, u32[]{:S(2)}) collective-permute-start(bf16[112,512]{1,0:T(8,128)(2,1)S(1)} %get-tuple-element.53.refs_0_), channel_id=1, source_target_pairs={{0,2},{1,3},{2,4},{3,5},{4,6},{5,7},{6,0},{7,1},{8,10},{9,11},{10,... | collective-permute-start | bytes 344072 | tf_op jit(solution)/shard_map/ppermute | solution.py:57
  67.1 10.2 %collective-permute-start.27 = (bf16[112,512]{1,0:T(8,128)(2,1)S(1)}, bf16[112,512]{1,0:T(8,128)(2,1)S(1)}, u32[]{:S(2)}, u32[]{:S(2)}) collective-permute-start(bf16[112,512]{1,0:T(8,128)(2,1)S(1)} %get-tuple-element.53.refs_0_), channel_id=1, source_target_pairs={{0,4},{1,5},{2,6},{3,7},{4,0},{5,1},{6,2},{7,3},{8,12},{9,13},{10,... | collective-permute-start | bytes 344072 | tf_op jit(solution)/shard_map/ppermute | solution.py:57
  70.7 6.7 %collective-permute-start.28 = (bf16[112,512]{1,0:T(8,128)(2,1)S(1)}, bf16[112,512]{1,0:T(8,128)(2,1)S(1)}, u32[]{:S(2)}, u32[]{:S(2)}) collective-permute-start(bf16[112,512]{1,0:T(8,128)(2,1)S(1)} %get-tuple-element.53.refs_0_), channel_id=1, source_target_pairs={{0,6},{1,7},{2,0},{3,1},{4,2},{5,3},{6,4},{7,5},{8,14},{9,15},{10,... | collective-permute-start | bytes 344072 | tf_op jit(solution)/shard_map/ppermute | solution.py:57
  71.7 7.1 %collective-permute-start.23 = (bf16[112,512]{1,0:T(8,128)(2,1)S(1)}, bf16[112,512]{1,0:T(8,128)(2,1)S(1)}, u32[]{:S(2)}, u32[]{:S(2)}) collective-permute-start(bf16[112,512]{1,0:T(8,128)(2,1)S(1)} %collective-permute-done.22.refs_3_), channel_id=1, source_target_pairs={{0,2},{1,3},{2,4},{3,5},{4,6},{5,7},{6,0},{7,1},{8,10},{9,11},{10,... | collective-permute-start | bytes 344072 | tf_op jit(solution)/shard_map/ppermute | solution.py:57
  73.8 6.3 %collective-permute-start.24 = (bf16[112,512]{1,0:T(8,128)(2,1)S(1)}, bf16[112,512]{1,0:T(8,128)(2,1)S(1)}, u32[]{:S(2)}, u32[]{:S(2)}) collective-permute-start(bf16[112,512]{1,0:T(8,128)(2,1)S(1)} %collective-permute-done.22.refs_3_), channel_id=1, source_target_pairs={{0,4},{1,5},{2,6},{3,7},{4,0},{5,1},{6,2},{7,3},{8,12},{9,13},{10,... | collective-permute-start | bytes 344072 | tf_op jit(solution)/shard_map/ppermute | solution.py:57
  74.9 5.2 %collective-permute-start.25 = (bf16[112,512]{1,0:T(8,128)(2,1)S(1)}, bf16[112,512]{1,0:T(8,128)(2,1)S(1)}, u32[]{:S(2)}, u32[]{:S(2)}) collective-permute-start(bf16[112,512]{1,0:T(8,128)(2,1)S(1)} %collective-permute-done.22.refs_3_), channel_id=1, source_target_pairs={{0,6},{1,7},{2,0},{3,1},{4,2},{5,3},{6,4},{7,5},{8,14},{9,15},{10,... | collective-permute-start | bytes 344072 | tf_op jit(solution)/shard_map/ppermute | solution.py:57

commit v8 on v7

--- a/solution.py
+++ b/solution.py
@@ -163,8 +163,8 @@
         out[ry * rows : (ry + 1) * rows, :] = t.astype(out.dtype)
 
 
-def low_rest_body(rz, acc, q, *refs):
-    low_near_body(0, acc, q, *refs[: SPLIT + 1])
+def low_pair_body(near, rz, acc, q, *refs):
+    low_near_body(near, acc, q, *refs[: SPLIT + 1])
     low_far_body(rz, acc, q, *refs[:SPLIT], *refs[SPLIT + 1 :])
 
 
@@ -286,21 +286,17 @@
     acc = call(low_own_body, [((NY, NZ * rows, rank), f32)], 5)(keep, p0, p1, p2, p3)[0]
     one, four = (rows, rank), (NY * rows, rank)
 
-    def low_far(rz):
-        return call(functools.partial(low_far_body, rz), [(one, f32)] + [(one, bf16)] * 3, 2 + SPLIT)(
-            acc, q, *other
-        )
+    def low_pair(near, rz, dtype):
+        outs = [(four, dtype), (one, f32)] + [(one, bf16)] * 3
+        return call(functools.partial(low_pair_body, near, rz), outs, 2 + SPLIT)(acc, q, *other)
 
     def over_y(s1, s2, s3):
         return to_y(s1, 1), to_y(s3, 3), to_y(s2, 2)
 
-    own3, *far3 = low_far(3)
+    send, own3, *far3 = low_pair(1, 3, bf16)
     far3 = over_y(*far3)
-    send = call(functools.partial(low_near_body, 1), [(four, bf16)], 2 + SPLIT)(acc, q, *other)[0]
     send = to_z(send, 1)
-    near, own2, *far2 = call(
-        functools.partial(low_rest_body, 2), [(four, f32), (one, f32)] + [(one, bf16)] * 3, 2 + SPLIT
-    )(acc, q, *other)
+    near, own2, *far2 = low_pair(0, 2, f32)
     far2 = over_y(*far2)
     z3 = to_z(call(sum_far_body, [(one, bf16)], 4)(own3, *far3)[0], 3)
     z2 = call(sum_far_body, [(one, bf16)], 5, in_specs=[VMEM] * 4 + [ANY])(own2, *far2, send)[0]

time: 83 us -> 82.5 us (level)
    ppermute x3, starting transfers between devices: 5.54 us -> 4.54 us  [to_z(): return lax.ppermute(a, 'dp', dp_perm(lambda y, z, c: (y, z ^ k, c)))]
    pallas_call x3 -> x2, Pallas kernels: 1.67 us -> 1.52 us  [low_pair(): call(functools.partial(low_pair_body, near, rz), outs, 2 + SPLIT)]
  transfers between devices with their start and end apart: 29 -> 29, of which waited for: 10 -> 11; matrix products, arithmetic and copies ran while one was open for 0% -> 0% of each run, Pallas kernels for 11% -> 10%
where the time goes in v8:
time: 82.5 us; the launch traced here: 81.3 us
  starting transfers between devices  50.4 us (61%)
  waiting for transfers between devices  17.4 us (21%)
  Pallas kernels  12.6 us (15%)
  between operations  0.94 us (1%)
    ppermute x12, starting transfers between devices, to_x(): return lax.ppermute(a, 'shard', shard_perm(lambda x, h: (x + k, h)))  18 us
    ppermute x9, starting transfers between devices, to_y(): return lax.ppermute(a, 'dp', dp_perm(lambda y, z, c: (y + k, z, c)))  15.6 us
    ppermute x2, starting transfers between devices, to_h(): return lax.ppermute(a, 'shard', shard_perm(lambda x, h: (x, 1 - h)))  11.5 us
    ppermute x12, waiting for transfers between devices, to_x(): return lax.ppermute(a, 'shard', shard_perm(lambda x, h: (x + k, h)))  7.62 us
    ppermute x2, waiting for transfers between devices, to_h(): return lax.ppermute(a, 'shard', shard_perm(lambda x, h: (x, 1 - h)))  5.66 us
    ppermute x3, starting transfers between devices, to_z(): return lax.ppermute(a, 'dp', dp_perm(lambda y, z, c: (y, z ^ k, c)))  4.54 us
    pallas_call x3, Pallas kernels, update_part(): call(functools.partial(update_body, moves, aliased), [((NX * NH, rows, co...  3.6 us
    pallas_call x1, Pallas kernels, per_device(): call(turn_body, [(block, bf16)] + [((NY // SPLIT, NZ, rows, tokens), bf16...  2.98 us
  transfers between devices with their start and end apart: 29, of which 11 were waited for; matrix products, arithmetic and copies ran while one was open for 0% of the time, Pallas kernels for 10%

profile of v8, /device:TPU:32, one launch (start us, length us, event | category | flops | bytes accessed | tf_op | source)
XLA Modules:
  0.0 81.3 jit_solution(18194485333080622392)
XLA Ops:
  0.6 2.0 %shard_map.76 = (f32[128,512]{1,0:T(8,128)S(1)}, bf16[128,512]{1,0:T(8,128)(2,1)S(1)}, bf16[128,512]{1,0:T(8,128)(2,1)S(1)}, bf16[128,512]{1,0:T(8,128)(2,1)S(1)}) custom-call(bf16[512,1024]{1,0:T(8,128)(2,1)} %feat.1, bf16[1024,512]{1,0:T(8,128)(2,1)} %basis.3), custom_call_target="tpu_custom_call" | custom-call | tf_op jit(solution)/shard_map/pallas_call | solution.py:250
  2.6 1.6 %collective-permute-start = (bf16[128,512]{1,0:T(8,128)(2,1)S(1)}, bf16[128,512]{1,0:T(8,128)(2,1)S(1)}, u32[]{:S(2)}, u32[]{:S(2)}) collective-permute-start(bf16[128,512]{1,0:T(8,128)(2,1)S(1)} %get-tuple-element.35), channel_id=1, source_target_pairs={{0,2},{1,3},{2,4},{3,5},{4,6},{5,7},{6,0},{7,1},{8,10},{9,11},{10,... | collective-permute-start | bytes 393224 | tf_op jit(solution)/shard_map/ppermute | solution.py:57
  4.2 1.7 %collective-permute-start.1 = (bf16[128,512]{1,0:T(8,128)(2,1)S(1)}, bf16[128,512]{1,0:T(8,128)(2,1)S(1)}, u32[]{:S(2)}, u32[]{:S(2)}) collective-permute-start(bf16[128,512]{1,0:T(8,128)(2,1)S(1)} %get-tuple-element.36), channel_id=1, source_target_pairs={{0,6},{1,7},{2,0},{3,1},{4,2},{5,3},{6,4},{7,5},{8,14},{9,15},{10,... | collective-permute-start | bytes 393224 | tf_op jit(solution)/shard_map/ppermute | solution.py:57
  6.0 1.8 %collective-permute-start.2 = (bf16[128,512]{1,0:T(8,128)(2,1)S(1)}, bf16[128,512]{1,0:T(8,128)(2,1)S(1)}, u32[]{:S(2)}, u32[]{:S(2)}) collective-permute-start(bf16[128,512]{1,0:T(8,128)(2,1)S(1)} %get-tuple-element.37), channel_id=1, source_target_pairs={{0,4},{1,5},{2,6},{3,7},{4,0},{5,1},{6,2},{7,3},{8,12},{9,13},{10,... | collective-permute-start | bytes 393224 | tf_op jit(solution)/shard_map/ppermute | solution.py:57
  7.8 3.0 %shard_map.77 = (bf16[4,4,112,512]{3,2,1,0:T(8,128)(2,1)S(1)}, bf16[2,4,112,512]{3,2,1,0:T(8,128)(2,1)S(1)}, bf16[2,4,112,512]{3,2,1,0:T(8,128)(2,1)S(1)}, bf16[512,1024]{1,0:T(8,128)(2,1)S(1)}) custom-call(bf16[512,3584]{1,0:T(8,128)(2,1)} %grads.1, bf16[1024,512]{1,0:T(8,128)(2,1)} %basis.3, f32[128,512]{1,0:T(8,128)S(1)} %get-tuple-element.33._.own), custom_call_target="tpu_custom_call" | custom-call | tf_op jit(solution)/shard_map/pallas_call | solution.py:267
  11.4 1.6 %collective-permute-done.2.r3 = bf16[128,512]{1,0:T(8,128)(2,1)S(1)} collective-permute-done((bf16[128,512]{1,0:T(8,128)(2,1)S(1)}, bf16[128,512]{1,0:T(8,128)(2,1)S(1)}, u32[]{:S(2)}, u32[]{:S(2)}) %collective-permute-start.2) | collective-permute-done | bytes 131104 | tf_op jit(solution)/shard_map/ppermute | solution.py:57
  13.0 6.4 %collective-permute-start.3 = (bf16[128,512]{1,0:T(8,128)(2,1)S(1)}, bf16[128,512]{1,0:T(8,128)(2,1)S(1)}, u32[]{:S(2)}, u32[]{:S(2)}) collective-permute-start(bf16[128,512]{1,0:T(8,128)(2,1)S(1)} %get-tuple-element.39), channel_id=1, source_target_pairs={{0,1},{1,0},{2,3},{3,2},{4,5},{5,4},{6,7},{7,6},{8,9},{9,8},{10,11... | collective-permute-start | bytes 393224 | tf_op jit(solution)/shard_map/ppermute | solution.py:61
  19.4 5.7 %collective-permute-done.3.other = bf16[128,512]{1,0:T(8,128)(2,1)S(1)} collective-permute-done((bf16[128,512]{1,0:T(8,128)(2,1)S(1)}, bf16[128,512]{1,0:T(8,128)(2,1)S(1)}, u32[]{:S(2)}, u32[]{:S(2)}) %collective-permute-start.3) | collective-permute-done | bytes 131104 | tf_op jit(solution)/shard_map/ppermute | solution.py:61
  25.2 3.1 %collective-permute-start.5 = (bf16[128,512]{1,0:T(8,128)(2,1)S(1)}, bf16[128,512]{1,0:T(8,128)(2,1)S(1)}, u32[]{:S(2)}, u32[]{:S(2)}) collective-permute-start(bf16[128,512]{1,0:T(8,128)(2,1)S(1)} %shard_map.79.p0), channel_id=1, source_target_pairs={{0,4},{1,5},{2,6},{3,7},{4,0},{5,1},{6,2},{7,3},{8,12},{9,13},{10,... | collective-permute-start | bytes 393224 | tf_op jit(solution)/shard_map/ppermute | solution.py:57
  28.9 2.5 %collective-permute-done.4.p1 = bf16[128,512]{1,0:T(8,128)(2,1)S(1)} collective-permute-done((bf16[128,512]{1,0:T(8,128)(2,1)S(1)}, bf16[128,512]{1,0:T(8,128)(2,1)S(1)}, u32[]{:S(2)}, u32[]{:S(2)}) %collective-permute-start.4) | collective-permute-done | bytes 131104 | tf_op jit(solution)/shard_map/ppermute | solution.py:57
  31.4 1.4 %collective-permute-done.5.p2 = bf16[128,512]{1,0:T(8,128)(2,1)S(1)} collective-permute-done((bf16[128,512]{1,0:T(8,128)(2,1)S(1)}, bf16[128,512]{1,0:T(8,128)(2,1)S(1)}, u32[]{:S(2)}, u32[]{:S(2)}) %collective-permute-start.5) | collective-permute-done | bytes 131104 | tf_op jit(solution)/shard_map/ppermute | solution.py:57
  33.8 1.1 %shard_map.80.acc = f32[4,448,512]{2,1,0:T(8,128)S(1)} custom-call(bf16[4,4,112,512]{3,2,1,0:T(8,128)(2,1)S(1)} %get-tuple-element.34.keep, bf16[128,512]{1,0:T(8,128)(2,1)S(1)} %shard_map.79.p0, bf16[128,512]{1,0:T(8,128)(2,1)S(1)} %collective-permute-done.4.p1, bf16[128,512]{1,0:T(8,128)(2,1)S(1)} %collective-permute-done.5.p2, ...), custom_call_target="tpu_custom_call" | custom-call | tf_op jit(solution)/shard_map/pallas_call | solution.py:286
  36.5 1.7 %collective-permute-start.10 = (bf16[112,512]{1,0:T(8,128)(2,1)S(1)}, bf16[112,512]{1,0:T(8,128)(2,1)S(1)}, u32[]{:S(2)}, u32[]{:S(2)}) collective-permute-start(bf16[112,512]{1,0:T(8,128)(2,1)S(1)} %get-tuple-element.43), channel_id=1, source_target_pairs={{0,64},{8,72},{16,80},{24,88},{32,96},{40,104},{48,112},{56,120},{... | collective-permute-start | bytes 344072 | tf_op jit(solution)/shard_map/ppermute | solution.py:49
  38.2 1.6 %collective-permute-start.11 = (bf16[112,512]{1,0:T(8,128)(2,1)S(1)}, bf16[112,512]{1,0:T(8,128)(2,1)S(1)}, u32[]{:S(2)}, u32[]{:S(2)}) collective-permute-start(bf16[112,512]{1,0:T(8,128)(2,1)S(1)} %get-tuple-element.44), channel_id=1, source_target_pairs={{0,192},{8,200},{16,208},{24,216},{32,224},{40,232},{48,240},{56,2... | collective-permute-start | bytes 344072 | tf_op jit(solution)/shard_map/ppermute | solution.py:49
  39.8 2.0 %collective-permute-start.12 = (bf16[112,512]{1,0:T(8,128)(2,1)S(1)}, bf16[112,512]{1,0:T(8,128)(2,1)S(1)}, u32[]{:S(2)}, u32[]{:S(2)}) collective-permute-start(bf16[112,512]{1,0:T(8,128)(2,1)S(1)} %get-tuple-element.45), channel_id=1, source_target_pairs={{0,128},{8,136},{16,144},{24,152},{32,160},{40,168},{48,176},{56,1... | collective-permute-start | bytes 344072 | tf_op jit(solution)/shard_map/ppermute | solution.py:49
  43.4 2.6 %collective-permute-start.18 = (bf16[112,512]{1,0:T(8,128)(2,1)S(1)}, bf16[112,512]{1,0:T(8,128)(2,1)S(1)}, u32[]{:S(2)}, u32[]{:S(2)}) collective-permute-start(bf16[112,512]{1,0:T(8,128)(2,1)S(1)} %get-tuple-element.53), channel_id=1, source_target_pairs={{0,192},{8,200},{16,208},{24,216},{32,224},{40,232},{48,240},{56,2... | collective-permute-start | bytes 344072 | tf_op jit(solution)/shard_map/ppermute | solution.py:49
  45.9 1.2 %collective-permute-start.19 = (bf16[112,512]{1,0:T(8,128)(2,1)S(1)}, bf16[112,512]{1,0:T(8,128)(2,1)S(1)}, u32[]{:S(2)}, u32[]{:S(2)}) collective-permute-start(bf16[112,512]{1,0:T(8,128)(2,1)S(1)} %get-tuple-element.54), channel_id=1, source_target_pairs={{0,128},{8,136},{16,144},{24,152},{32,160},{40,168},{48,176},{56,1... | collective-permute-start | bytes 344072 | tf_op jit(solution)/shard_map/ppermute | solution.py:49
  47.4 2.2 %collective-permute-start.13 = (bf16[112,512]{1,0:T(8,128)(2,1)S(1)}, bf16[112,512]{1,0:T(8,128)(2,1)S(1)}, u32[]{:S(2)}, u32[]{:S(2)}) collective-permute-start(bf16[112,512]{1,0:T(8,128)(2,1)S(1)} %shard_map.82), channel_id=1, source_target_pairs={{0,48},{8,56},{16,32},{24,40},{32,16},{40,24},{48,0},{56,8},{64,11... | collective-permute-start | bytes 344072 | tf_op jit(solution)/shard_map/ppermute | solution.py:53
  49.8 2.1 %collective-permute-start.15 = (bf16[112,512]{1,0:T(8,128)(2,1)S(1)}, bf16[112,512]{1,0:T(8,128)(2,1)S(1)}, u32[]{:S(2)}, u32[]{:S(2)}) collective-permute-start(bf16[112,512]{1,0:T(8,128)(2,1)S(1)} %get-tuple-element.49), channel_id=1, source_target_pairs={{0,64},{8,72},{16,80},{24,88},{32,96},{40,104},{48,112},{56,120},{... | collective-permute-start | bytes 344072 | tf_op jit(solution)/shard_map/ppermute | solution.py:49
  51.9 1.8 %collective-permute-start.16 = (bf16[112,512]{1,0:T(8,128)(2,1)S(1)}, bf16[112,512]{1,0:T(8,128)(2,1)S(1)}, u32[]{:S(2)}, u32[]{:S(2)}) collective-permute-start(bf16[112,512]{1,0:T(8,128)(2,1)S(1)} %get-tuple-element.50), channel_id=1, source_target_pairs={{0,128},{8,136},{16,144},{24,152},{32,160},{40,168},{48,176},{56,1... | collective-permute-start | bytes 344072 | tf_op jit(solution)/shard_map/ppermute | solution.py:49
  53.8 2.2 %collective-permute-start.20 = (bf16[112,512]{1,0:T(8,128)(2,1)S(1)}, bf16[112,512]{1,0:T(8,128)(2,1)S(1)}, u32[]{:S(2)}, u32[]{:S(2)}) collective-permute-start(bf16[112,512]{1,0:T(8,128)(2,1)S(1)} %shard_map.85.refs_0_), channel_id=1, source_target_pairs={{0,32},{8,40},{16,48},{24,56},{32,0},{40,8},{48,16},{56,24},{64,96... | collective-permute-start | bytes 344072 | tf_op jit(solution)/shard_map/ppermute | solution.py:53
  56.0 1.8 %collective-permute-start.21 = (bf16[112,512]{1,0:T(8,128)(2,1)S(1)}, bf16[112,512]{1,0:T(8,128)(2,1)S(1)}, u32[]{:S(2)}, u32[]{:S(2)}) collective-permute-start(bf16[112,512]{1,0:T(8,128)(2,1)S(1)} %shard_map.86), channel_id=1, source_target_pairs={{0,192},{8,200},{16,208},{24,216},{32,224},{40,232},{48,240},{56,2... | collective-permute-start | bytes 344072 | tf_op jit(solution)/shard_map/ppermute | solution.py:49
  58.5 1.1 %collective-permute-done.20.z2 = bf16[112,512]{1,0:T(8,128)(2,1)S(1)} collective-permute-done((bf16[112,512]{1,0:T(8,128)(2,1)S(1)}, bf16[112,512]{1,0:T(8,128)(2,1)S(1)}, u32[]{:S(2)}, u32[]{:S(2)}) %collective-permute-start.20) | collective-permute-done | bytes 114720 | tf_op jit(solution)/shard_map/ppermute | solution.py:53
  59.7 1.2 %collective-permute-done.21.y3 = bf16[112,512]{1,0:T(8,128)(2,1)S(1)} collective-permute-done((bf16[112,512]{1,0:T(8,128)(2,1)S(1)}, bf16[112,512]{1,0:T(8,128)(2,1)S(1)}, u32[]{:S(2)}, u32[]{:S(2)}) %collective-permute-start.21) | collective-permute-done | bytes 114720 | tf_op jit(solution)/shard_map/ppermute | solution.py:49
  61.2 5.2 %collective-permute-start.22 = (bf16[112,512]{1,0:T(8,128)(2,1)S(1)}, bf16[112,512]{1,0:T(8,128)(2,1)S(1)}, u32[]{:S(2)}, u32[]{:S(2)}) collective-permute-start(bf16[112,512]{1,0:T(8,128)(2,1)S(1)} %get-tuple-element.55.refs_0_), channel_id=1, source_target_pairs={{0,1},{1,0},{2,3},{3,2},{4,5},{5,4},{6,7},{7,6},{8,9},{9,8},{10,11... | collective-permute-start | bytes 344072 | tf_op jit(solution)/shard_map/ppermute | solution.py:61
  67.0 3.5 %collective-permute-start.27 = (bf16[112,512]{1,0:T(8,128)(2,1)S(1)}, bf16[112,512]{1,0:T(8,128)(2,1)S(1)}, u32[]{:S(2)}, u32[]{:S(2)}) collective-permute-start(bf16[112,512]{1,0:T(8,128)(2,1)S(1)} %get-tuple-element.55.refs_0_), channel_id=1, source_target_pairs={{0,4},{1,5},{2,6},{3,7},{4,0},{5,1},{6,2},{7,3},{8,12},{9,13},{10,... | collective-permute-start | bytes 344072 | tf_op jit(solution)/shard_map/ppermute | solution.py:57
  71.5 2.1 %collective-permute-start.23 = (bf16[112,512]{1,0:T(8,128)(2,1)S(1)}, bf16[112,512]{1,0:T(8,128)(2,1)S(1)}, u32[]{:S(2)}, u32[]{:S(2)}) collective-permute-start(bf16[112,512]{1,0:T(8,128)(2,1)S(1)} %collective-permute-done.22.refs_3_), channel_id=1, source_target_pairs={{0,2},{1,3},{2,4},{3,5},{4,6},{5,7},{6,0},{7,1},{8,10},{9,11},{10,... | collective-permute-start | bytes 344072 | tf_op jit(solution)/shard_map/ppermute | solution.py:57
  73.6 1.3 %collective-permute-start.24 = (bf16[112,512]{1,0:T(8,128)(2,1)S(1)}, bf16[112,512]{1,0:T(8,128)(2,1)S(1)}, u32[]{:S(2)}, u32[]{:S(2)}) collective-permute-start(bf16[112,512]{1,0:T(8,128)(2,1)S(1)} %collective-permute-done.22.refs_3_), channel_id=1, source_target_pairs={{0,4},{1,5},{2,6},{3,7},{4,0},{5,1},{6,2},{7,3},{8,12},{9,13},{10,... | collective-permute-start | bytes 344072 | tf_op jit(solution)/shard_map/ppermute | solution.py:57
  74.9 1.5 %collective-permute-start.25 = (bf16[112,512]{1,0:T(8,128)(2,1)S(1)}, bf16[112,512]{1,0:T(8,128)(2,1)S(1)}, u32[]{:S(2)}, u32[]{:S(2)}) collective-permute-start(bf16[112,512]{1,0:T(8,128)(2,1)S(1)} %collective-permute-done.22.refs_3_), channel_id=1, source_target_pairs={{0,6},{1,7},{2,0},{3,1},{4,2},{5,3},{6,4},{7,5},{8,14},{9,15},{10,... | collective-permute-start | bytes 344072 | tf_op jit(solution)/shard_map/ppermute | solution.py:57
  77.2 1.4 %shard_map.89.refs_4_ = bf16[8,112,1024]{2,1,0:T(8,128)(2,1)} custom-call(bf16[112,512]{1,0:T(8,128)(2,1)S(1)} %collective-permute-done.26.refs_0_, bf16[112,512]{1,0:T(8,128)(2,1)S(1)} %collective-permute-done.27.refs_1_, bf16[112,512]{1,0:T(8,128)(2,1)S(1)} %collective-permute-done.28.refs_2_, ...), custom_call_target="tpu_custom_call", output_to_operand_aliasing={{}: (5, {})} | custom-call | tf_op jit(solution)/shard_map/pallas_call | solution.py:230
  78.6 1.3 %collective-permute-done.24.refs_1_ = bf16[112,512]{1,0:T(8,128)(2,1)S(1)} collective-permute-done((bf16[112,512]{1,0:T(8,128)(2,1)S(1)}, bf16[112,512]{1,0:T(8,128)(2,1)S(1)}, u32[]{:S(2)}, u32[]{:S(2)}) %collective-permute-start.24) | collective-permute-done | bytes 114720 | tf_op jit(solution)/shard_map/ppermute | solution.py:57
  79.9 1.2 %shard_map.90 = bf16[8,112,1024]{2,1,0:T(8,128)(2,1)} custom-call(bf16[112,512]{1,0:T(8,128)(2,1)S(1)} %collective-permute-done.23.refs_0_, bf16[112,512]{1,0:T(8,128)(2,1)S(1)} %collective-permute-done.24.refs_1_, bf16[112,512]{1,0:T(8,128)(2,1)S(1)} %collective-permute-done.25.refs_2_, ...), custom_call_target="tpu_custom_call", output_to_operand_aliasing={{}: (4, {})} | custom-call | tf_op jit(solution)/shard_map/pallas_call | solution.py:230
  (47 shorter events, 9.4 us)
Async XLA Ops:
  2.6 8.7 %collective-permute-start = (bf16[128,512]{1,0:T(8,128)(2,1)S(1)}, bf16[128,512]{1,0:T(8,128)(2,1)S(1)}, u32[]{:S(2)}, u32[]{:S(2)}) collective-permute-start(bf16[128,512]{1,0:T(8,128)(2,1)S(1)} %get-tuple-element.35), channel_id=1, source_target_pairs={{0,2},{1,3},{2,4},{3,5},{4,6},{5,7},{6,0},{7,1},{8,10},{9,11},{10,... | collective-permute-start | bytes 393224 | tf_op jit(solution)/shard_map/ppermute | solution.py:57
  4.2 7.2 %collective-permute-start.1 = (bf16[128,512]{1,0:T(8,128)(2,1)S(1)}, bf16[128,512]{1,0:T(8,128)(2,1)S(1)}, u32[]{:S(2)}, u32[]{:S(2)}) collective-permute-start(bf16[128,512]{1,0:T(8,128)(2,1)S(1)} %get-tuple-element.36), channel_id=1, source_target_pairs={{0,6},{1,7},{2,0},{3,1},{4,2},{5,3},{6,4},{7,5},{8,14},{9,15},{10,... | collective-permute-start | bytes 393224 | tf_op jit(solution)/shard_map/ppermute | solution.py:57
  6.0 7.0 %collective-permute-start.2 = (bf16[128,512]{1,0:T(8,128)(2,1)S(1)}, bf16[128,512]{1,0:T(8,128)(2,1)S(1)}, u32[]{:S(2)}, u32[]{:S(2)}) collective-permute-start(bf16[128,512]{1,0:T(8,128)(2,1)S(1)} %get-tuple-element.37), channel_id=1, source_target_pairs={{0,4},{1,5},{2,6},{3,7},{4,0},{5,1},{6,2},{7,3},{8,12},{9,13},{10,... | collective-permute-start | bytes 393224 | tf_op jit(solution)/shard_map/ppermute | solution.py:57
  10.8 24.9 %collective-permute-start.8 = (bf16[2,4,112,512]{3,2,1,0:T(8,128)(2,1)S(1)}, bf16[2,4,112,512]{3,2,1,0:T(8,128)(2,1)S(1)}, u32[]{:S(2)}, u32[]{:S(2)}) collective-permute-start(bf16[2,4,112,512]{3,2,1,0:T(8,128)(2,1)S(1)} %get-tuple-element.40), channel_id=1, source_target_pairs={{0,8},{8,0},{16,24},{24,16},{32,40},{40,32},{48,56},{56,48},{64,72... | collective-permute-start | bytes 2752520 | tf_op jit(solution)/shard_map/ppermute | solution.py:45
  10.9 24.8 %collective-permute-start.9 = (bf16[2,4,112,512]{3,2,1,0:T(8,128)(2,1)S(1)}, bf16[2,4,112,512]{3,2,1,0:T(8,128)(2,1)S(1)}, u32[]{:S(2)}, u32[]{:S(2)}) collective-permute-start(bf16[2,4,112,512]{3,2,1,0:T(8,128)(2,1)S(1)} %get-tuple-element.41), channel_id=1, source_target_pairs={{0,8},{8,0},{16,24},{24,16},{32,40},{40,32},{48,56},{56,48},{64,72... | collective-permute-start | bytes 2752520 | tf_op jit(solution)/shard_map/ppermute | solution.py:45
  13.0 12.0 %collective-permute-start.3 = (bf16[128,512]{1,0:T(8,128)(2,1)S(1)}, bf16[128,512]{1,0:T(8,128)(2,1)S(1)}, u32[]{:S(2)}, u32[]{:S(2)}) collective-permute-start(bf16[128,512]{1,0:T(8,128)(2,1)S(1)} %get-tuple-element.39), channel_id=1, source_target_pairs={{0,1},{1,0},{2,3},{3,2},{4,5},{5,4},{6,7},{7,6},{8,9},{9,8},{10,11... | collective-permute-start | bytes 393224 | tf_op jit(solution)/shard_map/ppermute | solution.py:61
  25.1 6.3 %collective-permute-start.4 = (bf16[128,512]{1,0:T(8,128)(2,1)S(1)}, bf16[128,512]{1,0:T(8,128)(2,1)S(1)}, u32[]{:S(2)}, u32[]{:S(2)}) collective-permute-start(bf16[128,512]{1,0:T(8,128)(2,1)S(1)} %shard_map.79.p0), channel_id=1, source_target_pairs={{0,2},{1,3},{2,4},{3,5},{4,6},{5,7},{6,0},{7,1},{8,10},{9,11},{10,... | collective-permute-start | bytes 393224 | tf_op jit(solution)/shard_map/ppermute | solution.py:57
  25.2 7.5 %collective-permute-start.5 = (bf16[128,512]{1,0:T(8,128)(2,1)S(1)}, bf16[128,512]{1,0:T(8,128)(2,1)S(1)}, u32[]{:S(2)}, u32[]{:S(2)}) collective-permute-start(bf16[128,512]{1,0:T(8,128)(2,1)S(1)} %shard_map.79.p0), channel_id=1, source_target_pairs={{0,4},{1,5},{2,6},{3,7},{4,0},{5,1},{6,2},{7,3},{8,12},{9,13},{10,... | collective-permute-start | bytes 393224 | tf_op jit(solution)/shard_map/ppermute | solution.py:57
  28.3 5.3 %collective-permute-start.6 = (bf16[128,512]{1,0:T(8,128)(2,1)S(1)}, bf16[128,512]{1,0:T(8,128)(2,1)S(1)}, u32[]{:S(2)}, u32[]{:S(2)}) collective-permute-start(bf16[128,512]{1,0:T(8,128)(2,1)S(1)} %shard_map.79.p0), channel_id=1, source_target_pairs={{0,6},{1,7},{2,0},{3,1},{4,2},{5,3},{6,4},{7,5},{8,14},{9,15},{10,... | collective-permute-start | bytes 393224 | tf_op jit(solution)/shard_map/ppermute | solution.py:57
  33.7 2.0 %collective-permute-start.7 = (bf16[512,512]{1,0:T(8,128)(2,1)S(1)}, bf16[512,512]{1,0:T(8,128)(2,1)S(1)}, u32[]{:S(2)}, u32[]{:S(2)}) collective-permute-start(bf16[512,512]{1,0:T(8,128)(2,1)S(1)} %pad_maximum_fusion), channel_id=1, source_target_pairs={{0,8},{8,0},{16,24},{24,16},{32,40},{40,32},{48,56},{56,48},{64,72... | collective-permute-start | bytes 1572872 | tf_op jit(solution)/shard_map/ppermute | solution.py:45
  36.4 13.3 %collective-permute-start.14 = (bf16[448,512]{1,0:T(8,128)(2,1)S(1)}, bf16[448,512]{1,0:T(8,128)(2,1)S(1)}, u32[]{:S(2)}, u32[]{:S(2)}) collective-permute-start(bf16[448,512]{1,0:T(8,128)(2,1)S(1)} %get-tuple-element.47), channel_id=1, source_target_pairs={{0,16},{8,24},{16,0},{24,8},{32,48},{40,56},{48,32},{56,40},{64,80... | collective-permute-start | bytes 1376264 | tf_op jit(solution)/shard_map/ppermute | solution.py:53
  36.5 6.8 %collective-permute-start.10 = (bf16[112,512]{1,0:T(8,128)(2,1)S(1)}, bf16[112,512]{1,0:T(8,128)(2,1)S(1)}, u32[]{:S(2)}, u32[]{:S(2)}) collective-permute-start(bf16[112,512]{1,0:T(8,128)(2,1)S(1)} %get-tuple-element.43), channel_id=1, source_target_pairs={{0,64},{8,72},{16,80},{24,88},{32,96},{40,104},{48,112},{56,120},{... | collective-permute-start | bytes 344072 | tf_op jit(solution)/shard_map/ppermute | solution.py:49
  38.2 7.7 %collective-permute-start.11 = (bf16[112,512]{1,0:T(8,128)(2,1)S(1)}, bf16[112,512]{1,0:T(8,128)(2,1)S(1)}, u32[]{:S(2)}, u32[]{:S(2)}) collective-permute-start(bf16[112,512]{1,0:T(8,128)(2,1)S(1)} %get-tuple-element.44), channel_id=1, source_target_pairs={{0,192},{8,200},{16,208},{24,216},{32,224},{40,232},{48,240},{56,2... | collective-permute-start | bytes 344072 | tf_op jit(solution)/shard_map/ppermute | solution.py:49
  39.8 7.6 %collective-permute-start.12 = (bf16[112,512]{1,0:T(8,128)(2,1)S(1)}, bf16[112,512]{1,0:T(8,128)(2,1)S(1)}, u32[]{:S(2)}, u32[]{:S(2)}) collective-permute-start(bf16[112,512]{1,0:T(8,128)(2,1)S(1)} %get-tuple-element.45), channel_id=1, source_target_pairs={{0,128},{8,136},{16,144},{24,152},{32,160},{40,168},{48,176},{56,1... | collective-permute-start | bytes 344072 | tf_op jit(solution)/shard_map/ppermute | solution.py:49
  42.6 9.3 %collective-permute-start.17 = (bf16[112,512]{1,0:T(8,128)(2,1)S(1)}, bf16[112,512]{1,0:T(8,128)(2,1)S(1)}, u32[]{:S(2)}, u32[]{:S(2)}) collective-permute-start(bf16[112,512]{1,0:T(8,128)(2,1)S(1)} %get-tuple-element.52), channel_id=1, source_target_pairs={{0,64},{8,72},{16,80},{24,88},{32,96},{40,104},{48,112},{56,120},{... | collective-permute-start | bytes 344072 | tf_op jit(solution)/shard_map/ppermute | solution.py:49
  43.4 10.4 %collective-permute-start.18 = (bf16[112,512]{1,0:T(8,128)(2,1)S(1)}, bf16[112,512]{1,0:T(8,128)(2,1)S(1)}, u32[]{:S(2)}, u32[]{:S(2)}) collective-permute-start(bf16[112,512]{1,0:T(8,128)(2,1)S(1)} %get-tuple-element.53), channel_id=1, source_target_pairs={{0,192},{8,200},{16,208},{24,216},{32,224},{40,232},{48,240},{56,2... | collective-permute-start | bytes 344072 | tf_op jit(solution)/shard_map/ppermute | solution.py:49
  45.9 7.8 %collective-permute-start.19 = (bf16[112,512]{1,0:T(8,128)(2,1)S(1)}, bf16[112,512]{1,0:T(8,128)(2,1)S(1)}, u32[]{:S(2)}, u32[]{:S(2)}) collective-permute-start(bf16[112,512]{1,0:T(8,128)(2,1)S(1)} %get-tuple-element.54), channel_id=1, source_target_pairs={{0,128},{8,136},{16,144},{24,152},{32,160},{40,168},{48,176},{56,1... | collective-permute-start | bytes 344072 | tf_op jit(solution)/shard_map/ppermute | solution.py:49
  47.4 10.4 %collective-permute-start.13 = (bf16[112,512]{1,0:T(8,128)(2,1)S(1)}, bf16[112,512]{1,0:T(8,128)(2,1)S(1)}, u32[]{:S(2)}, u32[]{:S(2)}) collective-permute-start(bf16[112,512]{1,0:T(8,128)(2,1)S(1)} %shard_map.82), channel_id=1, source_target_pairs={{0,48},{8,56},{16,32},{24,40},{32,16},{40,24},{48,0},{56,8},{64,11... | collective-permute-start | bytes 344072 | tf_op jit(solution)/shard_map/ppermute | solution.py:53
  49.7 11.2 %copy-start = (f32[1,112,512]{2,1,0:T(8,128)S(1)}, f32[1,112,512]{2,1,0:T(8,128)}, u32[]{:S(2)}) copy-start(f32[1,112,512]{2,1,0:T(8,128)} %first.3) | copy-start | bytes 688132
  49.7 11.2 %copy-start.1 = (f32[1,112,512]{2,1,0:T(8,128)S(1)}, f32[1,112,512]{2,1,0:T(8,128)}, u32[]{:S(2)}) copy-start(f32[1,112,512]{2,1,0:T(8,128)} %second.3) | copy-start | bytes 688132
  49.8 8.1 %collective-permute-start.15 = (bf16[112,512]{1,0:T(8,128)(2,1)S(1)}, bf16[112,512]{1,0:T(8,128)(2,1)S(1)}, u32[]{:S(2)}, u32[]{:S(2)}) collective-permute-start(bf16[112,512]{1,0:T(8,128)(2,1)S(1)} %get-tuple-element.49), channel_id=1, source_target_pairs={{0,64},{8,72},{16,80},{24,88},{32,96},{40,104},{48,112},{56,120},{... | collective-permute-start | bytes 344072 | tf_op jit(solution)/shard_map/ppermute | solution.py:49
  51.9 6.6 %collective-permute-start.16 = (bf16[112,512]{1,0:T(8,128)(2,1)S(1)}, bf16[112,512]{1,0:T(8,128)(2,1)S(1)}, u32[]{:S(2)}, u32[]{:S(2)}) collective-permute-start(bf16[112,512]{1,0:T(8,128)(2,1)S(1)} %get-tuple-element.50), channel_id=1, source_target_pairs={{0,128},{8,136},{16,144},{24,152},{32,160},{40,168},{48,176},{56,1... | collective-permute-start | bytes 344072 | tf_op jit(solution)/shard_map/ppermute | solution.py:49
  53.8 5.9 %collective-permute-start.20 = (bf16[112,512]{1,0:T(8,128)(2,1)S(1)}, bf16[112,512]{1,0:T(8,128)(2,1)S(1)}, u32[]{:S(2)}, u32[]{:S(2)}) collective-permute-start(bf16[112,512]{1,0:T(8,128)(2,1)S(1)} %shard_map.85.refs_0_), channel_id=1, source_target_pairs={{0,32},{8,40},{16,48},{24,56},{32,0},{40,8},{48,16},{56,24},{64,96... | collective-permute-start | bytes 344072 | tf_op jit(solution)/shard_map/ppermute | solution.py:53
  56.0 4.9 %collective-permute-start.21 = (bf16[112,512]{1,0:T(8,128)(2,1)S(1)}, bf16[112,512]{1,0:T(8,128)(2,1)S(1)}, u32[]{:S(2)}, u32[]{:S(2)}) collective-permute-start(bf16[112,512]{1,0:T(8,128)(2,1)S(1)} %shard_map.86), channel_id=1, source_target_pairs={{0,192},{8,200},{16,208},{24,216},{32,224},{40,232},{48,240},{56,2... | collective-permute-start | bytes 344072 | tf_op jit(solution)/shard_map/ppermute | solution.py:49
  61.2 10.3 %collective-permute-start.22 = (bf16[112,512]{1,0:T(8,128)(2,1)S(1)}, bf16[112,512]{1,0:T(8,128)(2,1)S(1)}, u32[]{:S(2)}, u32[]{:S(2)}) collective-permute-start(bf16[112,512]{1,0:T(8,128)(2,1)S(1)} %get-tuple-element.55.refs_0_), channel_id=1, source_target_pairs={{0,1},{1,0},{2,3},{3,2},{4,5},{5,4},{6,7},{7,6},{8,9},{9,8},{10,11... | collective-permute-start | bytes 344072 | tf_op jit(solution)/shard_map/ppermute | solution.py:61
  66.3 8.5 %collective-permute-start.26 = (bf16[112,512]{1,0:T(8,128)(2,1)S(1)}, bf16[112,512]{1,0:T(8,128)(2,1)S(1)}, u32[]{:S(2)}, u32[]{:S(2)}) collective-permute-start(bf16[112,512]{1,0:T(8,128)(2,1)S(1)} %get-tuple-element.55.refs_0_), channel_id=1, source_target_pairs={{0,2},{1,3},{2,4},{3,5},{4,6},{5,7},{6,0},{7,1},{8,10},{9,11},{10,... | collective-permute-start | bytes 344072 | tf_op jit(solution)/shard_map/ppermute | solution.py:57
  67.0 10.2 %collective-permute-start.27 = (bf16[112,512]{1,0:T(8,128)(2,1)S(1)}, bf16[112,512]{1,0:T(8,128)(2,1)S(1)}, u32[]{:S(2)}, u32[]{:S(2)}) collective-permute-start(bf16[112,512]{1,0:T(8,128)(2,1)S(1)} %get-tuple-element.55.refs_0_), channel_id=1, source_target_pairs={{0,4},{1,5},{2,6},{3,7},{4,0},{5,1},{6,2},{7,3},{8,12},{9,13},{10,... | collective-permute-start | bytes 344072 | tf_op jit(solution)/shard_map/ppermute | solution.py:57
  70.5 6.7 %collective-permute-start.28 = (bf16[112,512]{1,0:T(8,128)(2,1)S(1)}, bf16[112,512]{1,0:T(8,128)(2,1)S(1)}, u32[]{:S(2)}, u32[]{:S(2)}) collective-permute-start(bf16[112,512]{1,0:T(8,128)(2,1)S(1)} %get-tuple-element.55.refs_0_), channel_id=1, source_target_pairs={{0,6},{1,7},{2,0},{3,1},{4,2},{5,3},{6,4},{7,5},{8,14},{9,15},{10,... | collective-permute-start | bytes 344072 | tf_op jit(solution)/shard_map/ppermute | solution.py:57
  71.5 7.1 %collective-permute-start.23 = (bf16[112,512]{1,0:T(8,128)(2,1)S(1)}, bf16[112,512]{1,0:T(8,128)(2,1)S(1)}, u32[]{:S(2)}, u32[]{:S(2)}) collective-permute-start(bf16[112,512]{1,0:T(8,128)(2,1)S(1)} %collective-permute-done.22.refs_3_), channel_id=1, source_target_pairs={{0,2},{1,3},{2,4},{3,5},{4,6},{5,7},{6,0},{7,1},{8,10},{9,11},{10,... | collective-permute-start | bytes 344072 | tf_op jit(solution)/shard_map/ppermute | solution.py:57
  73.6 6.3 %collective-permute-start.24 = (bf16[112,512]{1,0:T(8,128)(2,1)S(1)}, bf16[112,512]{1,0:T(8,128)(2,1)S(1)}, u32[]{:S(2)}, u32[]{:S(2)}) collective-permute-start(bf16[112,512]{1,0:T(8,128)(2,1)S(1)} %collective-permute-done.22.refs_3_), channel_id=1, source_target_pairs={{0,4},{1,5},{2,6},{3,7},{4,0},{5,1},{6,2},{7,3},{8,12},{9,13},{10,... | collective-permute-start | bytes 344072 | tf_op jit(solution)/shard_map/ppermute | solution.py:57
  74.9 5.0 %collective-permute-start.25 = (bf16[112,512]{1,0:T(8,128)(2,1)S(1)}, bf16[112,512]{1,0:T(8,128)(2,1)S(1)}, u32[]{:S(2)}, u32[]{:S(2)}) collective-permute-start(bf16[112,512]{1,0:T(8,128)(2,1)S(1)} %collective-permute-done.22.refs_3_), channel_id=1, source_target_pairs={{0,6},{1,7},{2,0},{3,1},{4,2},{5,3},{6,4},{7,5},{8,14},{9,15},{10,... | collective-permute-start | bytes 344072 | tf_op jit(solution)/shard_map/ppermute | solution.py:57
